TPU v7x, 32 devices: a whole 2x2x4 slice. The times are simulated.
32 devices in a mesh: tm: 4 (over z), height: 4 (over y, x), cam: 2 (over core).
Axes of the slice: x: 2, y: 2, z: 4, core: 2. Of those that a mesh axis runs over, the one named last changes fastest.
Arguments:
- video_clip: bfloat16 [2, 16, 16, 64, 256], P('cam', 'tm', 'height'), may hold values from -6 to 6
- valid_from: int32 [2], P('cam'), may hold values from 0 to 8, as said below
- norm_gain: float32 [256], replicated, may hold values from 0.5 to 1.5
- spatial_weight: bfloat16 [3, 3, 256, 256], replicated, may hold values from -0.125 to 0.125
- temporal_weight: bfloat16 [3, 256, 256], replicated, may hold values from -0.21875 to 0.21875
- mix_weight: bfloat16 [3, 256, 256], replicated, may hold values from -0.21875 to 0.21875
- cotangent: bfloat16 [2, 8, 16, 64, 256], P('cam', None, ('height', 'tm')), may hold values from -6 to 6
Outputs:
- encoded: bfloat16 [2, 8, 16, 64, 256], P('cam', None, ('height', 'tm'))
- video_gradient: bfloat16 [2, 16, 16, 64, 256], P('cam', 'tm', 'height')
- spatial_gradient: float32 [3, 3, 256, 256], replicated
- temporal_gradient: float32 [3, 256, 256], replicated
- mix_gradient: float32 [3, 256, 256], replicated
- gain_gradient: float32 [256], replicated
Inputs may be any that keep to these rules, and one draw needn't show every extreme that they name: Frames before valid_from of a camera are padding. In every draw some camera starts at 8.
All inputs are finite; a program needn't handle non-finite values.
Results may differ from a plain program's by a relative error of at most 0.0065.
Values may be sent and summed in bfloat16 or wider, within the bound.
No kernel may reach another device: no remote copies, remote signals or barrier semaphores. Data moves between devices by JAX's collectives and lax.ppermute only.
A program may use at most 128 MiB of HBM per device.

v0:
```python
import functools
import math

import jax
import jax.numpy as jnp
from jax import lax
from jax.experimental import pallas as pl
from jax.experimental.pallas import tpu as pltpu
from jax.sharding import PartitionSpec as P

F32 = jnp.float32
BF16 = jnp.bfloat16
VMEM_LIMIT = 16 * 1024 * 1024
SPLIT = 8


def dot(left, right):
    return jnp.dot(left, right, preferred_element_type=F32)


def dot_nt(left, right):
    return lax.dot_general(left, right, (((1,), (1,)), ((), ())), preferred_element_type=F32)


def dot_tn(left, right):
    return lax.dot_general(left, right, (((0,), (0,)), ((), ())), preferred_element_type=F32)


def from_left(cells, width):
    column = lax.broadcasted_iota(jnp.int32, cells.shape, 0) % width
    return jnp.where(column == 0, 0.0, pltpu.roll(cells, 1, 0))


def from_right(cells, width):
    column = lax.broadcasted_iota(jnp.int32, cells.shape, 0) % width
    return jnp.where(column == width - 1, 0.0, pltpu.roll(cells, cells.shape[0] - 1, 0))


def present(start, frame, frames):
    return (lax.axis_index("tm") * frames + frame >= start[0]).astype(F32)


def normalised(tile, keep):
    values = tile.astype(F32) * keep
    inverse = lax.rsqrt(jnp.mean(values * values, axis=-1, keepdims=True) + 1e-06)
    return (values * inverse, inverse)


def first_frame(shard, outs, span, total):
    return jnp.minimum(shard * outs, total - span)


def run_copies(pairs_of_refs, done):
    copies = [
        pltpu.make_async_copy(source, target, done.at[at])
        for at, (source, target) in enumerate(pairs_of_refs)
    ]
    for copy in copies:
        copy.start()
    for copy in copies:
        copy.wait()


def pieces_kernel(cotangent, *refs, outs):
    pieces, done = (refs[:-1], refs[-1])
    span = outs + 3
    me = lax.axis_index("tm")
    copies = []
    for step, piece in enumerate(pieces):
        begin = first_frame(me ^ (step + 1), outs, span, cotangent.shape[0])
        copies.append((cotangent.at[pl.ds(begin, span)], piece))
    run_copies(copies, done)


def edges_kernel(video, inner, outer, done, *, rows):
    odd = lax.axis_index("height") % 2
    run_copies(
        [
            (video.at[:, (1 - odd) * (rows - 1)], inner),
            (video.at[:, odd * (rows - 1)], outer),
        ],
        done,
    )


def first_frame(shard, outs, span, total):
    return jnp.minimum(shard * outs, total - span)


def place_halos(halo, inner, outer):
    odd = lax.axis_index("height") % 2
    halo[1 - odd] = inner[...]
    halo[odd] = outer[...]


def column_sum(cells, weight, taps, width):
    products = [
        dot(cells, jnp.concatenate([weight[i, j] for i in taps], axis=0)) for j in range(3)
    ]
    return from_left(products[0], width) + products[1] + from_right(products[2], width)


def halo_kernel(inner, outer, halo):
    place_halos(halo, inner, outer)


def own_kernel(
    valid_from, video, gain, weight, normed, partial, start, done, *, frames, rows, width
):
    run_copies([(valid_from, start)], done)
    block = frames * width
    for row in range(rows):
        for frame in range(frames):
            unit, _ = normalised(video[frame, row], present(start, frame, frames))
            at = row * block + frame * width
            normed[at : at + width] = (unit * gain[...]).astype(BF16)
    for row in range(rows):
        taps = [i for i in range(3) if 0 <= row + i - 1 < rows]
        cells = [normed[(row + i - 1) * block : (row + i) * block] for i in taps]
        partial[row * block : row * block + block] = column_sum(
            jnp.concatenate(cells, axis=1), weight, taps, width
        )


def front_kernel(
    valid_from, normed, partial, inner, outer, gain, weight, temporal, *refs,
    frames, rows, width, shards
):
    tall, slope, active, parts, *refs = refs
    strided, (halo, start, done, lines) = (refs[:shards], refs[shards:])
    outs = frames // 2
    plane = rows * width
    here = rows // shards
    block = frames * width

    run_copies([(valid_from, start)], done)
    place_halos(halo, inner, outer)
    tall[block : block + rows * block] = normed[...]
    for side, at in ((0, 0), (1, (rows + 1) * block)):
        for frame in range(frames):
            unit, _ = normalised(halo[side, frame], present(start, frame, frames))
            to = at + frame * width
            tall[to : to + width] = (unit * gain[...]).astype(BF16)
    for row in range(rows):
        pre = partial[row * block : row * block + block]
        if row == 0:
            pre = pre + column_sum(tall[:block], weight, [0], width)
        if row == rows - 1:
            pre = pre + column_sum(tall[(rows + 1) * block :], weight, [2], width)
        sigmoid = 1.0 / (1.0 + jnp.exp(-pre))
        slope[row * block : row * block + block] = sigmoid * (1.0 + pre * (1.0 - sigmoid))
        cells = (pre * sigmoid).astype(BF16)
        for frame in range(frames):
            at = (frame // 2) * plane + row * width
            active[frame % 2, at : at + width] = cells[frame * width : frame * width + width]
    evens = active[0]
    odds = active[1]
    carried = dot(odds, temporal[2])
    mixed = dot(odds, temporal[0]) + dot(evens, temporal[1])
    pieces = [mixed[:plane]]
    for s in range(1, outs):
        pieces.append(
            mixed[s * plane : s * plane + plane] + carried[(s - 1) * plane : s * plane]
        )
    pieces.append(carried[(outs - 1) * plane :])
    pieces = jnp.concatenate(pieces, axis=0).astype(BF16)
    parts[...] = pieces
    for frame in range(outs + 1):
        cells = pieces[frame * plane : frame * plane + plane]
        lines[:, frame] = cells.reshape(shards, here, width, 256)
    for step, piece in enumerate(strided):
        piece[...] = lines[lax.axis_index("tm") ^ step]


def middle_kernel(
    tall, slope, active, parts, temporal, mix, cotangent, *refs, frames, rows, width, shards
):
    pieces, refs = (refs[: shards - 1], refs[shards - 1 :])
    pre_gradient, inner_out, outer_out, keep, send, cot = refs
    outs = frames // 2
    plane = rows * width
    here = rows // shards
    me = lax.axis_index("tm")
    total = shards * outs
    cut = outs + 3
    skip = me * outs - first_frame(me, outs, cut, total)
    for frame in range(cut):
        here_is = (me * outs + frame < total).astype(F32)
        own = cotangent[jnp.minimum(me * outs + frame, total - 1)]
        others = [piece[jnp.minimum(frame + skip, cut - 1)] for piece in pieces]
        for step, cells in enumerate([own] + others[::-1]):
            cells = (cells.astype(F32) * here_is).astype(BF16)
            cot[frame, me ^ step] = cells.reshape(here * width, 256)

    def ahead(k, count=outs + 1):
        return cot[k : k + count].reshape(count * plane, 256)

    gradient = ahead(0).astype(F32)
    for k in range(3):
        gradient = gradient + dot_nt(ahead(k), mix[k])
    gradient = gradient.astype(BF16)
    now = gradient[: outs * plane]
    later = gradient[plane:]
    even_gradient = dot_nt(now, temporal[1])
    odd_gradient = dot_nt(now, temporal[0]) + dot_nt(later, temporal[2])
    for row in range(rows):
        for frame in range(frames):
            source = odd_gradient if frame % 2 else even_gradient
            at = (frame // 2) * plane + row * width
            to = (row * frames + frame) * width
            tile = (source[at : at + width] * slope[to : to + width]).astype(BF16)
            pre_gradient[row, frame] = tile
    side = (lax.axis_index("height") % 2) * (rows - 1)
    inner_out[...] = pre_gradient[rows - 1 - side]
    outer_out[...] = pre_gradient[side]
    evens = active[0]
    odds = active[1]
    for k in range(3):
        deliver(keep, send, k, dot_tn(parts[...], ahead(k)))
    deliver(keep, send, 3, dot_tn(odds, now))
    deliver(keep, send, 4, dot_tn(evens, now))
    deliver(keep, send, 5, dot_tn(odds, later))
    block = frames * width
    spatial_sums(tall, pre_gradient, keep, send, 6, range(SPLIT - 6), block, rows, width)


def spatial_kernel(tall, pre_gradient, keep, send, *, frames, rows, width):
    block = frames * width
    spatial_sums(tall, pre_gradient, keep, send, 0, range(SPLIT - 6, 9), block, rows, width)


def spatial_sums(tall, pre_gradient, keep, send, first, taps, block, rows, width):
    columns = column_shifts(pre_gradient, width)
    for i in range(3):
        here = [tap for tap in taps if tap // 3 == i]
        if not here:
            continue
        cells = tall[i * block : (i + rows) * block]
        product = dot_tn(cells, jnp.concatenate([columns[tap % 3] for tap in here], axis=1))
        for place, tap in enumerate(here):
            index = first + tap - taps[0]
            deliver(keep, send, index, product[:, place * 256 : place * 256 + 256])


def column_shifts(pre_gradient, width):
    gradient = pre_gradient[...].reshape(-1, 256)
    exact = gradient.astype(F32)
    left = from_right(exact, width).astype(BF16)
    right = from_left(exact, width).astype(BF16)
    return [left, gradient, right]


def deliver(keep, send, index, product):
    first = jnp.full((256, 128), lax.axis_index("cam")) == 0
    low, high = (product[:, :128], product[:, 128:])
    at = index * 256
    keep[at : at + 256] = jnp.where(first, low, high)
    send[at : at + 256] = jnp.where(first, high, low).astype(BF16)


def core_columns():
    mine = pl.ds(pl.multiple_of(lax.axis_index("cam") * 128, 128), 128)
    other = pl.ds(pl.multiple_of((1 - lax.axis_index("cam")) * 128, 128), 128)
    return (mine, other)


def deal_kernel(low, low_got, high, high_got, kept, *sends):
    me = lax.axis_index("height")
    cut = low.shape[1]

    def fill(target, at):
        target[:cut] = (low[at] + low_got[at].astype(F32)).astype(target.dtype)
        target[cut:] = (high[at] + high_got[at].astype(F32)).astype(target.dtype)

    fill(kept, me)
    for step, send in enumerate(sends):
        fill(send, me ^ (step + 1))


def halve_kernel(*refs):
    (kept_in, *received), (kept, send) = (refs[:-2], refs[-2:])
    mine = lax.axis_index("tm") % 2

    def total(at):
        value = kept_in[at]
        for piece in received:
            value = value + piece[at].astype(F32)
        return value

    kept[...] = total(mine)
    send[...] = total(1 - mine).astype(BF16)


def add_kernel(left, right, out):
    out[...] = (left[...].astype(F32) + right[...].astype(F32)).astype(BF16)


def whole_kernel(mine, other, out, *, axis, step):
    at = (lax.axis_index(axis) >> step) % 2
    out[at] = mine[...]
    out[1 - at] = other[...]


def input_kernel(
    valid_from, video, pre_gradient, halo, gain, weight, out, tall, start, done,
    *, frames, rows, width
):
    run_copies([(valid_from, start)], done)
    block = frames * width
    for row in range(-1, rows + 1):
        if row < 0:
            cells = halo[0]
        elif row == rows:
            cells = halo[1]
        else:
            cells = pre_gradient[row]
        cells = cells.reshape(block, 256)
        for tap in range(3):
            target = row - 1 + tap
            if 0 <= target < rows:
                tall[target * block : target * block + block, tap * 256 : tap * 256 + 256] = cells
    for row in range(rows):
        cells = tall[row * block : row * block + block]
        taps = [
            dot_nt(cells, jnp.concatenate([weight[0, j], weight[1, j], weight[2, j]], axis=1))
            for j in range(3)
        ]
        gradient = from_right(taps[0], width) + taps[1] + from_left(taps[2], width)
        gradient = gradient * gain[...]
        for frame in range(frames):
            keep = present(start, frame, frames)
            unit, inverse = normalised(video[frame, row], keep)
            tile = gradient[frame * width : frame * width + width]
            mean = jnp.mean(tile * unit, axis=-1, keepdims=True)
            out[frame, row] = (inverse * (tile - unit * mean) * keep).astype(BF16)


def encode_kernel(mix, *refs, width, shards):
    pieces, (out, line, strided) = (refs[:shards], refs[shards:])
    for step, piece in enumerate(pieces):
        strided[lax.axis_index("tm") ^ step] = piece[...]
    parts, here = strided.shape[1:3]
    outs = parts - 1
    plane = here * width
    total = shards * outs
    for frame in range(total):
        shard, part = (frame // outs, frame % outs)
        cells = strided[shard, part].reshape(plane, 256)
        if part == 0 and shard > 0:
            carried = strided[shard - 1, outs].reshape(plane, 256)
            cells = (cells.astype(F32) + carried.astype(F32)).astype(BF16)
        line[(frame + 2) * plane : (frame + 3) * plane] = cells
    line[0 : 2 * plane] = jnp.zeros((2 * plane, 256), BF16)
    span = total * plane
    result = line[2 * plane : 2 * plane + span].astype(F32)
    for k in range(3):
        result = result + dot(line[(2 - k) * plane : (2 - k) * plane + span], mix[k])
    out[...] = result.astype(BF16).reshape(out.shape)


def finish_kernel(*refs, scale, parts, last):
    (pieces, weight, refs) = (refs[:parts], refs[parts], refs[parts + 1 :])
    if last:
        before, gain, _, _, _, spatial, temporal, mix, gain_out, staged, row, done = refs
        total = before[...]
    else:
        spatial, temporal, mix, after, staged, done = refs
        total = jnp.zeros((256, 128), F32)
    columns = core_columns()[1 if last else 0]
    low, high = (SPLIT * 256 // parts, (15 - SPLIT) * 256 // parts)
    for step, piece in enumerate(pieces):
        part = lax.axis_index("height") ^ step
        at = pl.multiple_of(part * low, low)
        staged[pl.ds(at, low)] = piece[:low].astype(F32) * scale
        at = pl.multiple_of(SPLIT * 256 + part * high, high)
        staged[pl.ds(at, high)] = piece[low:].astype(F32) * scale
    results = [(mix, k) for k in range(3)] + [(temporal, k) for k in range(3)]
    results = results + [(spatial, k) for k in range(9)]
    copies = []
    for index, (result, k) in enumerate(results):
        cells = staged.at[pl.ds(index * 256, 256)]
        copies.append(pltpu.make_async_copy(cells, result.at[k, :, columns], done.at[index]))
        copies[-1].start()
    for k in range(9):
        cells = staged[1536 + k * 256 : 1792 + k * 256]
        total = total + cells * weight[k // 3, k % 3, :, columns].astype(F32)
    if last:
        upper = total.astype(BF16)
        lower = (total - upper.astype(F32)).astype(BF16)
        ones = jnp.ones((16, 128), BF16)
        row[...] = (dot_nt(ones, upper) + dot_nt(ones, lower))[:1] / gain[...]
        copies.append(pltpu.make_async_copy(row, gain_out, done.at[15]))
        copies[-1].start()
    else:
        after[...] = total
    for copy in copies:
        copy.wait()


def call(kernel, outs, scratch=(), flops=0, moved=0, aliases=None, far=0):
    where = pl.BlockSpec(memory_space=pltpu.VMEM)

    def run(*operands):
        results = pl.pallas_call(
            kernel,
            out_shape=[jax.ShapeDtypeStruct(shape, dtype) for shape, dtype in outs],
            in_specs=[
                pl.BlockSpec(memory_space=pltpu.HBM)
                if a.dtype == jnp.int32 or at in (aliases or ())
                else where
                for at, a in enumerate(operands)
            ],
            out_specs=[pl.BlockSpec(memory_space=pltpu.HBM)] * far + [where] * (len(outs) - far),
            input_output_aliases=aliases or {},
            scratch_shapes=list(scratch),
            compiler_params=pltpu.CompilerParams(vmem_limit_bytes=VMEM_LIMIT),
            cost_estimate=pl.CostEstimate(flops=flops, bytes_accessed=moved, transcendentals=0),
        )(*operands)
        return list(results)

    return run


def neighbours(inner, outer, axis):
    size = lax.axis_size(axis)
    links = [(i, i + 1) for i in range(1, size - 1, 2)]
    links = links + [(j, i) for i, j in links]
    return (pair(inner, axis, 1), lax.ppermute(outer, axis, links))


def pair(array, axis, step):
    return lax.ppermute(array, axis, [(i, i ^ step) for i in range(lax.axis_size(axis))])


def pairs(arrays, axis):
    return [pair(array, axis, step + 1) for step, array in enumerate(arrays)]


def together(*values):
    return lax.optimization_barrier(values)


def on_device(
    video_clip, valid_from, norm_gain, spatial_weight, temporal_weight, mix_weight, cotangent
):
    video = video_clip[0]
    frames, rows, width, channels = video.shape
    outs = frames // 2
    shards = lax.axis_size("tm")
    lines = lax.axis_size("height")
    here = rows // shards
    cells = frames * rows * width
    sizes = dict(frames=frames, rows=rows, width=width)
    gain = norm_gain.reshape(1, channels)
    edge = ((frames, width, channels), BF16)
    halo = pltpu.VMEM((2, frames, width, channels), BF16)

    scalar = [pltpu.SMEM((1,), jnp.int32), pltpu.SemaphoreType.DMA((1,))]
    pieces = call(
        functools.partial(pieces_kernel, outs=outs),
        [((outs + 3, here, width, channels), BF16)] * (shards - 1),
        [pltpu.SemaphoreType.DMA((shards - 1,))],
        moved=1024 * 1024,
    )(cotangent[0])
    *pieces, edges = together(*pieces, video)
    pieces = pairs(pieces, "tm")
    inner, outer = call(
        functools.partial(edges_kernel, rows=rows),
        [edge, edge],
        [pltpu.SemaphoreType.DMA((2,))],
        moved=512 * 1024,
    )(edges)
    inner, outer = neighbours(inner, outer, "height")

    normed, partial = call(
        functools.partial(own_kernel, **sizes),
        [((cells, channels), BF16), ((cells, channels), F32)],
        scalar,
        flops=18 * cells * channels * channels,
        moved=4 * 1024 * 1024,
    )(valid_from, video, gain, spatial_weight)

    tall, slope, active, parts, *strided = call(
        functools.partial(front_kernel, **sizes, shards=shards),
        [
            ((cells + 2 * frames * width, channels), BF16),
            ((cells, channels), F32),
            ((2, cells // 2, channels), BF16),
            (((outs + 1) * rows * width, channels), BF16),
        ]
        + [((outs + 1, here, width, channels), BF16)] * shards,
        [halo, *scalar, pltpu.VMEM((shards, outs + 1, here, width, channels), BF16)],
    )(valid_from, normed, partial, inner, outer, gain, spatial_weight, temporal_weight)

    half = channels // 2
    pre_gradient, inner, outer, *low = call(
        functools.partial(middle_kernel, **sizes, shards=shards),
        [
            ((rows, frames, width, channels), BF16),
            edge,
            edge,
            ((SPLIT * channels, half), F32),
            ((SPLIT * channels, half), BF16),
        ],
        [pltpu.VMEM((outs + 3, shards, here * width, channels), BF16)],
        flops=20 * cells * channels * channels,
        moved=6 * 1024 * 1024,
    )(
        tall, slope, active, parts, temporal_weight, mix_weight, cotangent[0],
        *reversed(pieces),
    )

    high = call(
        functools.partial(spatial_kernel, **sizes),
        [((size * channels, half), dtype) for size in (15 - SPLIT,) for dtype in (F32, BF16)],
        flops=16 * cells * channels * channels,
        moved=6 * 1024 * 1024,
    )(tall, pre_gradient)

    def shapes(rows_in, *types):
        return [((rows_in, half), dtype) for dtype in types]

    def halved(pieces):
        size = pieces[0].shape[0] // 2
        kept, send = call(halve_kernel, shapes(size, F32, BF16))(
            *[piece.reshape(2, size, half) for piece in pieces]
        )
        return (kept, pair(send, "tm", 1))

    def added(values):
        (total,) = call(add_kernel, shapes(values[0].shape[0], BF16))(*values)
        return total

    def doubled(total):
        for step in range(1, shards.bit_length() - 1):
            if step > 1:
                total = added((total, other))
            other = pair(total, "tm", 1 << step)
        return (total, other)

    def regained(values):
        total = added(values)
        return (total, pair(total, "tm", 1))

    def whole(values, axis, step):
        size = values[0].shape[0]
        (total,) = call(
            functools.partial(whole_kernel, axis=axis, step=step), [((2, size, half), BF16)]
        )(*values)
        return total.reshape(2 * size, half)

    def gathered(values):
        total = whole(values, "tm", 0)
        return [total] + pairs([total] * (lines - 1), "height")

    (low, low_send), (high, high_send) = (low, high)
    low_got = pair(low_send, "cam", 1)
    high_got = pair(high_send, "cam", 1)
    kept, *sends = call(deal_kernel, shapes(15 * channels // lines, F32, *[BF16] * (lines - 1)))(
        *[a.reshape(lines, -1, half) for a in (low, low_got, high, high_got)]
    )
    received = pairs(sends, "height")
    kept, *far = together(kept, *strided[2:])
    strided = strided[:2] + far
    strided = [strided[0]] + pairs(strided[1:], "tm")
    kept, *strided = together(kept, *strided)
    first = added(halved([kept] + received[::-1]))
    first, strided[0] = together(first, strided[0])
    (encoded,) = call(
        functools.partial(encode_kernel, width=width, shards=shards),
        [((shards * outs, here, width, channels), BF16)],
        [
            pltpu.VMEM(((shards * outs + 2) * here * width, channels), BF16),
            pltpu.VMEM((shards, outs + 1, here, width, channels), BF16),
        ],
        flops=3 * cells * channels * channels,
        moved=2 * 1024 * 1024,
    )(mix_weight, *strided)
    encoded, inner, outer = together(encoded, inner, outer)
    inner, outer = neighbours(inner, outer, "height")
    (halo_rows,) = call(halo_kernel, [((2, frames, width, channels), BF16)])(inner, outer)
    values = regained(doubled(first))
    values, halo_rows = together(values, halo_rows)
    pieces = gathered(values)
    (video_gradient,) = call(
        functools.partial(input_kernel, **sizes),
        [((frames, rows, width, channels), BF16)],
        [pltpu.VMEM((cells, 3 * channels), BF16)] + scalar,
        flops=18 * cells * channels * channels,
        moved=4 * 1024 * 1024,
    )(valid_from, video, pre_gradient, halo_rows, gain, spatial_weight)
    pieces[-1], video_gradient = together(pieces[-1], video_gradient)
    others = [pair(piece, "cam", 1) for piece in pieces]

    cell_count = cells * lax.axis_size("cam") * shards * lines
    scale = 1.0 / math.sqrt(cell_count)
    results = [((9, channels, channels), F32)] + [((3, channels, channels), F32)] * 2
    staged = pltpu.VMEM((15 * channels, half), F32)
    *results_own, total = call(
        functools.partial(finish_kernel, scale=scale, parts=lines, last=False),
        results + [((channels, half), F32)],
        [staged, pltpu.SemaphoreType.DMA((15,))],
        moved=4 * 1024 * 1024,
        far=3,
    )(*pieces, spatial_weight)
    spatial, temporal, mix, gain_gradient = call(
        functools.partial(finish_kernel, scale=scale, parts=lines, last=True),
        results + [((1, channels), F32)],
        [staged, pltpu.VMEM((1, channels), F32), pltpu.SemaphoreType.DMA((16,))],
        moved=4 * 1024 * 1024,
        far=4,
        aliases={lines + 3 + at: at for at in range(3)},
    )(*others, spatial_weight, total, gain, *results_own)

    return (
        encoded[None],
        video_gradient[None],
        spatial.reshape(spatial_weight.shape),
        temporal,
        mix,
        gain_gradient.reshape(channels),
    )


def solution(mesh):
    return jax.shard_map(
        on_device,
        mesh=mesh,
        in_specs=(
            P("cam", "tm", "height", None, None),
            P("cam"),
            P(),
            P(),
            P(),
            P(),
            P("cam", None, ("height", "tm"), None, None),
        ),
        out_specs=(
            P("cam", None, ("height", "tm"), None, None),
            P("cam", "tm", "height", None, None),
            P(),
            P(),
            P(),
            P(),
        ),
        check_vma=False,
    )
```

profile of v0, /device:TPU:0, one launch (start us, length us, event | category | flops | bytes accessed | tf_op | source)
XLA Modules:
  0.0 73.9 jit_solution(17846092248548902934)
XLA Ops:
  0.6 0.9 %copy-done.6 = bf16[1,8,1,64,256]{4,3,2,1,0:T(8,128)(2,1)S(1)} copy-done((bf16[1,8,1,64,256]{4,3,2,1,0:T(8,128)(2,1)S(1)}, bf16[1,8,1,64,256]{4,3,2,1,0:T(8,128)(2,1)}, u32[]{:S(2)}) %copy-start.6) | copy-done | bytes 262168
  2.2 5.1 %collective-permute-start.2 = (bf16[5,1,64,256]{3,2,1,0:T(8,128)(2,1)S(1)}, bf16[5,1,64,256]{3,2,1,0:T(8,128)(2,1)S(1)}, u32[]{:S(2)}, u32[]{:S(2)}) collective-permute-start(bf16[5,1,64,256]{3,2,1,0:T(8,128)(2,1)S(1)} %get-tuple-element.76), channel_id=1, source_target_pairs={{0,24},{8,16},{16,8},{24,0},{1,25},{9,17},{17,9},{25,1},{2,26},{10... | collective-permute-start | bytes 491528 | tf_op jit(solution)/shard_map/ppermute | solution.py:432
  8.0 1.0 %copy-done.2 = bf16[1,4,4,64,256]{4,3,2,1,0:T(8,128)(2,1)S(1)} copy-done((bf16[1,4,4,64,256]{4,3,2,1,0:T(8,128)(2,1)S(1)}, bf16[1,4,4,64,256]{4,3,2,1,0:T(8,128)(2,1)}, u32[]{:S(2)}) %copy-start.2) | copy-done | bytes 524312
  9.1 1.7 %collective-permute-start = (bf16[4,64,256]{2,1,0:T(8,128)(2,1)S(1)}, bf16[4,64,256]{2,1,0:T(8,128)(2,1)S(1)}, u32[]{:S(2)}, u32[]{:S(2)}) collective-permute-start(bf16[4,64,256]{2,1,0:T(8,128)(2,1)S(1)} %get-tuple-element.70), channel_id=1, source_target_pairs={{0,2},{2,0},{4,6},{6,4},{1,3},{3,1},{5,7},{7,5},{8,10},{10,8},{12,... | collective-permute-start | bytes 393224 | tf_op jit(solution)/shard_map/ppermute | solution.py:432
  10.8 0.7 collective-permute-start.1
  12.2 1.3 %copy-done = bf16[3,3,256,256]{3,2,1,0:T(8,128)(2,1)S(1)} copy-done((bf16[3,3,256,256]{3,2,1,0:T(8,128)(2,1)S(1)}, bf16[3,3,256,256]{3,2,1,0:T(8,128)(2,1)}, u32[]{:S(2)}) %copy-start) | copy-done | bytes 1179672
  13.4 0.7 copy-done.8
  14.1 1.9 %shard_map.118 = (bf16[1024,256]{1,0:T(8,128)(2,1)S(1)}, f32[1024,256]{1,0:T(8,128)S(1)}) custom-call(s32[1]{0:T(128)S(6)} %copy.20.valid_from, bf16[4,4,64,256]{3,2,1,0:T(8,128)(2,1)S(1)} %bitcast.26, f32[1,256]{1,0:T(1,128)S(1)} %bitcast.36, bf16[3,3,256,256]{3,2,1,0:T(8,128)(2,1)S(1)} %copy-done), custom_call_target="tpu_custom_call" | custom-call | flops 1207959552 | bytes 4194304 | tf_op jit(solution)/shard_map/pallas_call | solution.py:404
  16.0 1.7 %shard_map.121 = (bf16[1536,256]{1,0:T(8,128)(2,1)S(1)}, f32[1024,256]{1,0:T(8,128)S(1)}, bf16[2,512,256]{2,1,0:T(8,128)(2,1)S(1)}, bf16[768,256]{1,0:T(8,128)(2...) custom-call(s32[1]{0:T(128)S(6)} %copy.20.valid_from, ...), custom_call_target="tpu_custom_call" | custom-call | tf_op jit(solution)/shard_map/pallas_call | solution.py:404
  17.7 3.5 %collective-permute-done.3.refs_1_ = bf16[5,1,64,256]{3,2,1,0:T(8,128)(2,1)S(1)} collective-permute-done((bf16[5,1,64,256]{3,2,1,0:T(8,128)(2,1)S(1)}, bf16[5,1,64,256]{3,2,1,0:T(8,128)(2,1)S(1)}, u32[]{:S(2)}, u32[]{:S(2)}) %collective-permute-start.3) | collective-permute-done | bytes 163872 | tf_op jit(solution)/shard_map/ppermute | solution.py:432
  21.2 2.1 %shard_map.122 = (bf16[4,4,64,256]{3,2,1,0:T(8,128)(2,1)S(1)}, bf16[4,64,256]{2,1,0:T(8,128)(2,1)S(1)}, bf16[4,64,256]{2,1,0:T(8,128)(2,1)S(1)}, f32[2048,128]{1,0:T(8,128)S(1)}, bf16[2048,128]{1,0:T(8,128)(2,1)S(1)}) custom-call(bf16[1536,256]{1,0:T(8,128)(2,1)S(1)} %get-tuple-element.72.tall, f32[1024,256]{1,0:T(8,128)S(1)} %get-tuple-element.73.slope, ...), custom_call_target="tpu_custom_call" | custom-call | flops 1342177280 | bytes 6291456 | tf_op jit(solution)/shard_map/pallas_call | solution.py:404
  23.4 1.2 %shard_map.123 = (f32[1792,128]{1,0:T(8,128)S(1)}, bf16[1792,128]{1,0:T(8,128)(2,1)S(1)}) custom-call(bf16[1536,256]{1,0:T(8,128)(2,1)S(1)} %get-tuple-element.72.tall, bf16[4,4,64,256]{3,2,1,0:T(8,128)(2,1)S(1)} %get-tuple-element.81.pre_gradient), custom_call_target="tpu_custom_call" | custom-call | flops 1073741824 | bytes 6291456 | tf_op jit(solution)/shard_map/pallas_call | solution.py:404
  25.2 1.4 %collective-permute-done.6 = bf16[1792,128]{1,0:T(8,128)(2,1)S(1)} collective-permute-done((bf16[1792,128]{1,0:T(8,128)(2,1)S(1)}, bf16[1792,128]{1,0:T(8,128)(2,1)S(1)}, u32[]{:S(2)}, u32[]{:S(2)}) %collective-permute-start.6) | collective-permute-done | bytes 458784 | tf_op jit(solution)/shard_map/ppermute | solution.py:432
  26.8 2.5 %collective-permute-start.10 = (bf16[960,128]{1,0:T(8,128)(2,1)S(1)}, bf16[960,128]{1,0:T(8,128)(2,1)S(1)}, u32[]{:S(2)}, u32[]{:S(2)}) collective-permute-start(bf16[960,128]{1,0:T(8,128)(2,1)S(1)} %get-tuple-element.93), channel_id=1, source_target_pairs={{0,6},{2,4},{4,2},{6,0},{1,7},{3,5},{5,3},{7,1},{8,14},{10,12},{12... | collective-permute-start | bytes 737288 | tf_op jit(solution)/shard_map/ppermute | solution.py:432
  30.4 3.0 %collective-permute-start.8 = (bf16[3,1,64,256]{3,2,1,0:T(8,128)(2,1)S(1)}, bf16[3,1,64,256]{3,2,1,0:T(8,128)(2,1)S(1)}, u32[]{:S(2)}, u32[]{:S(2)}) collective-permute-start(bf16[3,1,64,256]{3,2,1,0:T(8,128)(2,1)S(1)} %get-tuple-element.90), channel_id=1, source_target_pairs={{0,16},{8,24},{16,0},{24,8},{1,17},{9,25},{17,1},{25,9},{2,18},{10... | collective-permute-start | bytes 294920 | tf_op jit(solution)/shard_map/ppermute | solution.py:432
  33.4 2.9 %collective-permute-done.7.refs_1_ = bf16[3,1,64,256]{3,2,1,0:T(8,128)(2,1)S(1)} collective-permute-done((bf16[3,1,64,256]{3,2,1,0:T(8,128)(2,1)S(1)}, bf16[3,1,64,256]{3,2,1,0:T(8,128)(2,1)S(1)}, u32[]{:S(2)}, u32[]{:S(2)}) %collective-permute-start.7) | collective-permute-done | bytes 98336 | tf_op jit(solution)/shard_map/ppermute | solution.py:432
  36.4 2.2 %collective-permute-start.9 = (bf16[3,1,64,256]{3,2,1,0:T(8,128)(2,1)S(1)}, bf16[3,1,64,256]{3,2,1,0:T(8,128)(2,1)S(1)}, u32[]{:S(2)}, u32[]{:S(2)}) collective-permute-start(bf16[3,1,64,256]{3,2,1,0:T(8,128)(2,1)S(1)} %get-tuple-element.91), channel_id=1, source_target_pairs={{0,24},{8,16},{16,8},{24,0},{1,25},{9,17},{17,9},{25,1},{2,26},{10... | collective-permute-start | bytes 294920 | tf_op jit(solution)/shard_map/ppermute | solution.py:432
  38.6 1.0 %collective-permute-done.8.refs_2_ = bf16[3,1,64,256]{3,2,1,0:T(8,128)(2,1)S(1)} collective-permute-done((bf16[3,1,64,256]{3,2,1,0:T(8,128)(2,1)S(1)}, bf16[3,1,64,256]{3,2,1,0:T(8,128)(2,1)S(1)}, u32[]{:S(2)}, u32[]{:S(2)}) %collective-permute-start.8) | collective-permute-done | bytes 98336 | tf_op jit(solution)/shard_map/ppermute | solution.py:432
  39.5 3.2 %collective-permute-done.9.refs_3_ = bf16[3,1,64,256]{3,2,1,0:T(8,128)(2,1)S(1)} collective-permute-done((bf16[3,1,64,256]{3,2,1,0:T(8,128)(2,1)S(1)}, bf16[3,1,64,256]{3,2,1,0:T(8,128)(2,1)S(1)}, u32[]{:S(2)}, u32[]{:S(2)}) %collective-permute-start.9) | collective-permute-done | bytes 98336 | tf_op jit(solution)/shard_map/ppermute | solution.py:432
  43.0 4.9 %collective-permute-done.13.right = bf16[480,128]{1,0:T(8,128)(2,1)S(1)} collective-permute-done((bf16[480,128]{1,0:T(8,128)(2,1)S(1)}, bf16[480,128]{1,0:T(8,128)(2,1)S(1)}, u32[]{:S(2)}, u32[]{:S(2)}) %collective-permute-start.13) | collective-permute-done | bytes 122912 | tf_op jit(solution)/shard_map/ppermute | solution.py:432
  47.9 0.8 %collective-permute-start.14 = (bf16[480,128]{1,0:T(8,128)(2,1)S(1)}, bf16[480,128]{1,0:T(8,128)(2,1)S(1)}, u32[]{:S(2)}, u32[]{:S(2)}) collective-permute-start(bf16[480,128]{1,0:T(8,128)(2,1)S(1)} %shard_map.126.left), channel_id=1, source_target_pairs={{0,16},{8,24},{16,0},{24,8},{1,17},{9,25},{17,1},{25,9},{2,18},{10... | collective-permute-start | bytes 368648 | tf_op jit(solution)/shard_map/ppermute | solution.py:432
  48.7 1.1 %shard_map.127 = bf16[8,1,64,256]{3,2,1,0:T(8,128)(2,1)} custom-call(bf16[3,256,256]{2,1,0:T(8,128)(2,1)S(1)} %copy-done.4, bf16[3,1,64,256]{3,2,1,0:T(8,128)(2,1)S(1)} %get-tuple-element.99.refs_0_, bf16[3,1,64,256]{3,2,1,0:T(8,128)(2,1)S(1)} %collective-permute-done.7.refs_1_, bf16[3,1,64,256]{3,2,1,0:T(8,128)(2,1)S(1)} %collective-permute-done.8.refs_2_, ...), custom_call_target="tpu_custom_call" | custom-call | flops 201326592 | bytes 2097152 | tf_op jit(solution)/shard_map/pallas_call | solution.py:404
  49.8 1.7 %collective-permute-start.16 = (bf16[4,64,256]{2,1,0:T(8,128)(2,1)S(1)}, bf16[4,64,256]{2,1,0:T(8,128)(2,1)S(1)}, u32[]{:S(2)}, u32[]{:S(2)}) collective-permute-start(bf16[4,64,256]{2,1,0:T(8,128)(2,1)S(1)} %get-tuple-element.107), channel_id=1, source_target_pairs={{0,2},{2,0},{4,6},{6,4},{1,3},{3,1},{5,7},{7,5},{8,10},{10,8},{12,... | collective-permute-start | bytes 393224 | tf_op jit(solution)/shard_map/ppermute | solution.py:432
  52.2 2.4 %collective-permute-done.14.right = bf16[480,128]{1,0:T(8,128)(2,1)S(1)} collective-permute-done((bf16[480,128]{1,0:T(8,128)(2,1)S(1)}, bf16[480,128]{1,0:T(8,128)(2,1)S(1)}, u32[]{:S(2)}, u32[]{:S(2)}) %collective-permute-start.14) | collective-permute-done | bytes 122912 | tf_op jit(solution)/shard_map/ppermute | solution.py:432
  54.7 1.2 %collective-permute-done.16.inner = bf16[4,64,256]{2,1,0:T(8,128)(2,1)S(1)} collective-permute-done((bf16[4,64,256]{2,1,0:T(8,128)(2,1)S(1)}, bf16[4,64,256]{2,1,0:T(8,128)(2,1)S(1)}, u32[]{:S(2)}, u32[]{:S(2)}) %collective-permute-start.16) | collective-permute-done | bytes 131104 | tf_op jit(solution)/shard_map/ppermute | solution.py:432
  55.9 3.6 %collective-permute-done.15.other = bf16[480,128]{1,0:T(8,128)(2,1)S(1)} collective-permute-done((bf16[480,128]{1,0:T(8,128)(2,1)S(1)}, bf16[480,128]{1,0:T(8,128)(2,1)S(1)}, u32[]{:S(2)}, u32[]{:S(2)}) %collective-permute-start.15) | collective-permute-done | bytes 122912 | tf_op jit(solution)/shard_map/ppermute | solution.py:432
  59.6 2.8 %collective-permute-start.18 = (bf16[960,128]{1,0:T(8,128)(2,1)S(1)}, bf16[960,128]{1,0:T(8,128)(2,1)S(1)}, u32[]{:S(2)}, u32[]{:S(2)}) collective-permute-start(bf16[960,128]{1,0:T(8,128)(2,1)S(1)} %bitcast.19), channel_id=1, source_target_pairs={{0,6},{2,4},{4,2},{6,0},{1,7},{3,5},{5,3},{7,1},{8,14},{10,12},{12... | collective-permute-start | bytes 737288 | tf_op jit(solution)/shard_map/ppermute | solution.py:432
  63.1 2.9 %shard_map.131 = bf16[4,4,64,256]{3,2,1,0:T(8,128)(2,1)} custom-call(s32[1]{0:T(128)S(6)} %copy.20.valid_from, bf16[4,4,64,256]{3,2,1,0:T(8,128)(2,1)S(1)} %bitcast.27, bf16[4,4,64,256]{3,2,1,0:T(8,128)(2,1)S(1)} %get-tuple-element.81.pre_gradient, bf16[2,4,64,256]{3,2,1,0:T(8,128)(2,1)S(1)} %shard_map.129.halo, f32[1,256]{1,0:T(1,128)S(1)} %bitcast.38, ...), custom_call_target="tpu_custom_call" | custom-call | flops 1207959552 | bytes 4194304 | tf_op jit(solution)/shard_map/pallas_call | solution.py:404
  66.1 1.5 %collective-permute-done.18.refs_3_ = bf16[960,128]{1,0:T(8,128)(2,1)S(1)} collective-permute-done((bf16[960,128]{1,0:T(8,128)(2,1)S(1)}, bf16[960,128]{1,0:T(8,128)(2,1)S(1)}, u32[]{:S(2)}, u32[]{:S(2)}) %collective-permute-start.18) | collective-permute-done | bytes 245792 | tf_op jit(solution)/shard_map/ppermute | solution.py:432
  67.6 2.5 %collective-permute-done.22.refs_2_ = bf16[960,128]{1,0:T(8,128)(2,1)S(1)} collective-permute-done((bf16[960,128]{1,0:T(8,128)(2,1)S(1)}, bf16[960,128]{1,0:T(8,128)(2,1)S(1)}, u32[]{:S(2)}, u32[]{:S(2)}) %collective-permute-start.22) | collective-permute-done | bytes 245792 | tf_op jit(solution)/shard_map/ppermute | solution.py:432
  70.6 1.6 %shard_map.132 = (f32[9,256,256]{2,1,0:T(8,128)}, f32[3,256,256]{2,1,0:T(8,128)}, f32[3,256,256]{2,1,0:T(8,128)}, f32[256,128]{1,0:T(8,128)S(1)}) custom-call(bf16[960,128]{1,0:T(8,128)(2,1)S(1)} %bitcast.23, bf16[960,128]{1,0:T(8,128)(2,1)S(1)} %collective-permute-done.20.refs_1_, bf16[960,128]{1,0:T(8,128)(2,1)S(1)} %collective-permute-done.22.refs_2_, ...), custom_call_target="tpu_custom_call" | custom-call | bytes 4194304 | tf_op jit(solution)/shard_map/pallas_call | solution.py:404
  72.3 1.6 %shard_map.133 = (f32[9,256,256]{2,1,0:T(8,128)}, f32[3,256,256]{2,1,0:T(8,128)}, f32[3,256,256]{2,1,0:T(8,128)}, f32[1,256]{1,0:T(1,128)}) custom-call(bf16[960,128]{1,0:T(8,128)(2,1)S(1)} %collective-permute-done.19.refs_0_, bf16[960,128]{1,0:T(8,128)(2,1)S(1)} %collective-permute-done.21.refs_1_, ...), custom_call_target="tpu_custom_call", output_to_operand_aliasing={{0}: (7, {}), {1}: (8, {}), {2}: (9, {})} | custom-call | bytes 4194304 | tf_op jit(solution)/shard_map/pallas_call | solution.py:404
  (54 shorter events, 5.7 us)
Async XLA Ops:
  2.2 15.5 %collective-permute-start.2 = (bf16[5,1,64,256]{3,2,1,0:T(8,128)(2,1)S(1)}, bf16[5,1,64,256]{3,2,1,0:T(8,128)(2,1)S(1)}, u32[]{:S(2)}, u32[]{:S(2)}) collective-permute-start(bf16[5,1,64,256]{3,2,1,0:T(8,128)(2,1)S(1)} %get-tuple-element.76), channel_id=1, source_target_pairs={{0,24},{8,16},{16,8},{24,0},{1,25},{9,17},{17,9},{25,1},{2,26},{10... | collective-permute-start | bytes 491528 | tf_op jit(solution)/shard_map/ppermute | solution.py:432
  7.3 13.9 %collective-permute-start.3 = (bf16[5,1,64,256]{3,2,1,0:T(8,128)(2,1)S(1)}, bf16[5,1,64,256]{3,2,1,0:T(8,128)(2,1)S(1)}, u32[]{:S(2)}, u32[]{:S(2)}) collective-permute-start(bf16[5,1,64,256]{3,2,1,0:T(8,128)(2,1)S(1)} %get-tuple-element.77), channel_id=1, source_target_pairs={{0,16},{8,24},{16,0},{24,8},{1,17},{9,25},{17,1},{25,9},{2,18},{10... | collective-permute-start | bytes 491528 | tf_op jit(solution)/shard_map/ppermute | solution.py:432
  7.3 13.9 %collective-permute-start.4 = (bf16[5,1,64,256]{3,2,1,0:T(8,128)(2,1)S(1)}, bf16[5,1,64,256]{3,2,1,0:T(8,128)(2,1)S(1)}, u32[]{:S(2)}, u32[]{:S(2)}) collective-permute-start(bf16[5,1,64,256]{3,2,1,0:T(8,128)(2,1)S(1)} %get-tuple-element.78), channel_id=1, source_target_pairs={{0,8},{8,0},{16,24},{24,16},{1,9},{9,1},{17,25},{25,17},{2,10},{10... | collective-permute-start | bytes 491528 | tf_op jit(solution)/shard_map/ppermute | solution.py:432
  9.0 7.0 %copy-start.5 = (bf16[3,256,256]{2,1,0:T(8,128)(2,1)S(1)}, bf16[3,256,256]{2,1,0:T(8,128)(2,1)}, u32[]{:S(2)}) copy-start(bf16[3,256,256]{2,1,0:T(8,128)(2,1)} %temporal.3) | copy-start | bytes 1179652
  9.1 6.9 %collective-permute-start = (bf16[4,64,256]{2,1,0:T(8,128)(2,1)S(1)}, bf16[4,64,256]{2,1,0:T(8,128)(2,1)S(1)}, u32[]{:S(2)}, u32[]{:S(2)}) collective-permute-start(bf16[4,64,256]{2,1,0:T(8,128)(2,1)S(1)} %get-tuple-element.70), channel_id=1, source_target_pairs={{0,2},{2,0},{4,6},{6,4},{1,3},{3,1},{5,7},{7,5},{8,10},{10,8},{12,... | collective-permute-start | bytes 393224 | tf_op jit(solution)/shard_map/ppermute | solution.py:432
  10.8 5.2 %collective-permute-start.1 = (bf16[4,64,256]{2,1,0:T(8,128)(2,1)S(1)}, bf16[4,64,256]{2,1,0:T(8,128)(2,1)S(1)}, u32[]{:S(2)}, u32[]{:S(2)}) collective-permute-start(bf16[4,64,256]{2,1,0:T(8,128)(2,1)S(1)} %get-tuple-element.71), channel_id=1, source_target_pairs={{2,4},{4,2},{3,5},{5,3},{10,12},{12,10},{11,13},{13,11},{18,20},{2... | collective-permute-start | bytes 393224 | tf_op jit(solution)/shard_map/ppermute | solution.py:428
  12.1 1.3 %copy-start = (bf16[3,3,256,256]{3,2,1,0:T(8,128)(2,1)S(1)}, bf16[3,3,256,256]{3,2,1,0:T(8,128)(2,1)}, u32[]{:S(2)}) copy-start(bf16[3,3,256,256]{3,2,1,0:T(8,128)(2,1)} %refs_4_.3) | copy-start | bytes 3538948
  14.1 1.9 %copy-start.1 = (bf16[3,3,256,256]{3,2,1,0:T(8,128)(2,1)S(1)}, bf16[3,3,256,256]{3,2,1,0:T(8,128)(2,1)}, u32[]{:S(2)}) copy-start(bf16[3,3,256,256]{3,2,1,0:T(8,128)(2,1)} %refs_4_.3) | copy-start | bytes 3538948
  16.0 5.2 %copy-start.4 = (bf16[3,256,256]{2,1,0:T(8,128)(2,1)S(1)}, bf16[3,256,256]{2,1,0:T(8,128)(2,1)}, u32[]{:S(2)}) copy-start(bf16[3,256,256]{2,1,0:T(8,128)(2,1)} %mix.3) | copy-start | bytes 1179652
  16.0 5.2 %copy-start.7 = (bf16[1,8,1,64,256]{4,3,2,1,0:T(8,128)(2,1)S(1)}, bf16[1,8,1,64,256]{4,3,2,1,0:T(8,128)(2,1)}, u32[]{:S(2)}) copy-start(bf16[1,8,1,64,256]{4,3,2,1,0:T(8,128)(2,1)} %param.13) | copy-start | bytes 786436
  23.3 3.3 %collective-permute-start.5 = (bf16[2048,128]{1,0:T(8,128)(2,1)S(1)}, bf16[2048,128]{1,0:T(8,128)(2,1)S(1)}, u32[]{:S(2)}, u32[]{:S(2)}) collective-permute-start(bf16[2048,128]{1,0:T(8,128)(2,1)S(1)} %get-tuple-element.80), channel_id=1, source_target_pairs={{0,1},{1,0},{2,3},{3,2},{4,5},{5,4},{6,7},{7,6},{8,9},{9,8},{10,11... | collective-permute-start | bytes 1572872 | tf_op jit(solution)/shard_map/ppermute | solution.py:432
  24.6 2.0 %collective-permute-start.6 = (bf16[1792,128]{1,0:T(8,128)(2,1)S(1)}, bf16[1792,128]{1,0:T(8,128)(2,1)S(1)}, u32[]{:S(2)}, u32[]{:S(2)}) collective-permute-start(bf16[1792,128]{1,0:T(8,128)(2,1)S(1)} %get-tuple-element.83), channel_id=1, source_target_pairs={{0,1},{1,0},{2,3},{3,2},{4,5},{5,4},{6,7},{7,6},{8,9},{9,8},{10,11... | collective-permute-start | bytes 1376264 | tf_op jit(solution)/shard_map/ppermute | solution.py:432
  26.8 36.4 %copy-start.3 = (bf16[1,4,4,64,256]{4,3,2,1,0:T(8,128)(2,1)S(1)}, bf16[1,4,4,64,256]{4,3,2,1,0:T(8,128)(2,1)}, u32[]{:S(2)}) copy-start(bf16[1,4,4,64,256]{4,3,2,1,0:T(8,128)(2,1)} %param.7) | copy-start | bytes 1572868
  26.8 36.4 %copy-start.9 = (f32[256]{0:T(256)S(1)}, f32[256]{0:T(256)}, u32[]{:S(2)}) copy-start(f32[256]{0:T(256)} %param.9) | copy-start | bytes 3076
  26.8 16.0 %collective-permute-start.10 = (bf16[960,128]{1,0:T(8,128)(2,1)S(1)}, bf16[960,128]{1,0:T(8,128)(2,1)S(1)}, u32[]{:S(2)}, u32[]{:S(2)}) collective-permute-start(bf16[960,128]{1,0:T(8,128)(2,1)S(1)} %get-tuple-element.93), channel_id=1, source_target_pairs={{0,6},{2,4},{4,2},{6,0},{1,7},{3,5},{5,3},{7,1},{8,14},{10,12},{12... | collective-permute-start | bytes 737288 | tf_op jit(solution)/shard_map/ppermute | solution.py:432
  29.3 13.5 %collective-permute-start.11 = (bf16[960,128]{1,0:T(8,128)(2,1)S(1)}, bf16[960,128]{1,0:T(8,128)(2,1)S(1)}, u32[]{:S(2)}, u32[]{:S(2)}) collective-permute-start(bf16[960,128]{1,0:T(8,128)(2,1)S(1)} %get-tuple-element.94), channel_id=1, source_target_pairs={{0,4},{2,6},{4,0},{6,2},{1,5},{3,7},{5,1},{7,3},{8,12},{10,14},{12... | collective-permute-start | bytes 737288 | tf_op jit(solution)/shard_map/ppermute | solution.py:432
  29.8 12.9 %collective-permute-start.12 = (bf16[960,128]{1,0:T(8,128)(2,1)S(1)}, bf16[960,128]{1,0:T(8,128)(2,1)S(1)}, u32[]{:S(2)}, u32[]{:S(2)}) collective-permute-start(bf16[960,128]{1,0:T(8,128)(2,1)S(1)} %get-tuple-element.95), channel_id=1, source_target_pairs={{0,2},{2,0},{4,6},{6,4},{1,3},{3,1},{5,7},{7,5},{8,10},{10,8},{12,... | collective-permute-start | bytes 737288 | tf_op jit(solution)/shard_map/ppermute | solution.py:432
  30.4 6.0 %collective-permute-start.7 = (bf16[3,1,64,256]{3,2,1,0:T(8,128)(2,1)S(1)}, bf16[3,1,64,256]{3,2,1,0:T(8,128)(2,1)S(1)}, u32[]{:S(2)}, u32[]{:S(2)}) collective-permute-start(bf16[3,1,64,256]{3,2,1,0:T(8,128)(2,1)S(1)} %get-tuple-element.89), channel_id=1, source_target_pairs={{0,8},{8,0},{16,24},{24,16},{1,9},{9,1},{17,25},{25,17},{2,10},{10... | collective-permute-start | bytes 294920 | tf_op jit(solution)/shard_map/ppermute | solution.py:432
  30.4 9.1 %collective-permute-start.8 = (bf16[3,1,64,256]{3,2,1,0:T(8,128)(2,1)S(1)}, bf16[3,1,64,256]{3,2,1,0:T(8,128)(2,1)S(1)}, u32[]{:S(2)}, u32[]{:S(2)}) collective-permute-start(bf16[3,1,64,256]{3,2,1,0:T(8,128)(2,1)S(1)} %get-tuple-element.90), channel_id=1, source_target_pairs={{0,16},{8,24},{16,0},{24,8},{1,17},{9,25},{17,1},{25,9},{2,18},{10... | collective-permute-start | bytes 294920 | tf_op jit(solution)/shard_map/ppermute | solution.py:432
  36.4 6.4 %collective-permute-start.9 = (bf16[3,1,64,256]{3,2,1,0:T(8,128)(2,1)S(1)}, bf16[3,1,64,256]{3,2,1,0:T(8,128)(2,1)S(1)}, u32[]{:S(2)}, u32[]{:S(2)}) collective-permute-start(bf16[3,1,64,256]{3,2,1,0:T(8,128)(2,1)S(1)} %get-tuple-element.91), channel_id=1, source_target_pairs={{0,24},{8,16},{16,8},{24,0},{1,25},{9,17},{17,9},{25,1},{2,26},{10... | collective-permute-start | bytes 294920 | tf_op jit(solution)/shard_map/ppermute | solution.py:432
  42.9 4.9 %collective-permute-start.13 = (bf16[480,128]{1,0:T(8,128)(2,1)S(1)}, bf16[480,128]{1,0:T(8,128)(2,1)S(1)}, u32[]{:S(2)}, u32[]{:S(2)}) collective-permute-start(bf16[480,128]{1,0:T(8,128)(2,1)S(1)} %get-tuple-element.97), channel_id=1, source_target_pairs={{0,8},{8,0},{16,24},{24,16},{1,9},{9,1},{17,25},{25,17},{2,10},{10... | collective-permute-start | bytes 368648 | tf_op jit(solution)/shard_map/ppermute | solution.py:432
  47.9 6.7 %collective-permute-start.14 = (bf16[480,128]{1,0:T(8,128)(2,1)S(1)}, bf16[480,128]{1,0:T(8,128)(2,1)S(1)}, u32[]{:S(2)}, u32[]{:S(2)}) collective-permute-start(bf16[480,128]{1,0:T(8,128)(2,1)S(1)} %shard_map.126.left), channel_id=1, source_target_pairs={{0,16},{8,24},{16,0},{24,8},{1,17},{9,25},{17,1},{25,9},{2,18},{10... | collective-permute-start | bytes 368648 | tf_op jit(solution)/shard_map/ppermute | solution.py:432
  49.8 6.1 %collective-permute-start.16 = (bf16[4,64,256]{2,1,0:T(8,128)(2,1)S(1)}, bf16[4,64,256]{2,1,0:T(8,128)(2,1)S(1)}, u32[]{:S(2)}, u32[]{:S(2)}) collective-permute-start(bf16[4,64,256]{2,1,0:T(8,128)(2,1)S(1)} %get-tuple-element.107), channel_id=1, source_target_pairs={{0,2},{2,0},{4,6},{6,4},{1,3},{3,1},{5,7},{7,5},{8,10},{10,8},{12,... | collective-permute-start | bytes 393224 | tf_op jit(solution)/shard_map/ppermute | solution.py:432
  51.5 4.4 %collective-permute-start.17 = (bf16[4,64,256]{2,1,0:T(8,128)(2,1)S(1)}, bf16[4,64,256]{2,1,0:T(8,128)(2,1)S(1)}, u32[]{:S(2)}, u32[]{:S(2)}) collective-permute-start(bf16[4,64,256]{2,1,0:T(8,128)(2,1)S(1)} %get-tuple-element.108), channel_id=1, source_target_pairs={{2,4},{4,2},{3,5},{5,3},{10,12},{12,10},{11,13},{13,11},{18,20},{2... | collective-permute-start | bytes 393224 | tf_op jit(solution)/shard_map/ppermute | solution.py:428
  54.6 4.9 %collective-permute-start.15 = (bf16[480,128]{1,0:T(8,128)(2,1)S(1)}, bf16[480,128]{1,0:T(8,128)(2,1)S(1)}, u32[]{:S(2)}, u32[]{:S(2)}) collective-permute-start(bf16[480,128]{1,0:T(8,128)(2,1)S(1)} %shard_map.128.mine), channel_id=1, source_target_pairs={{0,8},{8,0},{16,24},{24,16},{1,9},{9,1},{17,25},{25,17},{2,10},{10... | collective-permute-start | bytes 368648 | tf_op jit(solution)/shard_map/ppermute | solution.py:432
  59.6 8.0 %collective-permute-start.18 = (bf16[960,128]{1,0:T(8,128)(2,1)S(1)}, bf16[960,128]{1,0:T(8,128)(2,1)S(1)}, u32[]{:S(2)}, u32[]{:S(2)}) collective-permute-start(bf16[960,128]{1,0:T(8,128)(2,1)S(1)} %bitcast.19), channel_id=1, source_target_pairs={{0,6},{2,4},{4,2},{6,0},{1,7},{3,5},{5,3},{7,1},{8,14},{10,12},{12... | collective-permute-start | bytes 737288 | tf_op jit(solution)/shard_map/ppermute | solution.py:432
  62.4 7.7 %collective-permute-start.22 = (bf16[960,128]{1,0:T(8,128)(2,1)S(1)}, bf16[960,128]{1,0:T(8,128)(2,1)S(1)}, u32[]{:S(2)}, u32[]{:S(2)}) collective-permute-start(bf16[960,128]{1,0:T(8,128)(2,1)S(1)} %bitcast.20), channel_id=1, source_target_pairs={{0,4},{2,6},{4,0},{6,2},{1,5},{3,7},{5,1},{7,3},{8,12},{10,14},{12... | collective-permute-start | bytes 737288 | tf_op jit(solution)/shard_map/ppermute | solution.py:432
  62.7 7.4 %collective-permute-start.20 = (bf16[960,128]{1,0:T(8,128)(2,1)S(1)}, bf16[960,128]{1,0:T(8,128)(2,1)S(1)}, u32[]{:S(2)}, u32[]{:S(2)}) collective-permute-start(bf16[960,128]{1,0:T(8,128)(2,1)S(1)} %bitcast.21), channel_id=1, source_target_pairs={{0,2},{2,0},{4,6},{6,4},{1,3},{3,1},{5,7},{7,5},{8,10},{10,8},{12,... | collective-permute-start | bytes 737288 | tf_op jit(solution)/shard_map/ppermute | solution.py:432
  63.1 9.0 %collective-permute-start.19 = (bf16[960,128]{1,0:T(8,128)(2,1)S(1)}, bf16[960,128]{1,0:T(8,128)(2,1)S(1)}, u32[]{:S(2)}, u32[]{:S(2)}) collective-permute-start(bf16[960,128]{1,0:T(8,128)(2,1)S(1)} %bitcast.22), channel_id=1, source_target_pairs={{0,1},{1,0},{2,3},{3,2},{4,5},{5,4},{6,7},{7,6},{8,9},{9,8},{10,11... | collective-permute-start | bytes 737288 | tf_op jit(solution)/shard_map/ppermute | solution.py:432
  70.1 2.1 %collective-permute-start.23 = (bf16[960,128]{1,0:T(8,128)(2,1)S(1)}, bf16[960,128]{1,0:T(8,128)(2,1)S(1)}, u32[]{:S(2)}, u32[]{:S(2)}) collective-permute-start(bf16[960,128]{1,0:T(8,128)(2,1)S(1)} %collective-permute-done.22.refs_2_), channel_id=1, source_target_pairs={{0,1},{1,0},{2,3},{3,2},{4,5},{5,4},{6,7},{7,6},{8,9},{9,8},{10,11... | collective-permute-start | bytes 737288 | tf_op jit(solution)/shard_map/ppermute | solution.py:432
  70.1 2.1 %collective-permute-start.21 = (bf16[960,128]{1,0:T(8,128)(2,1)S(1)}, bf16[960,128]{1,0:T(8,128)(2,1)S(1)}, u32[]{:S(2)}, u32[]{:S(2)}) collective-permute-start(bf16[960,128]{1,0:T(8,128)(2,1)S(1)} %collective-permute-done.20.refs_1_), channel_id=1, source_target_pairs={{0,1},{1,0},{2,3},{3,2},{4,5},{5,4},{6,7},{7,6},{8,9},{9,8},{10,11... | collective-permute-start | bytes 737288 | tf_op jit(solution)/shard_map/ppermute | solution.py:432
  70.6 1.7 %collective-permute-start.24 = (bf16[960,128]{1,0:T(8,128)(2,1)S(1)}, bf16[960,128]{1,0:T(8,128)(2,1)S(1)}, u32[]{:S(2)}, u32[]{:S(2)}) collective-permute-start(bf16[960,128]{1,0:T(8,128)(2,1)S(1)} %collective-permute-done.18.refs_3_), channel_id=1, source_target_pairs={{0,1},{1,0},{2,3},{3,2},{4,5},{5,4},{6,7},{7,6},{8,9},{9,8},{10,11... | collective-permute-start | bytes 737288 | tf_op jit(solution)/shard_map/ppermute | solution.py:432
  (3 other events, 2.7 us)
where the time goes:
time: 74.2 us; the launch traced here: 73.9 us
  waiting for transfers between devices  28.3 us (38%)
  starting transfers between devices  25 us (34%)
  Pallas kernels  15.1 us (20%)
  local copies, waits for them, and re-layouts  3.96 us (5%)
  between operations  1.56 us (2%)
    ppermute x23, waiting for transfers between devices, pair(): lax.ppermute(array, axis, [(i, i ^ step) for i in range(lax.axis_size(axi...  28.3 us
    ppermute x23, starting transfers between devices, pair(): lax.ppermute(array, axis, [(i, i ^ step) for i in range(lax.axis_size(axi...  23.7 us
    pallas_call x16, Pallas kernels, run(): pl.pallas_call(kernel, out_shape=[jax.ShapeDtypeStruct(shape, dtype) for...  15.1 us
    unnamed x20, local copies, waits for them, and re-layouts  3.96 us
  transfers between devices with their start and end apart: 25, of which 12 were waited for; matrix products, arithmetic and copies ran while one was open for 0% of the time, Pallas kernels for 14%

commit v1 on v0

--- a/solution.py
+++ b/solution.py
@@ -72,14 +72,14 @@
     run_copies(copies, done)
 
 
-def edges_kernel(video, inner, outer, done, *, rows):
+def edges_kernel(source, inner, outer, done, *, rows, frames_first):
     odd = lax.axis_index("height") % 2
+
+    def row(at):
+        return source.at[:, at] if frames_first else source.at[at]
+
     run_copies(
-        [
-            (video.at[:, (1 - odd) * (rows - 1)], inner),
-            (video.at[:, odd * (rows - 1)], outer),
-        ],
-        done,
+        [(row((1 - odd) * (rows - 1)), inner), (row(odd * (rows - 1)), outer)], done
     )
 
 
@@ -127,7 +127,7 @@
     frames, rows, width, shards
 ):
     tall, slope, active, parts, *refs = refs
-    strided, (halo, start, done, lines) = (refs[:shards], refs[shards:])
+    strided, (halo, start, done, lines) = (refs[:2], refs[2:])
     outs = frames // 2
     plane = rows * width
     here = rows // shards
@@ -168,15 +168,26 @@
     for frame in range(outs + 1):
         cells = pieces[frame * plane : frame * plane + plane]
         lines[:, frame] = cells.reshape(shards, here, width, 256)
-    for step, piece in enumerate(strided):
-        piece[...] = lines[lax.axis_index("tm") ^ step]
+    stay, leave = strided
+    for step in range(shards):
+        target = leave if step % 2 else stay
+        target[0, step // 2] = lines[lax.axis_index("tm") ^ step]
+
+
+def split_kernel(stay_in, came_in, stay, leave):
+    count, pieces = stay_in.shape[:2]
+    for place, source in enumerate((stay_in, came_in)):
+        for at in range(count):
+            for piece in range(pieces):
+                target = leave if piece % 2 else stay
+                target[place * count + at, piece // 2] = source[at, piece]
 
 
 def middle_kernel(
     tall, slope, active, parts, temporal, mix, cotangent, *refs, frames, rows, width, shards
 ):
     pieces, refs = (refs[: shards - 1], refs[shards - 1 :])
-    pre_gradient, inner_out, outer_out, keep, send, cot = refs
+    pre_gradient, keep, send, cot = refs
     outs = frames // 2
     plane = rows * width
     here = rows // shards
@@ -210,9 +221,6 @@
             to = (row * frames + frame) * width
             tile = (source[at : at + width] * slope[to : to + width]).astype(BF16)
             pre_gradient[row, frame] = tile
-    side = (lax.axis_index("height") % 2) * (rows - 1)
-    inner_out[...] = pre_gradient[rows - 1 - side]
-    outer_out[...] = pre_gradient[side]
     evens = active[0]
     odds = active[1]
     for k in range(3):
@@ -264,41 +272,32 @@
     return (mine, other)
 
 
-def deal_kernel(low, low_got, high, high_got, kept, *sends):
+def deal_kernel(low, low_got, high, high_got, *outs):
     me = lax.axis_index("height")
-    cut = low.shape[1]
-
-    def fill(target, at):
-        target[:cut] = (low[at] + low_got[at].astype(F32)).astype(target.dtype)
-        target[cut:] = (high[at] + high_got[at].astype(F32)).astype(target.dtype)
-
-    fill(kept, me)
-    for step, send in enumerate(sends):
-        fill(send, me ^ (step + 1))
-
-
-def halve_kernel(*refs):
-    (kept_in, *received), (kept, send) = (refs[:-2], refs[-2:])
-    mine = lax.axis_index("tm") % 2
-
-    def total(at):
-        value = kept_in[at]
-        for piece in received:
-            value = value + piece[at].astype(F32)
-        return value
-
-    kept[...] = total(mine)
-    send[...] = total(1 - mine).astype(BF16)
+    home = lax.axis_index("tm") % 2
+    cut = low.shape[2]
+    count = len(outs) // 2
+    for target, half in [(outs[:count], 1 - home), (outs[count:], home)]:
+        for step, out in enumerate(target):
+            at = me ^ step
+            out[:cut] = (low[at, half] + low_got[at, half].astype(F32)).astype(out.dtype)
+            out[cut:] = (high[at, half] + high_got[at, half].astype(F32)).astype(out.dtype)
+
+
+def gather_sum_kernel(kept, *refs):
+    value = kept[...]
+    for piece in refs[:-1]:
+        value = value + piece[...].astype(F32)
+    refs[-1][...] = value.astype(BF16)
 
 
 def add_kernel(left, right, out):
     out[...] = (left[...].astype(F32) + right[...].astype(F32)).astype(BF16)
 
 
-def whole_kernel(mine, other, out, *, axis, step):
-    at = (lax.axis_index(axis) >> step) % 2
-    out[at] = mine[...]
-    out[1 - at] = other[...]
+def join_kernel(*refs):
+    for step, piece in enumerate(refs[:-1]):
+        refs[-1][lax.axis_index("height") ^ step] = piece[...]
 
 
 def input_kernel(
@@ -335,10 +334,10 @@
             out[frame, row] = (inverse * (tile - unit * mean) * keep).astype(BF16)
 
 
-def encode_kernel(mix, *refs, width, shards):
-    pieces, (out, line, strided) = (refs[:shards], refs[shards:])
-    for step, piece in enumerate(pieces):
-        strided[lax.axis_index("tm") ^ step] = piece[...]
+def encode_kernel(mix, stay, came, out, line, strided, *, width, shards):
+    for step in range(shards):
+        source = came if step >= shards // 2 else stay
+        strided[lax.axis_index("tm") ^ step] = source[step % (shards // 2), 0]
     parts, here = strided.shape[1:3]
     outs = parts - 1
     plane = here * width
@@ -358,8 +357,7 @@
     out[...] = result.astype(BF16).reshape(out.shape)
 
 
-def finish_kernel(*refs, scale, parts, last):
-    (pieces, weight, refs) = (refs[:parts], refs[parts], refs[parts + 1 :])
+def finish_kernel(home, away, weight, *refs, scale, last):
     if last:
         before, gain, _, _, _, spatial, temporal, mix, gain_out, staged, row, done = refs
         total = before[...]
@@ -367,13 +365,15 @@
         spatial, temporal, mix, after, staged, done = refs
         total = jnp.zeros((256, 128), F32)
     columns = core_columns()[1 if last else 0]
-    low, high = (SPLIT * 256 // parts, (15 - SPLIT) * 256 // parts)
-    for step, piece in enumerate(pieces):
-        part = lax.axis_index("height") ^ step
-        at = pl.multiple_of(part * low, low)
-        staged[pl.ds(at, low)] = piece[:low].astype(F32) * scale
-        at = pl.multiple_of(SPLIT * 256 + part * high, high)
-        staged[pl.ds(at, high)] = piece[low:].astype(F32) * scale
+    parts = home.shape[0]
+    low, high = (SPLIT * 128 // parts, (15 - SPLIT) * 128 // parts)
+    mine = lax.axis_index("tm") % 2
+    for half, source in ((mine, home), (1 - mine, away)):
+        for part in range(parts):
+            at = pl.multiple_of((2 * part + half) * low, low)
+            staged[pl.ds(at, low)] = source[part, :low].astype(F32) * scale
+            at = pl.multiple_of(SPLIT * 256 + (2 * part + half) * high, high)
+            staged[pl.ds(at, high)] = source[part, low:].astype(F32) * scale
     results = [(mix, k) for k in range(3)] + [(temporal, k) for k in range(3)]
     results = results + [(spatial, k) for k in range(9)]
     copies = []
@@ -465,7 +465,7 @@
     *pieces, edges = together(*pieces, video)
     pieces = pairs(pieces, "tm")
     inner, outer = call(
-        functools.partial(edges_kernel, rows=rows),
+        functools.partial(edges_kernel, rows=rows, frames_first=True),
         [edge, edge],
         [pltpu.SemaphoreType.DMA((2,))],
         moved=512 * 1024,
@@ -480,7 +480,7 @@
         moved=4 * 1024 * 1024,
     )(valid_from, video, gain, spatial_weight)
 
-    tall, slope, active, parts, *strided = call(
+    tall, slope, active, parts, stay, leave = call(
         functools.partial(front_kernel, **sizes, shards=shards),
         [
             ((cells + 2 * frames * width, channels), BF16),
@@ -488,17 +488,15 @@
             ((2, cells // 2, channels), BF16),
             (((outs + 1) * rows * width, channels), BF16),
         ]
-        + [((outs + 1, here, width, channels), BF16)] * shards,
+        + [((1, shards // 2, outs + 1, here, width, channels), BF16)] * 2,
         [halo, *scalar, pltpu.VMEM((shards, outs + 1, here, width, channels), BF16)],
     )(valid_from, normed, partial, inner, outer, gain, spatial_weight, temporal_weight)
 
     half = channels // 2
-    pre_gradient, inner, outer, *low = call(
+    pre_gradient, *low = call(
         functools.partial(middle_kernel, **sizes, shards=shards),
         [
             ((rows, frames, width, channels), BF16),
-            edge,
-            edge,
             ((SPLIT * channels, half), F32),
             ((SPLIT * channels, half), BF16),
         ],
@@ -520,52 +518,65 @@
     def shapes(rows_in, *types):
         return [((rows_in, half), dtype) for dtype in types]
 
-    def halved(pieces):
-        size = pieces[0].shape[0] // 2
-        kept, send = call(halve_kernel, shapes(size, F32, BF16))(
-            *[piece.reshape(2, size, half) for piece in pieces]
-        )
-        return (kept, pair(send, "tm", 1))
-
-    def added(values):
-        (total,) = call(add_kernel, shapes(values[0].shape[0], BF16))(*values)
+    def added(left, right):
+        (total,) = call(add_kernel, shapes(left.shape[0], BF16))(left, right)
         return total
 
-    def doubled(total):
-        for step in range(1, shards.bit_length() - 1):
-            if step > 1:
-                total = added((total, other))
-            other = pair(total, "tm", 1 << step)
-        return (total, other)
-
-    def regained(values):
-        total = added(values)
-        return (total, pair(total, "tm", 1))
-
-    def whole(values, axis, step):
-        size = values[0].shape[0]
-        (total,) = call(
-            functools.partial(whole_kernel, axis=axis, step=step), [((2, size, half), BF16)]
-        )(*values)
-        return total.reshape(2 * size, half)
-
-    def gathered(values):
-        total = whole(values, "tm", 0)
-        return [total] + pairs([total] * (lines - 1), "height")
+    def joined(pieces):
+        (total,) = call(join_kernel, [((lines,) + pieces[0].shape, BF16)])(*pieces)
+        return total
+
+    def summed(pieces):
+        (total,) = call(gather_sum_kernel, shapes(pieces[0].shape[0], BF16))(*pieces)
+        return total
 
     (low, low_send), (high, high_send) = (low, high)
     low_got = pair(low_send, "cam", 1)
     high_got = pair(high_send, "cam", 1)
-    kept, *sends = call(deal_kernel, shapes(15 * channels // lines, F32, *[BF16] * (lines - 1)))(
-        *[a.reshape(lines, -1, half) for a in (low, low_got, high, high_got)]
+    size = 15 * channels // lines // 2
+    dealt = call(deal_kernel, shapes(size, *([F32] + [BF16] * (lines - 1)) * 2))(
+        *[a.reshape(lines, 2, -1, half) for a in (low, low_got, high, high_got)]
     )
-    received = pairs(sends, "height")
-    kept, *far = together(kept, *strided[2:])
-    strided = strided[:2] + far
-    strided = [strided[0]] + pairs(strided[1:], "tm")
-    kept, *strided = together(kept, *strided)
-    first = added(halved([kept] + received[::-1]))
-    first, strided[0] = together(first, strided[0])
+    (away, *away_sends), (home, *home_sends) = (dealt[:lines], dealt[lines:])
+    away_came = pairs(away_sends, "height")
+    home_came = pairs(home_sends, "height")
+    came = pair(leave, "tm", 1)
+    away, came = together(away, came)
+    crossed = pair(summed([away] + away_came[::-1]), "tm", 1)
+    total = summed([home] + home_came[::-1] + [crossed])
+    pre_gradient, total = together(pre_gradient, total)
+    inner, outer = call(
+        functools.partial(edges_kernel, rows=rows, frames_first=False),
+        [edge, edge],
+        [pltpu.SemaphoreType.DMA((2,))],
+        flops=240 * cells * channels * channels,
+        moved=512 * 1024,
+    )(pre_gradient)
+    inner, outer = neighbours(inner, outer, "height")
+    (halo_rows,) = call(halo_kernel, [((2, frames, width, channels), BF16)])(inner, outer)
+    for step in range(1, shards.bit_length() - 1):
+        if step > 1:
+            total = added(total, other)
+        other = pair(total, "tm", 1 << step)
+    total = added(total, other)
+    total, stay, came = together(total, stay, came)
+    other = pair(total, "tm", 1)
+    other, halo_rows = together(other, halo_rows)
+    for step in range(1, shards.bit_length() - 1):
+        count, pieces = (2 * stay.shape[0], stay.shape[1] // 2)
+        stay, leave = call(split_kernel, [((count, pieces) + stay.shape[2:], BF16)] * 2)(stay, came)
+        came = pair(leave, "tm", 1 << step)
+    home_pieces = [total] + pairs([total] * (lines - 1), "height")
+    away_pieces = [other] + pairs([other] * (lines - 1), "height")
+    (video_gradient,) = call(
+        functools.partial(input_kernel, **sizes),
+        [((frames, rows, width, channels), BF16)],
+        [pltpu.VMEM((cells, 3 * channels), BF16)] + scalar,
+        flops=18 * cells * channels * channels,
+        moved=4 * 1024 * 1024,
+    )(valid_from, video, pre_gradient, halo_rows, gain, spatial_weight)
+    home = joined(home_pieces)
+    home, came = together(home, came)
     (encoded,) = call(
         functools.partial(encode_kernel, width=width, shards=shards),
         [((shards * outs, here, width, channels), BF16)],
@@ -575,41 +586,32 @@
         ],
         flops=3 * cells * channels * channels,
         moved=2 * 1024 * 1024,
-    )(mix_weight, *strided)
-    encoded, inner, outer = together(encoded, inner, outer)
-    inner, outer = neighbours(inner, outer, "height")
-    (halo_rows,) = call(halo_kernel, [((2, frames, width, channels), BF16)])(inner, outer)
-    values = regained(doubled(first))
-    values, halo_rows = together(values, halo_rows)
-    pieces = gathered(values)
-    (video_gradient,) = call(
-        functools.partial(input_kernel, **sizes),
-        [((frames, rows, width, channels), BF16)],
-        [pltpu.VMEM((cells, 3 * channels), BF16)] + scalar,
-        flops=18 * cells * channels * channels,
-        moved=4 * 1024 * 1024,
-    )(valid_from, video, pre_gradient, halo_rows, gain, spatial_weight)
-    pieces[-1], video_gradient = together(pieces[-1], video_gradient)
-    others = [pair(piece, "cam", 1) for piece in pieces]
+    )(mix_weight, stay, came)
+    away_pieces[-1], home, video_gradient, encoded = together(
+        away_pieces[-1], home, video_gradient, encoded
+    )
+    away = joined(away_pieces)
+    own = (home, away)
+    others = (pair(home, "cam", 1), pair(away, "cam", 1))
 
     cell_count = cells * lax.axis_size("cam") * shards * lines
     scale = 1.0 / math.sqrt(cell_count)
     results = [((9, channels, channels), F32)] + [((3, channels, channels), F32)] * 2
     staged = pltpu.VMEM((15 * channels, half), F32)
     *results_own, total = call(
-        functools.partial(finish_kernel, scale=scale, parts=lines, last=False),
+        functools.partial(finish_kernel, scale=scale, last=False),
         results + [((channels, half), F32)],
         [staged, pltpu.SemaphoreType.DMA((15,))],
         moved=4 * 1024 * 1024,
         far=3,
-    )(*pieces, spatial_weight)
+    )(*own, spatial_weight)
     spatial, temporal, mix, gain_gradient = call(
-        functools.partial(finish_kernel, scale=scale, parts=lines, last=True),
+        functools.partial(finish_kernel, scale=scale, last=True),
         results + [((1, channels), F32)],
         [staged, pltpu.VMEM((1, channels), F32), pltpu.SemaphoreType.DMA((16,))],
         moved=4 * 1024 * 1024,
         far=4,
-        aliases={lines + 3 + at: at for at in range(3)},
+        aliases={5 + at: at for at in range(3)},
     )(*others, spatial_weight, total, gain, *results_own)
 
     return (

time: 74.2 us -> 71.9 us (0.969)
  waiting for transfers between devices: 28.3 us -> 20.5 us
  starting transfers between devices: 25 us -> 29.8 us
    ppermute x23 -> x26, waiting for transfers between devices: 28.3 us -> 20.5 us  [pair(): lax.ppermute(array, axis, [(i, i ^ step) for i in range(lax.axis_size(axi...]
    ppermute x23 -> x26, starting transfers between devices: 23.7 us -> 28.5 us  [pair(): lax.ppermute(array, axis, [(i, i ^ step) for i in range(lax.axis_size(axi...]
    pallas_call x16 -> x19, Pallas kernels: 15.1 us -> 15.8 us  [run(): pl.pallas_call(kernel, out_shape=[jax.ShapeDtypeStruct(shape, dtype) for...]
  transfers between devices with their start and end apart: 25 -> 28, of which waited for: 12 -> 13; matrix products, arithmetic and copies ran while one was open for 0% -> 0% of each run, Pallas kernels for 14% -> 15%
where the time goes in v1:
time: 71.9 us; the launch traced here: 71.6 us
  starting transfers between devices  29.8 us (41%)
  waiting for transfers between devices  20.5 us (29%)
  Pallas kernels  15.8 us (22%)
  local copies, waits for them, and re-layouts  3.96 us (6%)
  between operations  1.58 us (2%)
    ppermute x26, starting transfers between devices, pair(): lax.ppermute(array, axis, [(i, i ^ step) for i in range(lax.axis_size(axi...  28.5 us
    ppermute x26, waiting for transfers between devices, pair(): lax.ppermute(array, axis, [(i, i ^ step) for i in range(lax.axis_size(axi...  20.5 us
    pallas_call x19, Pallas kernels, run(): pl.pallas_call(kernel, out_shape=[jax.ShapeDtypeStruct(shape, dtype) for...  15.8 us
    unnamed x20, local copies, waits for them, and re-layouts  3.96 us
  transfers between devices with their start and end apart: 28, of which 13 were waited for; matrix products, arithmetic and copies ran while one was open for 0% of the time, Pallas kernels for 15%

profile of v1, /device:TPU:0, one launch (start us, length us, event | category | flops | bytes accessed | tf_op | source)
XLA Modules:
  0.0 71.6 jit_solution(226907030991127544)
XLA Ops:
  0.6 0.9 %copy-done.6 = bf16[1,8,1,64,256]{4,3,2,1,0:T(8,128)(2,1)S(1)} copy-done((bf16[1,8,1,64,256]{4,3,2,1,0:T(8,128)(2,1)S(1)}, bf16[1,8,1,64,256]{4,3,2,1,0:T(8,128)(2,1)}, u32[]{:S(2)}) %copy-start.6) | copy-done | bytes 262168
  2.2 5.1 %collective-permute-start.2 = (bf16[5,1,64,256]{3,2,1,0:T(8,128)(2,1)S(1)}, bf16[5,1,64,256]{3,2,1,0:T(8,128)(2,1)S(1)}, u32[]{:S(2)}, u32[]{:S(2)}) collective-permute-start(bf16[5,1,64,256]{3,2,1,0:T(8,128)(2,1)S(1)} %get-tuple-element.75), channel_id=1, source_target_pairs={{0,24},{8,16},{16,8},{24,0},{1,25},{9,17},{17,9},{25,1},{2,26},{10... | collective-permute-start | bytes 491528 | tf_op jit(solution)/shard_map/ppermute | solution.py:432
  8.0 1.0 %copy-done.2 = bf16[1,4,4,64,256]{4,3,2,1,0:T(8,128)(2,1)S(1)} copy-done((bf16[1,4,4,64,256]{4,3,2,1,0:T(8,128)(2,1)S(1)}, bf16[1,4,4,64,256]{4,3,2,1,0:T(8,128)(2,1)}, u32[]{:S(2)}) %copy-start.2) | copy-done | bytes 524312
  9.1 1.7 %collective-permute-start = (bf16[4,64,256]{2,1,0:T(8,128)(2,1)S(1)}, bf16[4,64,256]{2,1,0:T(8,128)(2,1)S(1)}, u32[]{:S(2)}, u32[]{:S(2)}) collective-permute-start(bf16[4,64,256]{2,1,0:T(8,128)(2,1)S(1)} %get-tuple-element.69), channel_id=1, source_target_pairs={{0,2},{2,0},{4,6},{6,4},{1,3},{3,1},{5,7},{7,5},{8,10},{10,8},{12,... | collective-permute-start | bytes 393224 | tf_op jit(solution)/shard_map/ppermute | solution.py:432
  12.2 1.3 %copy-done = bf16[3,3,256,256]{3,2,1,0:T(8,128)(2,1)S(1)} copy-done((bf16[3,3,256,256]{3,2,1,0:T(8,128)(2,1)S(1)}, bf16[3,3,256,256]{3,2,1,0:T(8,128)(2,1)}, u32[]{:S(2)}) %copy-start) | copy-done | bytes 1179672
  13.4 0.7 copy-done.8
  14.1 1.9 %shard_map.118 = (bf16[1024,256]{1,0:T(8,128)(2,1)S(1)}, f32[1024,256]{1,0:T(8,128)S(1)}) custom-call(s32[1]{0:T(128)S(6)} %copy.20.valid_from, bf16[4,4,64,256]{3,2,1,0:T(8,128)(2,1)S(1)} %bitcast.16, f32[1,256]{1,0:T(1,128)S(1)} %bitcast.22, bf16[3,3,256,256]{3,2,1,0:T(8,128)(2,1)S(1)} %copy-done), custom_call_target="tpu_custom_call" | custom-call | flops 1207959552 | bytes 4194304 | tf_op jit(solution)/shard_map/pallas_call | solution.py:404
  16.0 1.7 %shard_map.121 = (bf16[1536,256]{1,0:T(8,128)(2,1)S(1)}, f32[1024,256]{1,0:T(8,128)S(1)}, bf16[2,512,256]{2,1,0:T(8,128)(2,1)S(1)}, bf16[768,256]{1,0:T(8,128)(2...) custom-call(s32[1]{0:T(128)S(6)} %copy.20.valid_from, ...), custom_call_target="tpu_custom_call" | custom-call | tf_op jit(solution)/shard_map/pallas_call | solution.py:404
  17.7 3.5 %collective-permute-done.3.refs_1_ = bf16[5,1,64,256]{3,2,1,0:T(8,128)(2,1)S(1)} collective-permute-done((bf16[5,1,64,256]{3,2,1,0:T(8,128)(2,1)S(1)}, bf16[5,1,64,256]{3,2,1,0:T(8,128)(2,1)S(1)}, u32[]{:S(2)}, u32[]{:S(2)}) %collective-permute-start.3) | collective-permute-done | bytes 163872 | tf_op jit(solution)/shard_map/ppermute | solution.py:432
  21.2 2.0 %shard_map.122 = (bf16[4,4,64,256]{3,2,1,0:T(8,128)(2,1)S(1)}, f32[2048,128]{1,0:T(8,128)S(1)}, bf16[2048,128]{1,0:T(8,128)(2,1)S(1)}) custom-call(bf16[1536,256]{1,0:T(8,128)(2,1)S(1)} %get-tuple-element.71.tall, f32[1024,256]{1,0:T(8,128)S(1)} %get-tuple-element.72.slope, bf16[2,512,256]{2,1,0:T(8,128)(2,1)S(1)} %get-tuple-element.73.active, ...), custom_call_target="tpu_custom_call" | custom-call | flops 1342177280 | bytes 6291456 | tf_op jit(solution)/shard_map/pallas_call | solution.py:404
  23.4 1.2 %shard_map.123 = (f32[1792,128]{1,0:T(8,128)S(1)}, bf16[1792,128]{1,0:T(8,128)(2,1)S(1)}) custom-call(bf16[1536,256]{1,0:T(8,128)(2,1)S(1)} %get-tuple-element.71.tall, bf16[4,4,64,256]{3,2,1,0:T(8,128)(2,1)S(1)} %get-tuple-element.97.pre_gradient.source), custom_call_target="tpu_custom_call" | custom-call | flops 1073741824 | bytes 6291456 | tf_op jit(solution)/shard_map/pallas_call | solution.py:404
  25.1 1.4 %collective-permute-done.6 = bf16[1792,128]{1,0:T(8,128)(2,1)S(1)} collective-permute-done((bf16[1792,128]{1,0:T(8,128)(2,1)S(1)}, bf16[1792,128]{1,0:T(8,128)(2,1)S(1)}, u32[]{:S(2)}, u32[]{:S(2)}) %collective-permute-start.6) | collective-permute-done | bytes 458784 | tf_op jit(solution)/shard_map/ppermute | solution.py:432
  26.8 2.5 %collective-permute-start.11 = (bf16[480,128]{1,0:T(8,128)(2,1)S(1)}, bf16[480,128]{1,0:T(8,128)(2,1)S(1)}, u32[]{:S(2)}, u32[]{:S(2)}) collective-permute-start(bf16[480,128]{1,0:T(8,128)(2,1)S(1)} %get-tuple-element.90), channel_id=1, source_target_pairs={{0,6},{2,4},{4,2},{6,0},{1,7},{3,5},{5,3},{7,1},{8,14},{10,12},{12... | collective-permute-start | bytes 368648 | tf_op jit(solution)/shard_map/ppermute | solution.py:432
  30.3 1.7 %collective-permute-done.10.came_in = bf16[1,2,3,1,64,256]{5,4,3,2,1,0:T(8,128)(2,1)S(1)} collective-permute-done((bf16[1,2,3,1,64,256]{5,4,3,2,1,0:T(8,128)(2,1)S(1)}, bf16[1,2,3,1,64,256]{5,4,3,2,1,0:T(8,128)(2,1)S(1)}, u32[]{:S(2)}, u32[]{:S(2)}) %collective-permute-start.10) | collective-permute-done | bytes 196640 | tf_op jit(solution)/shard_map/ppermute | solution.py:432
  32.0 2.5 %collective-permute-start.7 = (bf16[480,128]{1,0:T(8,128)(2,1)S(1)}, bf16[480,128]{1,0:T(8,128)(2,1)S(1)}, u32[]{:S(2)}, u32[]{:S(2)}) collective-permute-start(bf16[480,128]{1,0:T(8,128)(2,1)S(1)} %get-tuple-element.84), channel_id=1, source_target_pairs={{0,6},{2,4},{4,2},{6,0},{1,7},{3,5},{5,3},{7,1},{8,14},{10,12},{12... | collective-permute-start | bytes 368648 | tf_op jit(solution)/shard_map/ppermute | solution.py:432
  35.5 1.6 %collective-permute-done.12.refs_1_ = bf16[480,128]{1,0:T(8,128)(2,1)S(1)} collective-permute-done((bf16[480,128]{1,0:T(8,128)(2,1)S(1)}, bf16[480,128]{1,0:T(8,128)(2,1)S(1)}, u32[]{:S(2)}, u32[]{:S(2)}) %collective-permute-start.12) | collective-permute-done | bytes 122912 | tf_op jit(solution)/shard_map/ppermute | solution.py:432
  37.3 2.3 %collective-permute-done.7.refs_0_ = bf16[480,128]{1,0:T(8,128)(2,1)S(1)} collective-permute-done((bf16[480,128]{1,0:T(8,128)(2,1)S(1)}, bf16[480,128]{1,0:T(8,128)(2,1)S(1)}, u32[]{:S(2)}, u32[]{:S(2)}) %collective-permute-start.7) | collective-permute-done | bytes 122912 | tf_op jit(solution)/shard_map/ppermute | solution.py:432
  39.6 1.6 %collective-permute-done.8.refs_1_ = bf16[480,128]{1,0:T(8,128)(2,1)S(1)} collective-permute-done((bf16[480,128]{1,0:T(8,128)(2,1)S(1)}, bf16[480,128]{1,0:T(8,128)(2,1)S(1)}, u32[]{:S(2)}, u32[]{:S(2)}) %collective-permute-start.8) | collective-permute-done | bytes 122912 | tf_op jit(solution)/shard_map/ppermute | solution.py:432
  41.4 0.9 %collective-permute-done.14.refs_3_ = bf16[480,128]{1,0:T(8,128)(2,1)S(1)} collective-permute-done((bf16[480,128]{1,0:T(8,128)(2,1)S(1)}, bf16[480,128]{1,0:T(8,128)(2,1)S(1)}, u32[]{:S(2)}, u32[]{:S(2)}) %collective-permute-start.14) | collective-permute-done | bytes 122912 | tf_op jit(solution)/shard_map/ppermute | solution.py:432
  42.8 1.1 %collective-permute-start.17 = (bf16[4,64,256]{2,1,0:T(8,128)(2,1)S(1)}, bf16[4,64,256]{2,1,0:T(8,128)(2,1)S(1)}, u32[]{:S(2)}, u32[]{:S(2)}) collective-permute-start(bf16[4,64,256]{2,1,0:T(8,128)(2,1)S(1)} %get-tuple-element.98), channel_id=1, source_target_pairs={{0,2},{2,0},{4,6},{6,4},{1,3},{3,1},{5,7},{7,5},{8,10},{10,8},{12,... | collective-permute-start | bytes 393224 | tf_op jit(solution)/shard_map/ppermute | solution.py:432
  43.8 1.7 %collective-permute-start.15 = (bf16[480,128]{1,0:T(8,128)(2,1)S(1)}, bf16[480,128]{1,0:T(8,128)(2,1)S(1)}, u32[]{:S(2)}, u32[]{:S(2)}) collective-permute-start(bf16[480,128]{1,0:T(8,128)(2,1)S(1)} %shard_map.126.left), channel_id=1, source_target_pairs={{0,16},{8,24},{16,0},{24,8},{1,17},{9,25},{17,1},{25,9},{2,18},{10... | collective-permute-start | bytes 368648 | tf_op jit(solution)/shard_map/ppermute | solution.py:432
  46.2 5.5 %collective-permute-done.15.right = bf16[480,128]{1,0:T(8,128)(2,1)S(1)} collective-permute-done((bf16[480,128]{1,0:T(8,128)(2,1)S(1)}, bf16[480,128]{1,0:T(8,128)(2,1)S(1)}, u32[]{:S(2)}, u32[]{:S(2)}) %collective-permute-start.15) | collective-permute-done | bytes 122912 | tf_op jit(solution)/shard_map/ppermute | solution.py:432
  51.8 1.6 %collective-permute-start.22 = (bf16[480,128]{1,0:T(8,128)(2,1)S(1)}, bf16[480,128]{1,0:T(8,128)(2,1)S(1)}, u32[]{:S(2)}, u32[]{:S(2)}) collective-permute-start(bf16[480,128]{1,0:T(8,128)(2,1)S(1)} %shard_map.127.refs_0_), channel_id=1, source_target_pairs={{0,6},{2,4},{4,2},{6,0},{1,7},{3,5},{5,3},{7,1},{8,14},{10,12},{12... | collective-permute-start | bytes 368648 | tf_op jit(solution)/shard_map/ppermute | solution.py:432
  54.0 1.4 %collective-permute-start.20 = (bf16[480,128]{1,0:T(8,128)(2,1)S(1)}, bf16[480,128]{1,0:T(8,128)(2,1)S(1)}, u32[]{:S(2)}, u32[]{:S(2)}) collective-permute-start(bf16[480,128]{1,0:T(8,128)(2,1)S(1)} %shard_map.127.refs_0_), channel_id=1, source_target_pairs={{0,2},{2,0},{4,6},{6,4},{1,3},{3,1},{5,7},{7,5},{8,10},{10,8},{12,... | collective-permute-start | bytes 368648 | tf_op jit(solution)/shard_map/ppermute | solution.py:432
  55.4 3.0 %collective-permute-start.23 = (bf16[2,1,3,1,64,256]{5,4,3,2,1,0:T(8,128)(2,1)S(1)}, bf16[2,1,3,1,64,256]{5,4,3,2,1,0:T(8,128)(2,1)S(1)}, u32[]{:S(2)}, u32[]{:S(2)}) collective-permute-start(bf16[2,1,3,1,64,256]{5,4,3,2,1,0:T(8,128)(2,1)S(1)} %get-tuple-element.103), channel_id=1, source_target_pairs={{0,16},{8,24},{16,0},{24,8},{1,17},{9,25},{17,1},{25,9},{2,18},{10... | collective-permute-start | bytes 589832 | tf_op jit(solution)/shard_map/ppermute | solution.py:432
  59.0 1.4 %collective-permute-start.25 = (bf16[480,128]{1,0:T(8,128)(2,1)S(1)}, bf16[480,128]{1,0:T(8,128)(2,1)S(1)}, u32[]{:S(2)}, u32[]{:S(2)}) collective-permute-start(bf16[480,128]{1,0:T(8,128)(2,1)S(1)} %collective-permute-done.16.refs_0_), channel_id=1, source_target_pairs={{0,2},{2,0},{4,6},{6,4},{1,3},{3,1},{5,7},{7,5},{8,10},{10,8},{12,... | collective-permute-start | bytes 368648 | tf_op jit(solution)/shard_map/ppermute | solution.py:432
  60.6 1.5 %collective-permute-start.19 = (bf16[480,128]{1,0:T(8,128)(2,1)S(1)}, bf16[480,128]{1,0:T(8,128)(2,1)S(1)}, u32[]{:S(2)}, u32[]{:S(2)}) collective-permute-start(bf16[480,128]{1,0:T(8,128)(2,1)S(1)} %collective-permute-done.16.refs_0_), channel_id=1, source_target_pairs={{0,6},{2,4},{4,2},{6,0},{1,7},{3,5},{5,3},{7,1},{8,14},{10,12},{12... | collective-permute-start | bytes 368648 | tf_op jit(solution)/shard_map/ppermute | solution.py:432
  62.2 3.0 %shard_map.132 = bf16[4,4,64,256]{3,2,1,0:T(8,128)(2,1)} custom-call(s32[1]{0:T(128)S(6)} %copy.20.valid_from, bf16[4,4,64,256]{3,2,1,0:T(8,128)(2,1)S(1)} %bitcast.17, bf16[4,4,64,256]{3,2,1,0:T(8,128)(2,1)S(1)} %get-tuple-element.97.pre_gradient.source, bf16[2,4,64,256]{3,2,1,0:T(8,128)(2,1)S(1)} %shard_map.129.halo, f32[1,256]{1,0:T(1,128)S(1)} %bitcast.24, ...), custom_call_target="tpu_custom_call" | custom-call | flops 1207959552 | bytes 4194304 | tf_op jit(solution)/shard_map/pallas_call | solution.py:404
  65.2 0.9 %collective-permute-done.23.came = bf16[2,1,3,1,64,256]{5,4,3,2,1,0:T(8,128)(2,1)S(1)} collective-permute-done((bf16[2,1,3,1,64,256]{5,4,3,2,1,0:T(8,128)(2,1)S(1)}, bf16[2,1,3,1,64,256]{5,4,3,2,1,0:T(8,128)(2,1)S(1)}, u32[]{:S(2)}, u32[]{:S(2)}) %collective-permute-start.23) | collective-permute-done | bytes 196640 | tf_op jit(solution)/shard_map/ppermute | solution.py:432
  66.1 1.1 %shard_map.133 = bf16[8,1,64,256]{3,2,1,0:T(8,128)(2,1)} custom-call(bf16[3,256,256]{2,1,0:T(8,128)(2,1)S(1)} %copy-done.4, bf16[2,1,3,1,64,256]{5,4,3,2,1,0:T(8,128)(2,1)S(1)} %get-tuple-element.106.stay, bf16[2,1,3,1,64,256]{5,4,3,2,1,0:T(8,128)(2,1)S(1)} %collective-permute-done.23.came), custom_call_target="tpu_custom_call" | custom-call | flops 201326592 | bytes 2097152 | tf_op jit(solution)/shard_map/pallas_call | solution.py:404
  67.8 1.5 %shard_map.135 = (f32[9,256,256]{2,1,0:T(8,128)}, f32[3,256,256]{2,1,0:T(8,128)}, f32[3,256,256]{2,1,0:T(8,128)}, f32[256,128]{1,0:T(8,128)S(1)}) custom-call(bf16[4,480,128]{2,1,0:T(8,128)(2,1)S(1)} %shard_map.130.home, bf16[4,480,128]{2,1,0:T(8,128)(2,1)S(1)} %shard_map.134.away, bf16[3,3,256,256]{3,2,1,0:T(8,128)(2,1)S(1)} %copy-done.1), custom_call_target="tpu_custom_call" | custom-call | bytes 4194304 | tf_op jit(solution)/shard_map/pallas_call | solution.py:404
  69.9 1.7 %shard_map.136 = (f32[9,256,256]{2,1,0:T(8,128)}, f32[3,256,256]{2,1,0:T(8,128)}, f32[3,256,256]{2,1,0:T(8,128)}, f32[1,256]{1,0:T(1,128)}) custom-call(bf16[4,480,128]{2,1,0:T(8,128)(2,1)S(1)} %collective-permute-done.24.home, bf16[4,480,128]{2,1,0:T(8,128)(2,1)S(1)} %collective-permute-done.27.away, ...), custom_call_target="tpu_custom_call", output_to_operand_aliasing={{0}: (5, {}), {1}: (6, {}), {2}: (7, {})} | custom-call | bytes 4194304 | tf_op jit(solution)/shard_map/pallas_call | solution.py:404
  (63 shorter events, 9.2 us)
Async XLA Ops:
  2.2 15.5 %collective-permute-start.2 = (bf16[5,1,64,256]{3,2,1,0:T(8,128)(2,1)S(1)}, bf16[5,1,64,256]{3,2,1,0:T(8,128)(2,1)S(1)}, u32[]{:S(2)}, u32[]{:S(2)}) collective-permute-start(bf16[5,1,64,256]{3,2,1,0:T(8,128)(2,1)S(1)} %get-tuple-element.75), channel_id=1, source_target_pairs={{0,24},{8,16},{16,8},{24,0},{1,25},{9,17},{17,9},{25,1},{2,26},{10... | collective-permute-start | bytes 491528 | tf_op jit(solution)/shard_map/ppermute | solution.py:432
  7.3 13.9 %collective-permute-start.3 = (bf16[5,1,64,256]{3,2,1,0:T(8,128)(2,1)S(1)}, bf16[5,1,64,256]{3,2,1,0:T(8,128)(2,1)S(1)}, u32[]{:S(2)}, u32[]{:S(2)}) collective-permute-start(bf16[5,1,64,256]{3,2,1,0:T(8,128)(2,1)S(1)} %get-tuple-element.76), channel_id=1, source_target_pairs={{0,16},{8,24},{16,0},{24,8},{1,17},{9,25},{17,1},{25,9},{2,18},{10... | collective-permute-start | bytes 491528 | tf_op jit(solution)/shard_map/ppermute | solution.py:432
  7.3 13.9 %collective-permute-start.4 = (bf16[5,1,64,256]{3,2,1,0:T(8,128)(2,1)S(1)}, bf16[5,1,64,256]{3,2,1,0:T(8,128)(2,1)S(1)}, u32[]{:S(2)}, u32[]{:S(2)}) collective-permute-start(bf16[5,1,64,256]{3,2,1,0:T(8,128)(2,1)S(1)} %get-tuple-element.77), channel_id=1, source_target_pairs={{0,8},{8,0},{16,24},{24,16},{1,9},{9,1},{17,25},{25,17},{2,10},{10... | collective-permute-start | bytes 491528 | tf_op jit(solution)/shard_map/ppermute | solution.py:432
  9.0 7.0 %copy-start.5 = (bf16[3,256,256]{2,1,0:T(8,128)(2,1)S(1)}, bf16[3,256,256]{2,1,0:T(8,128)(2,1)}, u32[]{:S(2)}) copy-start(bf16[3,256,256]{2,1,0:T(8,128)(2,1)} %temporal.3) | copy-start | bytes 1179652
  9.1 6.9 %collective-permute-start = (bf16[4,64,256]{2,1,0:T(8,128)(2,1)S(1)}, bf16[4,64,256]{2,1,0:T(8,128)(2,1)S(1)}, u32[]{:S(2)}, u32[]{:S(2)}) collective-permute-start(bf16[4,64,256]{2,1,0:T(8,128)(2,1)S(1)} %get-tuple-element.69), channel_id=1, source_target_pairs={{0,2},{2,0},{4,6},{6,4},{1,3},{3,1},{5,7},{7,5},{8,10},{10,8},{12,... | collective-permute-start | bytes 393224 | tf_op jit(solution)/shard_map/ppermute | solution.py:432
  10.8 5.2 %collective-permute-start.1 = (bf16[4,64,256]{2,1,0:T(8,128)(2,1)S(1)}, bf16[4,64,256]{2,1,0:T(8,128)(2,1)S(1)}, u32[]{:S(2)}, u32[]{:S(2)}) collective-permute-start(bf16[4,64,256]{2,1,0:T(8,128)(2,1)S(1)} %get-tuple-element.70), channel_id=1, source_target_pairs={{2,4},{4,2},{3,5},{5,3},{10,12},{12,10},{11,13},{13,11},{18,20},{2... | collective-permute-start | bytes 393224 | tf_op jit(solution)/shard_map/ppermute | solution.py:428
  16.0 5.2 %copy-start.4 = (bf16[3,256,256]{2,1,0:T(8,128)(2,1)S(1)}, bf16[3,256,256]{2,1,0:T(8,128)(2,1)}, u32[]{:S(2)}) copy-start(bf16[3,256,256]{2,1,0:T(8,128)(2,1)} %mix.3) | copy-start | bytes 1179652
  23.3 3.3 %collective-permute-start.5 = (bf16[2048,128]{1,0:T(8,128)(2,1)S(1)}, bf16[2048,128]{1,0:T(8,128)(2,1)S(1)}, u32[]{:S(2)}, u32[]{:S(2)}) collective-permute-start(bf16[2048,128]{1,0:T(8,128)(2,1)S(1)} %get-tuple-element.80), channel_id=1, source_target_pairs={{0,1},{1,0},{2,3},{3,2},{4,5},{5,4},{6,7},{7,6},{8,9},{9,8},{10,11... | collective-permute-start | bytes 1572872 | tf_op jit(solution)/shard_map/ppermute | solution.py:432
  24.6 2.0 %collective-permute-start.6 = (bf16[1792,128]{1,0:T(8,128)(2,1)S(1)}, bf16[1792,128]{1,0:T(8,128)(2,1)S(1)}, u32[]{:S(2)}, u32[]{:S(2)}) collective-permute-start(bf16[1792,128]{1,0:T(8,128)(2,1)S(1)} %get-tuple-element.82), channel_id=1, source_target_pairs={{0,1},{1,0},{2,3},{3,2},{4,5},{5,4},{6,7},{7,6},{8,9},{9,8},{10,11... | collective-permute-start | bytes 1376264 | tf_op jit(solution)/shard_map/ppermute | solution.py:432
  25.1 6.9 %collective-permute-start.10 = (bf16[1,2,3,1,64,256]{5,4,3,2,1,0:T(8,128)(2,1)S(1)}, bf16[1,2,3,1,64,256]{5,4,3,2,1,0:T(8,128)(2,1)S(1)}, u32[]{:S(2)}, u32[]{:S(2)}) collective-permute-start(bf16[1,2,3,1,64,256]{5,4,3,2,1,0:T(8,128)(2,1)S(1)} %get-tuple-element.88), channel_id=1, source_target_pairs={{0,8},{8,0},{16,24},{24,16},{1,9},{9,1},{17,25},{25,17},{2,10},{10... | collective-permute-start | bytes 589832 | tf_op jit(solution)/shard_map/ppermute | solution.py:432
  26.8 8.2 %collective-permute-start.11 = (bf16[480,128]{1,0:T(8,128)(2,1)S(1)}, bf16[480,128]{1,0:T(8,128)(2,1)S(1)}, u32[]{:S(2)}, u32[]{:S(2)}) collective-permute-start(bf16[480,128]{1,0:T(8,128)(2,1)S(1)} %get-tuple-element.90), channel_id=1, source_target_pairs={{0,6},{2,4},{4,2},{6,0},{1,7},{3,5},{5,3},{7,1},{8,14},{10,12},{12... | collective-permute-start | bytes 368648 | tf_op jit(solution)/shard_map/ppermute | solution.py:432
  29.3 7.8 %collective-permute-start.12 = (bf16[480,128]{1,0:T(8,128)(2,1)S(1)}, bf16[480,128]{1,0:T(8,128)(2,1)S(1)}, u32[]{:S(2)}, u32[]{:S(2)}) collective-permute-start(bf16[480,128]{1,0:T(8,128)(2,1)S(1)} %get-tuple-element.91), channel_id=1, source_target_pairs={{0,4},{2,6},{4,0},{6,2},{1,5},{3,7},{5,1},{7,3},{8,12},{10,14},{12... | collective-permute-start | bytes 368648 | tf_op jit(solution)/shard_map/ppermute | solution.py:432
  29.8 7.3 %collective-permute-start.13 = (bf16[480,128]{1,0:T(8,128)(2,1)S(1)}, bf16[480,128]{1,0:T(8,128)(2,1)S(1)}, u32[]{:S(2)}, u32[]{:S(2)}) collective-permute-start(bf16[480,128]{1,0:T(8,128)(2,1)S(1)} %get-tuple-element.92), channel_id=1, source_target_pairs={{0,2},{2,0},{4,6},{6,4},{1,3},{3,1},{5,7},{7,5},{8,10},{10,8},{12,... | collective-permute-start | bytes 368648 | tf_op jit(solution)/shard_map/ppermute | solution.py:432
  32.0 7.6 %collective-permute-start.7 = (bf16[480,128]{1,0:T(8,128)(2,1)S(1)}, bf16[480,128]{1,0:T(8,128)(2,1)S(1)}, u32[]{:S(2)}, u32[]{:S(2)}) collective-permute-start(bf16[480,128]{1,0:T(8,128)(2,1)S(1)} %get-tuple-element.84), channel_id=1, source_target_pairs={{0,6},{2,4},{4,2},{6,0},{1,7},{3,5},{5,3},{7,1},{8,14},{10,12},{12... | collective-permute-start | bytes 368648 | tf_op jit(solution)/shard_map/ppermute | solution.py:432
  34.5 6.8 %collective-permute-start.8 = (bf16[480,128]{1,0:T(8,128)(2,1)S(1)}, bf16[480,128]{1,0:T(8,128)(2,1)S(1)}, u32[]{:S(2)}, u32[]{:S(2)}) collective-permute-start(bf16[480,128]{1,0:T(8,128)(2,1)S(1)} %get-tuple-element.85), channel_id=1, source_target_pairs={{0,4},{2,6},{4,0},{6,2},{1,5},{3,7},{5,1},{7,3},{8,12},{10,14},{12... | collective-permute-start | bytes 368648 | tf_op jit(solution)/shard_map/ppermute | solution.py:432
  35.0 6.4 %collective-permute-start.9 = (bf16[480,128]{1,0:T(8,128)(2,1)S(1)}, bf16[480,128]{1,0:T(8,128)(2,1)S(1)}, u32[]{:S(2)}, u32[]{:S(2)}) collective-permute-start(bf16[480,128]{1,0:T(8,128)(2,1)S(1)} %get-tuple-element.86), channel_id=1, source_target_pairs={{0,2},{2,0},{4,6},{6,4},{1,3},{3,1},{5,7},{7,5},{8,10},{10,8},{12,... | collective-permute-start | bytes 368648 | tf_op jit(solution)/shard_map/ppermute | solution.py:432
  37.2 5.1 %collective-permute-start.14 = (bf16[480,128]{1,0:T(8,128)(2,1)S(1)}, bf16[480,128]{1,0:T(8,128)(2,1)S(1)}, u32[]{:S(2)}, u32[]{:S(2)}) collective-permute-start(bf16[480,128]{1,0:T(8,128)(2,1)S(1)} %shard_map.125), channel_id=1, source_target_pairs={{0,8},{8,0},{16,24},{24,16},{1,9},{9,1},{17,25},{25,17},{2,10},{10... | collective-permute-start | bytes 368648 | tf_op jit(solution)/shard_map/ppermute | solution.py:432
  42.4 19.8 %copy-start.3 = (bf16[1,4,4,64,256]{4,3,2,1,0:T(8,128)(2,1)S(1)}, bf16[1,4,4,64,256]{4,3,2,1,0:T(8,128)(2,1)}, u32[]{:S(2)}) copy-start(bf16[1,4,4,64,256]{4,3,2,1,0:T(8,128)(2,1)} %param.7) | copy-start | bytes 1572868
  42.4 19.8 %copy-start.9 = (f32[256]{0:T(256)S(1)}, f32[256]{0:T(256)}, u32[]{:S(2)}) copy-start(f32[256]{0:T(256)} %param.9) | copy-start | bytes 3076
  42.8 11.2 %collective-permute-start.17 = (bf16[4,64,256]{2,1,0:T(8,128)(2,1)S(1)}, bf16[4,64,256]{2,1,0:T(8,128)(2,1)S(1)}, u32[]{:S(2)}, u32[]{:S(2)}) collective-permute-start(bf16[4,64,256]{2,1,0:T(8,128)(2,1)S(1)} %get-tuple-element.98), channel_id=1, source_target_pairs={{0,2},{2,0},{4,6},{6,4},{1,3},{3,1},{5,7},{7,5},{8,10},{10,8},{12,... | collective-permute-start | bytes 393224 | tf_op jit(solution)/shard_map/ppermute | solution.py:432
  43.8 7.8 %collective-permute-start.15 = (bf16[480,128]{1,0:T(8,128)(2,1)S(1)}, bf16[480,128]{1,0:T(8,128)(2,1)S(1)}, u32[]{:S(2)}, u32[]{:S(2)}) collective-permute-start(bf16[480,128]{1,0:T(8,128)(2,1)S(1)} %shard_map.126.left), channel_id=1, source_target_pairs={{0,16},{8,24},{16,0},{24,8},{1,17},{9,25},{17,1},{25,9},{2,18},{10... | collective-permute-start | bytes 368648 | tf_op jit(solution)/shard_map/ppermute | solution.py:432
  45.6 9.8 %collective-permute-start.18 = (bf16[4,64,256]{2,1,0:T(8,128)(2,1)S(1)}, bf16[4,64,256]{2,1,0:T(8,128)(2,1)S(1)}, u32[]{:S(2)}, u32[]{:S(2)}) collective-permute-start(bf16[4,64,256]{2,1,0:T(8,128)(2,1)S(1)} %get-tuple-element.99), channel_id=1, source_target_pairs={{2,4},{4,2},{3,5},{5,3},{10,12},{12,10},{11,13},{13,11},{18,20},{2... | collective-permute-start | bytes 393224 | tf_op jit(solution)/shard_map/ppermute | solution.py:428
  51.7 6.7 %collective-permute-start.16 = (bf16[480,128]{1,0:T(8,128)(2,1)S(1)}, bf16[480,128]{1,0:T(8,128)(2,1)S(1)}, u32[]{:S(2)}, u32[]{:S(2)}) collective-permute-start(bf16[480,128]{1,0:T(8,128)(2,1)S(1)} %shard_map.127.refs_0_), channel_id=1, source_target_pairs={{0,8},{8,0},{16,24},{24,16},{1,9},{9,1},{17,25},{25,17},{2,10},{10... | collective-permute-start | bytes 368648 | tf_op jit(solution)/shard_map/ppermute | solution.py:432
  51.8 7.2 %collective-permute-start.22 = (bf16[480,128]{1,0:T(8,128)(2,1)S(1)}, bf16[480,128]{1,0:T(8,128)(2,1)S(1)}, u32[]{:S(2)}, u32[]{:S(2)}) collective-permute-start(bf16[480,128]{1,0:T(8,128)(2,1)S(1)} %shard_map.127.refs_0_), channel_id=1, source_target_pairs={{0,6},{2,4},{4,2},{6,0},{1,7},{3,5},{5,3},{7,1},{8,14},{10,12},{12... | collective-permute-start | bytes 368648 | tf_op jit(solution)/shard_map/ppermute | solution.py:432
  53.4 7.3 %collective-permute-start.21 = (bf16[480,128]{1,0:T(8,128)(2,1)S(1)}, bf16[480,128]{1,0:T(8,128)(2,1)S(1)}, u32[]{:S(2)}, u32[]{:S(2)}) collective-permute-start(bf16[480,128]{1,0:T(8,128)(2,1)S(1)} %shard_map.127.refs_0_), channel_id=1, source_target_pairs={{0,4},{2,6},{4,0},{6,2},{1,5},{3,7},{5,1},{7,3},{8,12},{10,14},{12... | collective-permute-start | bytes 368648 | tf_op jit(solution)/shard_map/ppermute | solution.py:432
  54.0 8.2 %collective-permute-start.20 = (bf16[480,128]{1,0:T(8,128)(2,1)S(1)}, bf16[480,128]{1,0:T(8,128)(2,1)S(1)}, u32[]{:S(2)}, u32[]{:S(2)}) collective-permute-start(bf16[480,128]{1,0:T(8,128)(2,1)S(1)} %shard_map.127.refs_0_), channel_id=1, source_target_pairs={{0,2},{2,0},{4,6},{6,4},{1,3},{3,1},{5,7},{7,5},{8,10},{10,8},{12,... | collective-permute-start | bytes 368648 | tf_op jit(solution)/shard_map/ppermute | solution.py:432
  55.4 10.6 %collective-permute-start.23 = (bf16[2,1,3,1,64,256]{5,4,3,2,1,0:T(8,128)(2,1)S(1)}, bf16[2,1,3,1,64,256]{5,4,3,2,1,0:T(8,128)(2,1)S(1)}, u32[]{:S(2)}, u32[]{:S(2)}) collective-permute-start(bf16[2,1,3,1,64,256]{5,4,3,2,1,0:T(8,128)(2,1)S(1)} %get-tuple-element.103), channel_id=1, source_target_pairs={{0,16},{8,24},{16,0},{24,8},{1,17},{9,25},{17,1},{25,9},{2,18},{10... | collective-permute-start | bytes 589832 | tf_op jit(solution)/shard_map/ppermute | solution.py:432
  58.5 8.7 %collective-permute-start.26 = (bf16[480,128]{1,0:T(8,128)(2,1)S(1)}, bf16[480,128]{1,0:T(8,128)(2,1)S(1)}, u32[]{:S(2)}, u32[]{:S(2)}) collective-permute-start(bf16[480,128]{1,0:T(8,128)(2,1)S(1)} %collective-permute-done.16.refs_0_), channel_id=1, source_target_pairs={{0,4},{2,6},{4,0},{6,2},{1,5},{3,7},{5,1},{7,3},{8,12},{10,14},{12... | collective-permute-start | bytes 368648 | tf_op jit(solution)/shard_map/ppermute | solution.py:432
  59.0 8.2 %collective-permute-start.25 = (bf16[480,128]{1,0:T(8,128)(2,1)S(1)}, bf16[480,128]{1,0:T(8,128)(2,1)S(1)}, u32[]{:S(2)}, u32[]{:S(2)}) collective-permute-start(bf16[480,128]{1,0:T(8,128)(2,1)S(1)} %collective-permute-done.16.refs_0_), channel_id=1, source_target_pairs={{0,2},{2,0},{4,6},{6,4},{1,3},{3,1},{5,7},{7,5},{8,10},{10,8},{12,... | collective-permute-start | bytes 368648 | tf_op jit(solution)/shard_map/ppermute | solution.py:432
  60.6 6.5 %collective-permute-start.19 = (bf16[480,128]{1,0:T(8,128)(2,1)S(1)}, bf16[480,128]{1,0:T(8,128)(2,1)S(1)}, u32[]{:S(2)}, u32[]{:S(2)}) collective-permute-start(bf16[480,128]{1,0:T(8,128)(2,1)S(1)} %collective-permute-done.16.refs_0_), channel_id=1, source_target_pairs={{0,6},{2,4},{4,2},{6,0},{1,7},{3,5},{5,3},{7,1},{8,14},{10,12},{12... | collective-permute-start | bytes 368648 | tf_op jit(solution)/shard_map/ppermute | solution.py:432
  67.2 2.1 %collective-permute-start.27 = (bf16[4,480,128]{2,1,0:T(8,128)(2,1)S(1)}, bf16[4,480,128]{2,1,0:T(8,128)(2,1)S(1)}, u32[]{:S(2)}, u32[]{:S(2)}) collective-permute-start(bf16[4,480,128]{2,1,0:T(8,128)(2,1)S(1)} %shard_map.134.away), channel_id=1, source_target_pairs={{0,1},{1,0},{2,3},{3,2},{4,5},{5,4},{6,7},{7,6},{8,9},{9,8},{10,11... | collective-permute-start | bytes 1474568 | tf_op jit(solution)/shard_map/ppermute | solution.py:432
  67.3 2.6 %collective-permute-start.24 = (bf16[4,480,128]{2,1,0:T(8,128)(2,1)S(1)}, bf16[4,480,128]{2,1,0:T(8,128)(2,1)S(1)}, u32[]{:S(2)}, u32[]{:S(2)}) collective-permute-start(bf16[4,480,128]{2,1,0:T(8,128)(2,1)S(1)} %shard_map.130.home), channel_id=1, source_target_pairs={{0,1},{1,0},{2,3},{3,2},{4,5},{5,4},{6,7},{7,6},{8,9},{9,8},{10,11... | collective-permute-start | bytes 1474568 | tf_op jit(solution)/shard_map/ppermute | solution.py:432
  (6 other events, 11.1 us)

commit v2 on v1

--- a/solution.py
+++ b/solution.py
@@ -543,13 +543,12 @@
     came = pair(leave, "tm", 1)
     away, came = together(away, came)
     crossed = pair(summed([away] + away_came[::-1]), "tm", 1)
+    pre_gradient, home_came[-1] = together(pre_gradient, home_came[-1])
     total = summed([home] + home_came[::-1] + [crossed])
-    pre_gradient, total = together(pre_gradient, total)
     inner, outer = call(
         functools.partial(edges_kernel, rows=rows, frames_first=False),
         [edge, edge],
         [pltpu.SemaphoreType.DMA((2,))],
-        flops=240 * cells * channels * channels,
         moved=512 * 1024,
     )(pre_gradient)
     inner, outer = neighbours(inner, outer, "height")
@@ -558,16 +557,6 @@
         if step > 1:
             total = added(total, other)
         other = pair(total, "tm", 1 << step)
-    total = added(total, other)
-    total, stay, came = together(total, stay, came)
-    other = pair(total, "tm", 1)
-    other, halo_rows = together(other, halo_rows)
-    for step in range(1, shards.bit_length() - 1):
-        count, pieces = (2 * stay.shape[0], stay.shape[1] // 2)
-        stay, leave = call(split_kernel, [((count, pieces) + stay.shape[2:], BF16)] * 2)(stay, came)
-        came = pair(leave, "tm", 1 << step)
-    home_pieces = [total] + pairs([total] * (lines - 1), "height")
-    away_pieces = [other] + pairs([other] * (lines - 1), "height")
     (video_gradient,) = call(
         functools.partial(input_kernel, **sizes),
         [((frames, rows, width, channels), BF16)],
@@ -575,6 +564,15 @@
         flops=18 * cells * channels * channels,
         moved=4 * 1024 * 1024,
     )(valid_from, video, pre_gradient, halo_rows, gain, spatial_weight)
+    other, video_gradient = together(other, video_gradient)
+    total = added(total, other)
+    other = pair(total, "tm", 1)
+    for step in range(1, shards.bit_length() - 1):
+        count, pieces = (2 * stay.shape[0], stay.shape[1] // 2)
+        stay, leave = call(split_kernel, [((count, pieces) + stay.shape[2:], BF16)] * 2)(stay, came)
+        came = pair(leave, "tm", 1 << step)
+    home_pieces = [total] + pairs([total] * (lines - 1), "height")
+    away_pieces = [other] + pairs([other] * (lines - 1), "height")
     home = joined(home_pieces)
     home, came = together(home, came)
     (encoded,) = call(

time: 71.9 us -> 71.2 us (level)
  waiting for transfers between devices: 20.5 us -> 14.8 us
  starting transfers between devices: 29.8 us -> 34.9 us
    ppermute x26, waiting for transfers between devices: 20.5 us -> 14.8 us  [pair(): lax.ppermute(array, axis, [(i, i ^ step) for i in range(lax.axis_size(axi...]
    ppermute x26, starting transfers between devices: 28.5 us -> 33.5 us  [pair(): lax.ppermute(array, axis, [(i, i ^ step) for i in range(lax.axis_size(axi...]
  transfers between devices with their start and end apart: 28 -> 28, of which waited for: 13 -> 11; matrix products, arithmetic and copies ran while one was open for 0% -> 0% of each run, Pallas kernels for 15% -> 16%
where the time goes in v2:
time: 71.2 us; the launch traced here: 70.9 us
  starting transfers between devices  34.9 us (49%)
  Pallas kernels  15.8 us (22%)
  waiting for transfers between devices  14.8 us (21%)
  local copies, waits for them, and re-layouts  3.96 us (6%)
  between operations  1.56 us (2%)
    ppermute x26, starting transfers between devices, pair(): lax.ppermute(array, axis, [(i, i ^ step) for i in range(lax.axis_size(axi...  33.5 us
    pallas_call x19, Pallas kernels, run(): pl.pallas_call(kernel, out_shape=[jax.ShapeDtypeStruct(shape, dtype) for...  15.8 us
    ppermute x26, waiting for transfers between devices, pair(): lax.ppermute(array, axis, [(i, i ^ step) for i in range(lax.axis_size(axi...  14.8 us
    unnamed x20, local copies, waits for them, and re-layouts  3.96 us
  transfers between devices with their start and end apart: 28, of which 11 were waited for; matrix products, arithmetic and copies ran while one was open for 0% of the time, Pallas kernels for 16%

profile of v2, /device:TPU:0, one launch (start us, length us, event | category | flops | bytes accessed | tf_op | source)
XLA Modules:
  0.0 70.9 jit_solution(1379123939662332115)
XLA Ops:
  0.6 0.9 %copy-done.6 = bf16[1,8,1,64,256]{4,3,2,1,0:T(8,128)(2,1)S(1)} copy-done((bf16[1,8,1,64,256]{4,3,2,1,0:T(8,128)(2,1)S(1)}, bf16[1,8,1,64,256]{4,3,2,1,0:T(8,128)(2,1)}, u32[]{:S(2)}) %copy-start.6) | copy-done | bytes 262168
  2.2 5.1 %collective-permute-start.2 = (bf16[5,1,64,256]{3,2,1,0:T(8,128)(2,1)S(1)}, bf16[5,1,64,256]{3,2,1,0:T(8,128)(2,1)S(1)}, u32[]{:S(2)}, u32[]{:S(2)}) collective-permute-start(bf16[5,1,64,256]{3,2,1,0:T(8,128)(2,1)S(1)} %get-tuple-element.72), channel_id=1, source_target_pairs={{0,24},{8,16},{16,8},{24,0},{1,25},{9,17},{17,9},{25,1},{2,26},{10... | collective-permute-start | bytes 491528 | tf_op jit(solution)/shard_map/ppermute | solution.py:432
  8.0 1.0 %copy-done.2 = bf16[1,4,4,64,256]{4,3,2,1,0:T(8,128)(2,1)S(1)} copy-done((bf16[1,4,4,64,256]{4,3,2,1,0:T(8,128)(2,1)S(1)}, bf16[1,4,4,64,256]{4,3,2,1,0:T(8,128)(2,1)}, u32[]{:S(2)}) %copy-start.2) | copy-done | bytes 524312
  9.1 1.7 %collective-permute-start = (bf16[4,64,256]{2,1,0:T(8,128)(2,1)S(1)}, bf16[4,64,256]{2,1,0:T(8,128)(2,1)S(1)}, u32[]{:S(2)}, u32[]{:S(2)}) collective-permute-start(bf16[4,64,256]{2,1,0:T(8,128)(2,1)S(1)} %get-tuple-element.66), channel_id=1, source_target_pairs={{0,2},{2,0},{4,6},{6,4},{1,3},{3,1},{5,7},{7,5},{8,10},{10,8},{12,... | collective-permute-start | bytes 393224 | tf_op jit(solution)/shard_map/ppermute | solution.py:432
  12.2 1.3 %copy-done = bf16[3,3,256,256]{3,2,1,0:T(8,128)(2,1)S(1)} copy-done((bf16[3,3,256,256]{3,2,1,0:T(8,128)(2,1)S(1)}, bf16[3,3,256,256]{3,2,1,0:T(8,128)(2,1)}, u32[]{:S(2)}) %copy-start) | copy-done | bytes 1179672
  14.1 1.9 %shard_map.118 = (bf16[1024,256]{1,0:T(8,128)(2,1)S(1)}, f32[1024,256]{1,0:T(8,128)S(1)}) custom-call(s32[1]{0:T(128)S(6)} %copy.20.valid_from, bf16[4,4,64,256]{3,2,1,0:T(8,128)(2,1)S(1)} %bitcast.16, f32[1,256]{1,0:T(1,128)S(1)} %bitcast.22, bf16[3,3,256,256]{3,2,1,0:T(8,128)(2,1)S(1)} %copy-done), custom_call_target="tpu_custom_call" | custom-call | flops 1207959552 | bytes 4194304 | tf_op jit(solution)/shard_map/pallas_call | solution.py:404
  16.0 1.7 %shard_map.121 = (bf16[1536,256]{1,0:T(8,128)(2,1)S(1)}, f32[1024,256]{1,0:T(8,128)S(1)}, bf16[2,512,256]{2,1,0:T(8,128)(2,1)S(1)}, bf16[768,256]{1,0:T(8,128)(2...) custom-call(s32[1]{0:T(128)S(6)} %copy.20.valid_from, ...), custom_call_target="tpu_custom_call" | custom-call | tf_op jit(solution)/shard_map/pallas_call | solution.py:404
  17.7 3.5 %collective-permute-done.3.refs_1_ = bf16[5,1,64,256]{3,2,1,0:T(8,128)(2,1)S(1)} collective-permute-done((bf16[5,1,64,256]{3,2,1,0:T(8,128)(2,1)S(1)}, bf16[5,1,64,256]{3,2,1,0:T(8,128)(2,1)S(1)}, u32[]{:S(2)}, u32[]{:S(2)}) %collective-permute-start.3) | collective-permute-done | bytes 163872 | tf_op jit(solution)/shard_map/ppermute | solution.py:432
  21.2 2.0 %shard_map.122 = (bf16[4,4,64,256]{3,2,1,0:T(8,128)(2,1)S(1)}, f32[2048,128]{1,0:T(8,128)S(1)}, bf16[2048,128]{1,0:T(8,128)(2,1)S(1)}) custom-call(bf16[1536,256]{1,0:T(8,128)(2,1)S(1)} %get-tuple-element.68.tall, f32[1024,256]{1,0:T(8,128)S(1)} %get-tuple-element.69.slope, bf16[2,512,256]{2,1,0:T(8,128)(2,1)S(1)} %get-tuple-element.70.active, ...), custom_call_target="tpu_custom_call" | custom-call | flops 1342177280 | bytes 6291456 | tf_op jit(solution)/shard_map/pallas_call | solution.py:404
  23.4 1.2 %shard_map.123 = (f32[1792,128]{1,0:T(8,128)S(1)}, bf16[1792,128]{1,0:T(8,128)(2,1)S(1)}) custom-call(bf16[1536,256]{1,0:T(8,128)(2,1)S(1)} %get-tuple-element.68.tall, bf16[4,4,64,256]{3,2,1,0:T(8,128)(2,1)S(1)} %get-tuple-element.91.pre_gradient.source), custom_call_target="tpu_custom_call" | custom-call | flops 1073741824 | bytes 6291456 | tf_op jit(solution)/shard_map/pallas_call | solution.py:404
  25.1 1.4 %collective-permute-done.6 = bf16[1792,128]{1,0:T(8,128)(2,1)S(1)} collective-permute-done((bf16[1792,128]{1,0:T(8,128)(2,1)S(1)}, bf16[1792,128]{1,0:T(8,128)(2,1)S(1)}, u32[]{:S(2)}, u32[]{:S(2)}) %collective-permute-start.6) | collective-permute-done | bytes 458784 | tf_op jit(solution)/shard_map/ppermute | solution.py:432
  26.8 2.5 %collective-permute-start.11 = (bf16[480,128]{1,0:T(8,128)(2,1)S(1)}, bf16[480,128]{1,0:T(8,128)(2,1)S(1)}, u32[]{:S(2)}, u32[]{:S(2)}) collective-permute-start(bf16[480,128]{1,0:T(8,128)(2,1)S(1)} %get-tuple-element.88), channel_id=1, source_target_pairs={{0,6},{2,4},{4,2},{6,0},{1,7},{3,5},{5,3},{7,1},{8,14},{10,12},{12... | collective-permute-start | bytes 368648 | tf_op jit(solution)/shard_map/ppermute | solution.py:432
  30.4 2.4 %collective-permute-start.7 = (bf16[480,128]{1,0:T(8,128)(2,1)S(1)}, bf16[480,128]{1,0:T(8,128)(2,1)S(1)}, u32[]{:S(2)}, u32[]{:S(2)}) collective-permute-start(bf16[480,128]{1,0:T(8,128)(2,1)S(1)} %get-tuple-element.81), channel_id=1, source_target_pairs={{0,6},{2,4},{4,2},{6,0},{1,7},{3,5},{5,3},{7,1},{8,14},{10,12},{12... | collective-permute-start | bytes 368648 | tf_op jit(solution)/shard_map/ppermute | solution.py:432
  32.8 0.7 %collective-permute-start.8 = (bf16[480,128]{1,0:T(8,128)(2,1)S(1)}, bf16[480,128]{1,0:T(8,128)(2,1)S(1)}, u32[]{:S(2)}, u32[]{:S(2)}) collective-permute-start(bf16[480,128]{1,0:T(8,128)(2,1)S(1)} %get-tuple-element.83), channel_id=1, source_target_pairs={{0,4},{2,6},{4,0},{6,2},{1,5},{3,7},{5,1},{7,3},{8,12},{10,14},{12... | collective-permute-start | bytes 368648 | tf_op jit(solution)/shard_map/ppermute | solution.py:432
  33.5 1.9 %collective-permute-start.9 = (bf16[480,128]{1,0:T(8,128)(2,1)S(1)}, bf16[480,128]{1,0:T(8,128)(2,1)S(1)}, u32[]{:S(2)}, u32[]{:S(2)}) collective-permute-start(bf16[480,128]{1,0:T(8,128)(2,1)S(1)} %get-tuple-element.84), channel_id=1, source_target_pairs={{0,2},{2,0},{4,6},{6,4},{1,3},{3,1},{5,7},{7,5},{8,10},{10,8},{12,... | collective-permute-start | bytes 368648 | tf_op jit(solution)/shard_map/ppermute | solution.py:432
  35.4 1.7 %collective-permute-done.12.refs_1_ = bf16[480,128]{1,0:T(8,128)(2,1)S(1)} collective-permute-done((bf16[480,128]{1,0:T(8,128)(2,1)S(1)}, bf16[480,128]{1,0:T(8,128)(2,1)S(1)}, u32[]{:S(2)}, u32[]{:S(2)}) %collective-permute-start.12) | collective-permute-done | bytes 122912 | tf_op jit(solution)/shard_map/ppermute | solution.py:432
  37.6 2.0 %collective-permute-done.7.refs_0_ = bf16[480,128]{1,0:T(8,128)(2,1)S(1)} collective-permute-done((bf16[480,128]{1,0:T(8,128)(2,1)S(1)}, bf16[480,128]{1,0:T(8,128)(2,1)S(1)}, u32[]{:S(2)}, u32[]{:S(2)}) %collective-permute-start.7) | collective-permute-done | bytes 122912 | tf_op jit(solution)/shard_map/ppermute | solution.py:432
  40.0 1.2 %collective-permute-start.16 = (bf16[4,64,256]{2,1,0:T(8,128)(2,1)S(1)}, bf16[4,64,256]{2,1,0:T(8,128)(2,1)S(1)}, u32[]{:S(2)}, u32[]{:S(2)}) collective-permute-start(bf16[4,64,256]{2,1,0:T(8,128)(2,1)S(1)} %get-tuple-element.92), channel_id=1, source_target_pairs={{0,2},{2,0},{4,6},{6,4},{1,3},{3,1},{5,7},{7,5},{8,10},{10,8},{12,... | collective-permute-start | bytes 393224 | tf_op jit(solution)/shard_map/ppermute | solution.py:432
  42.4 1.6 %collective-permute-start.15 = (bf16[480,128]{1,0:T(8,128)(2,1)S(1)}, bf16[480,128]{1,0:T(8,128)(2,1)S(1)}, u32[]{:S(2)}, u32[]{:S(2)}) collective-permute-start(bf16[480,128]{1,0:T(8,128)(2,1)S(1)} %shard_map.126.left), channel_id=1, source_target_pairs={{0,16},{8,24},{16,0},{24,8},{1,17},{9,25},{17,1},{25,9},{2,18},{10... | collective-permute-start | bytes 368648 | tf_op jit(solution)/shard_map/ppermute | solution.py:432
  44.0 1.0 %collective-permute-done.16.inner = bf16[4,64,256]{2,1,0:T(8,128)(2,1)S(1)} collective-permute-done((bf16[4,64,256]{2,1,0:T(8,128)(2,1)S(1)}, bf16[4,64,256]{2,1,0:T(8,128)(2,1)S(1)}, u32[]{:S(2)}, u32[]{:S(2)}) %collective-permute-start.16) | collective-permute-done | bytes 131104 | tf_op jit(solution)/shard_map/ppermute | solution.py:432
  45.0 3.0 %shard_map.129 = bf16[4,4,64,256]{3,2,1,0:T(8,128)(2,1)} custom-call(s32[1]{0:T(128)S(6)} %copy.20.valid_from, bf16[4,4,64,256]{3,2,1,0:T(8,128)(2,1)S(1)} %bitcast.17, bf16[4,4,64,256]{3,2,1,0:T(8,128)(2,1)S(1)} %get-tuple-element.91.pre_gradient.source, bf16[2,4,64,256]{3,2,1,0:T(8,128)(2,1)S(1)} %shard_map.128.halo, f32[1,256]{1,0:T(1,128)S(1)} %bitcast.24, ...), custom_call_target="tpu_custom_call" | custom-call | flops 1207959552 | bytes 4194304 | tf_op jit(solution)/shard_map/pallas_call | solution.py:404
  48.1 2.0 %collective-permute-done.15.right = bf16[480,128]{1,0:T(8,128)(2,1)S(1)} collective-permute-done((bf16[480,128]{1,0:T(8,128)(2,1)S(1)}, bf16[480,128]{1,0:T(8,128)(2,1)S(1)}, u32[]{:S(2)}, u32[]{:S(2)}) %collective-permute-start.15) | collective-permute-done | bytes 122912 | tf_op jit(solution)/shard_map/ppermute | solution.py:432
  50.2 2.0 %collective-permute-start.22 = (bf16[480,128]{1,0:T(8,128)(2,1)S(1)}, bf16[480,128]{1,0:T(8,128)(2,1)S(1)}, u32[]{:S(2)}, u32[]{:S(2)}) collective-permute-start(bf16[480,128]{1,0:T(8,128)(2,1)S(1)} %shard_map.130.refs_0_), channel_id=1, source_target_pairs={{0,6},{2,4},{4,2},{6,0},{1,7},{3,5},{5,3},{7,1},{8,14},{10,12},{12... | collective-permute-start | bytes 368648 | tf_op jit(solution)/shard_map/ppermute | solution.py:432
  52.1 3.0 %collective-permute-start.21 = (bf16[480,128]{1,0:T(8,128)(2,1)S(1)}, bf16[480,128]{1,0:T(8,128)(2,1)S(1)}, u32[]{:S(2)}, u32[]{:S(2)}) collective-permute-start(bf16[480,128]{1,0:T(8,128)(2,1)S(1)} %shard_map.130.refs_0_), channel_id=1, source_target_pairs={{0,4},{2,6},{4,0},{6,2},{1,5},{3,7},{5,1},{7,3},{8,12},{10,14},{12... | collective-permute-start | bytes 368648 | tf_op jit(solution)/shard_map/ppermute | solution.py:432
  55.1 2.9 %collective-permute-start.23 = (bf16[2,1,3,1,64,256]{5,4,3,2,1,0:T(8,128)(2,1)S(1)}, bf16[2,1,3,1,64,256]{5,4,3,2,1,0:T(8,128)(2,1)S(1)}, u32[]{:S(2)}, u32[]{:S(2)}) collective-permute-start(bf16[2,1,3,1,64,256]{5,4,3,2,1,0:T(8,128)(2,1)S(1)} %get-tuple-element.97), channel_id=1, source_target_pairs={{0,16},{8,24},{16,0},{24,8},{1,17},{9,25},{17,1},{25,9},{2,18},{10... | collective-permute-start | bytes 589832 | tf_op jit(solution)/shard_map/ppermute | solution.py:432
  58.2 1.5 %collective-permute-start.19 = (bf16[480,128]{1,0:T(8,128)(2,1)S(1)}, bf16[480,128]{1,0:T(8,128)(2,1)S(1)}, u32[]{:S(2)}, u32[]{:S(2)}) collective-permute-start(bf16[480,128]{1,0:T(8,128)(2,1)S(1)} %collective-permute-done.18.refs_0_), channel_id=1, source_target_pairs={{0,6},{2,4},{4,2},{6,0},{1,7},{3,5},{5,3},{7,1},{8,14},{10,12},{12... | collective-permute-start | bytes 368648 | tf_op jit(solution)/shard_map/ppermute | solution.py:432
  59.7 1.8 %collective-permute-start.26 = (bf16[480,128]{1,0:T(8,128)(2,1)S(1)}, bf16[480,128]{1,0:T(8,128)(2,1)S(1)}, u32[]{:S(2)}, u32[]{:S(2)}) collective-permute-start(bf16[480,128]{1,0:T(8,128)(2,1)S(1)} %collective-permute-done.18.refs_0_), channel_id=1, source_target_pairs={{0,4},{2,6},{4,0},{6,2},{1,5},{3,7},{5,1},{7,3},{8,12},{10,14},{12... | collective-permute-start | bytes 368648 | tf_op jit(solution)/shard_map/ppermute | solution.py:432
  61.5 1.7 %collective-permute-start.25 = (bf16[480,128]{1,0:T(8,128)(2,1)S(1)}, bf16[480,128]{1,0:T(8,128)(2,1)S(1)}, u32[]{:S(2)}, u32[]{:S(2)}) collective-permute-start(bf16[480,128]{1,0:T(8,128)(2,1)S(1)} %collective-permute-done.18.refs_0_), channel_id=1, source_target_pairs={{0,2},{2,0},{4,6},{6,4},{1,3},{3,1},{5,7},{7,5},{8,10},{10,8},{12,... | collective-permute-start | bytes 368648 | tf_op jit(solution)/shard_map/ppermute | solution.py:432
  63.9 1.2 %collective-permute-done.23.came = bf16[2,1,3,1,64,256]{5,4,3,2,1,0:T(8,128)(2,1)S(1)} collective-permute-done((bf16[2,1,3,1,64,256]{5,4,3,2,1,0:T(8,128)(2,1)S(1)}, bf16[2,1,3,1,64,256]{5,4,3,2,1,0:T(8,128)(2,1)S(1)}, u32[]{:S(2)}, u32[]{:S(2)}) %collective-permute-start.23) | collective-permute-done | bytes 196640 | tf_op jit(solution)/shard_map/ppermute | solution.py:432
  65.1 1.1 %shard_map.133 = bf16[8,1,64,256]{3,2,1,0:T(8,128)(2,1)} custom-call(bf16[3,256,256]{2,1,0:T(8,128)(2,1)S(1)} %copy-done.4, bf16[2,1,3,1,64,256]{5,4,3,2,1,0:T(8,128)(2,1)S(1)} %get-tuple-element.100.stay, bf16[2,1,3,1,64,256]{5,4,3,2,1,0:T(8,128)(2,1)S(1)} %collective-permute-done.23.came), custom_call_target="tpu_custom_call" | custom-call | flops 201326592 | bytes 2097152 | tf_op jit(solution)/shard_map/pallas_call | solution.py:404
  67.1 1.5 %shard_map.135 = (f32[9,256,256]{2,1,0:T(8,128)}, f32[3,256,256]{2,1,0:T(8,128)}, f32[3,256,256]{2,1,0:T(8,128)}, f32[256,128]{1,0:T(8,128)S(1)}) custom-call(bf16[4,480,128]{2,1,0:T(8,128)(2,1)S(1)} %shard_map.131.home, bf16[4,480,128]{2,1,0:T(8,128)(2,1)S(1)} %shard_map.134.away, bf16[3,3,256,256]{3,2,1,0:T(8,128)(2,1)S(1)} %copy-done.1), custom_call_target="tpu_custom_call" | custom-call | bytes 4194304 | tf_op jit(solution)/shard_map/pallas_call | solution.py:404
  69.2 1.7 %shard_map.136 = (f32[9,256,256]{2,1,0:T(8,128)}, f32[3,256,256]{2,1,0:T(8,128)}, f32[3,256,256]{2,1,0:T(8,128)}, f32[1,256]{1,0:T(1,128)}) custom-call(bf16[4,480,128]{2,1,0:T(8,128)(2,1)S(1)} %collective-permute-done.24.home, bf16[4,480,128]{2,1,0:T(8,128)(2,1)S(1)} %collective-permute-done.27.away, ...), custom_call_target="tpu_custom_call", output_to_operand_aliasing={{0}: (5, {}), {1}: (6, {}), {2}: (7, {})} | custom-call | bytes 4194304 | tf_op jit(solution)/shard_map/pallas_call | solution.py:404
  (63 shorter events, 9.1 us)
Async XLA Ops:
  2.2 15.5 %collective-permute-start.2 = (bf16[5,1,64,256]{3,2,1,0:T(8,128)(2,1)S(1)}, bf16[5,1,64,256]{3,2,1,0:T(8,128)(2,1)S(1)}, u32[]{:S(2)}, u32[]{:S(2)}) collective-permute-start(bf16[5,1,64,256]{3,2,1,0:T(8,128)(2,1)S(1)} %get-tuple-element.72), channel_id=1, source_target_pairs={{0,24},{8,16},{16,8},{24,0},{1,25},{9,17},{17,9},{25,1},{2,26},{10... | collective-permute-start | bytes 491528 | tf_op jit(solution)/shard_map/ppermute | solution.py:432
  7.3 13.9 %collective-permute-start.3 = (bf16[5,1,64,256]{3,2,1,0:T(8,128)(2,1)S(1)}, bf16[5,1,64,256]{3,2,1,0:T(8,128)(2,1)S(1)}, u32[]{:S(2)}, u32[]{:S(2)}) collective-permute-start(bf16[5,1,64,256]{3,2,1,0:T(8,128)(2,1)S(1)} %get-tuple-element.73), channel_id=1, source_target_pairs={{0,16},{8,24},{16,0},{24,8},{1,17},{9,25},{17,1},{25,9},{2,18},{10... | collective-permute-start | bytes 491528 | tf_op jit(solution)/shard_map/ppermute | solution.py:432
  7.3 13.9 %collective-permute-start.4 = (bf16[5,1,64,256]{3,2,1,0:T(8,128)(2,1)S(1)}, bf16[5,1,64,256]{3,2,1,0:T(8,128)(2,1)S(1)}, u32[]{:S(2)}, u32[]{:S(2)}) collective-permute-start(bf16[5,1,64,256]{3,2,1,0:T(8,128)(2,1)S(1)} %get-tuple-element.74), channel_id=1, source_target_pairs={{0,8},{8,0},{16,24},{24,16},{1,9},{9,1},{17,25},{25,17},{2,10},{10... | collective-permute-start | bytes 491528 | tf_op jit(solution)/shard_map/ppermute | solution.py:432
  9.0 7.0 %copy-start.5 = (bf16[3,256,256]{2,1,0:T(8,128)(2,1)S(1)}, bf16[3,256,256]{2,1,0:T(8,128)(2,1)}, u32[]{:S(2)}) copy-start(bf16[3,256,256]{2,1,0:T(8,128)(2,1)} %temporal.3) | copy-start | bytes 1179652
  9.1 6.9 %collective-permute-start = (bf16[4,64,256]{2,1,0:T(8,128)(2,1)S(1)}, bf16[4,64,256]{2,1,0:T(8,128)(2,1)S(1)}, u32[]{:S(2)}, u32[]{:S(2)}) collective-permute-start(bf16[4,64,256]{2,1,0:T(8,128)(2,1)S(1)} %get-tuple-element.66), channel_id=1, source_target_pairs={{0,2},{2,0},{4,6},{6,4},{1,3},{3,1},{5,7},{7,5},{8,10},{10,8},{12,... | collective-permute-start | bytes 393224 | tf_op jit(solution)/shard_map/ppermute | solution.py:432
  10.8 5.2 %collective-permute-start.1 = (bf16[4,64,256]{2,1,0:T(8,128)(2,1)S(1)}, bf16[4,64,256]{2,1,0:T(8,128)(2,1)S(1)}, u32[]{:S(2)}, u32[]{:S(2)}) collective-permute-start(bf16[4,64,256]{2,1,0:T(8,128)(2,1)S(1)} %get-tuple-element.67), channel_id=1, source_target_pairs={{2,4},{4,2},{3,5},{5,3},{10,12},{12,10},{11,13},{13,11},{18,20},{2... | collective-permute-start | bytes 393224 | tf_op jit(solution)/shard_map/ppermute | solution.py:428
  16.0 5.2 %copy-start.4 = (bf16[3,256,256]{2,1,0:T(8,128)(2,1)S(1)}, bf16[3,256,256]{2,1,0:T(8,128)(2,1)}, u32[]{:S(2)}) copy-start(bf16[3,256,256]{2,1,0:T(8,128)(2,1)} %mix.3) | copy-start | bytes 1179652
  23.3 3.3 %collective-permute-start.5 = (bf16[2048,128]{1,0:T(8,128)(2,1)S(1)}, bf16[2048,128]{1,0:T(8,128)(2,1)S(1)}, u32[]{:S(2)}, u32[]{:S(2)}) collective-permute-start(bf16[2048,128]{1,0:T(8,128)(2,1)S(1)} %get-tuple-element.76), channel_id=1, source_target_pairs={{0,1},{1,0},{2,3},{3,2},{4,5},{5,4},{6,7},{7,6},{8,9},{9,8},{10,11... | collective-permute-start | bytes 1572872 | tf_op jit(solution)/shard_map/ppermute | solution.py:432
  24.6 2.0 %collective-permute-start.6 = (bf16[1792,128]{1,0:T(8,128)(2,1)S(1)}, bf16[1792,128]{1,0:T(8,128)(2,1)S(1)}, u32[]{:S(2)}, u32[]{:S(2)}) collective-permute-start(bf16[1792,128]{1,0:T(8,128)(2,1)S(1)} %get-tuple-element.79), channel_id=1, source_target_pairs={{0,1},{1,0},{2,3},{3,2},{4,5},{5,4},{6,7},{7,6},{8,9},{9,8},{10,11... | collective-permute-start | bytes 1376264 | tf_op jit(solution)/shard_map/ppermute | solution.py:432
  25.1 7.7 %collective-permute-start.10 = (bf16[1,2,3,1,64,256]{5,4,3,2,1,0:T(8,128)(2,1)S(1)}, bf16[1,2,3,1,64,256]{5,4,3,2,1,0:T(8,128)(2,1)S(1)}, u32[]{:S(2)}, u32[]{:S(2)}) collective-permute-start(bf16[1,2,3,1,64,256]{5,4,3,2,1,0:T(8,128)(2,1)S(1)} %get-tuple-element.86), channel_id=1, source_target_pairs={{0,8},{8,0},{16,24},{24,16},{1,9},{9,1},{17,25},{25,17},{2,10},{10... | collective-permute-start | bytes 589832 | tf_op jit(solution)/shard_map/ppermute | solution.py:432
  26.6 18.5 %copy-start.3 = (bf16[1,4,4,64,256]{4,3,2,1,0:T(8,128)(2,1)S(1)}, bf16[1,4,4,64,256]{4,3,2,1,0:T(8,128)(2,1)}, u32[]{:S(2)}) copy-start(bf16[1,4,4,64,256]{4,3,2,1,0:T(8,128)(2,1)} %param.7) | copy-start | bytes 1572868
  26.6 18.5 %copy-start.9 = (f32[256]{0:T(256)S(1)}, f32[256]{0:T(256)}, u32[]{:S(2)}) copy-start(f32[256]{0:T(256)} %param.9) | copy-start | bytes 3076
  26.8 6.8 %collective-permute-start.11 = (bf16[480,128]{1,0:T(8,128)(2,1)S(1)}, bf16[480,128]{1,0:T(8,128)(2,1)S(1)}, u32[]{:S(2)}, u32[]{:S(2)}) collective-permute-start(bf16[480,128]{1,0:T(8,128)(2,1)S(1)} %get-tuple-element.88), channel_id=1, source_target_pairs={{0,6},{2,4},{4,2},{6,0},{1,7},{3,5},{5,3},{7,1},{8,14},{10,12},{12... | collective-permute-start | bytes 368648 | tf_op jit(solution)/shard_map/ppermute | solution.py:432
  29.3 7.8 %collective-permute-start.12 = (bf16[480,128]{1,0:T(8,128)(2,1)S(1)}, bf16[480,128]{1,0:T(8,128)(2,1)S(1)}, u32[]{:S(2)}, u32[]{:S(2)}) collective-permute-start(bf16[480,128]{1,0:T(8,128)(2,1)S(1)} %get-tuple-element.89), channel_id=1, source_target_pairs={{0,4},{2,6},{4,0},{6,2},{1,5},{3,7},{5,1},{7,3},{8,12},{10,14},{12... | collective-permute-start | bytes 368648 | tf_op jit(solution)/shard_map/ppermute | solution.py:432
  29.8 7.3 %collective-permute-start.13 = (bf16[480,128]{1,0:T(8,128)(2,1)S(1)}, bf16[480,128]{1,0:T(8,128)(2,1)S(1)}, u32[]{:S(2)}, u32[]{:S(2)}) collective-permute-start(bf16[480,128]{1,0:T(8,128)(2,1)S(1)} %get-tuple-element.90), channel_id=1, source_target_pairs={{0,2},{2,0},{4,6},{6,4},{1,3},{3,1},{5,7},{7,5},{8,10},{10,8},{12,... | collective-permute-start | bytes 368648 | tf_op jit(solution)/shard_map/ppermute | solution.py:432
  30.4 9.3 %collective-permute-start.7 = (bf16[480,128]{1,0:T(8,128)(2,1)S(1)}, bf16[480,128]{1,0:T(8,128)(2,1)S(1)}, u32[]{:S(2)}, u32[]{:S(2)}) collective-permute-start(bf16[480,128]{1,0:T(8,128)(2,1)S(1)} %get-tuple-element.81), channel_id=1, source_target_pairs={{0,6},{2,4},{4,2},{6,0},{1,7},{3,5},{5,3},{7,1},{8,14},{10,12},{12... | collective-permute-start | bytes 368648 | tf_op jit(solution)/shard_map/ppermute | solution.py:432
  32.8 9.0 %collective-permute-start.8 = (bf16[480,128]{1,0:T(8,128)(2,1)S(1)}, bf16[480,128]{1,0:T(8,128)(2,1)S(1)}, u32[]{:S(2)}, u32[]{:S(2)}) collective-permute-start(bf16[480,128]{1,0:T(8,128)(2,1)S(1)} %get-tuple-element.83), channel_id=1, source_target_pairs={{0,4},{2,6},{4,0},{6,2},{1,5},{3,7},{5,1},{7,3},{8,12},{10,14},{12... | collective-permute-start | bytes 368648 | tf_op jit(solution)/shard_map/ppermute | solution.py:432
  33.5 8.3 %collective-permute-start.9 = (bf16[480,128]{1,0:T(8,128)(2,1)S(1)}, bf16[480,128]{1,0:T(8,128)(2,1)S(1)}, u32[]{:S(2)}, u32[]{:S(2)}) collective-permute-start(bf16[480,128]{1,0:T(8,128)(2,1)S(1)} %get-tuple-element.84), channel_id=1, source_target_pairs={{0,2},{2,0},{4,6},{6,4},{1,3},{3,1},{5,7},{7,5},{8,10},{10,8},{12,... | collective-permute-start | bytes 368648 | tf_op jit(solution)/shard_map/ppermute | solution.py:432
  37.2 5.1 %collective-permute-start.14 = (bf16[480,128]{1,0:T(8,128)(2,1)S(1)}, bf16[480,128]{1,0:T(8,128)(2,1)S(1)}, u32[]{:S(2)}, u32[]{:S(2)}) collective-permute-start(bf16[480,128]{1,0:T(8,128)(2,1)S(1)} %shard_map.125), channel_id=1, source_target_pairs={{0,8},{8,0},{16,24},{24,16},{1,9},{9,1},{17,25},{25,17},{2,10},{10... | collective-permute-start | bytes 368648 | tf_op jit(solution)/shard_map/ppermute | solution.py:432
  40.0 5.0 %collective-permute-start.16 = (bf16[4,64,256]{2,1,0:T(8,128)(2,1)S(1)}, bf16[4,64,256]{2,1,0:T(8,128)(2,1)S(1)}, u32[]{:S(2)}, u32[]{:S(2)}) collective-permute-start(bf16[4,64,256]{2,1,0:T(8,128)(2,1)S(1)} %get-tuple-element.92), channel_id=1, source_target_pairs={{0,2},{2,0},{4,6},{6,4},{1,3},{3,1},{5,7},{7,5},{8,10},{10,8},{12,... | collective-permute-start | bytes 393224 | tf_op jit(solution)/shard_map/ppermute | solution.py:432
  41.1 3.9 %collective-permute-start.17 = (bf16[4,64,256]{2,1,0:T(8,128)(2,1)S(1)}, bf16[4,64,256]{2,1,0:T(8,128)(2,1)S(1)}, u32[]{:S(2)}, u32[]{:S(2)}) collective-permute-start(bf16[4,64,256]{2,1,0:T(8,128)(2,1)S(1)} %get-tuple-element.93), channel_id=1, source_target_pairs={{2,4},{4,2},{3,5},{5,3},{10,12},{12,10},{11,13},{13,11},{18,20},{2... | collective-permute-start | bytes 393224 | tf_op jit(solution)/shard_map/ppermute | solution.py:428
  42.4 7.7 %collective-permute-start.15 = (bf16[480,128]{1,0:T(8,128)(2,1)S(1)}, bf16[480,128]{1,0:T(8,128)(2,1)S(1)}, u32[]{:S(2)}, u32[]{:S(2)}) collective-permute-start(bf16[480,128]{1,0:T(8,128)(2,1)S(1)} %shard_map.126.left), channel_id=1, source_target_pairs={{0,16},{8,24},{16,0},{24,8},{1,17},{9,25},{17,1},{25,9},{2,18},{10... | collective-permute-start | bytes 368648 | tf_op jit(solution)/shard_map/ppermute | solution.py:432
  50.1 8.1 %collective-permute-start.18 = (bf16[480,128]{1,0:T(8,128)(2,1)S(1)}, bf16[480,128]{1,0:T(8,128)(2,1)S(1)}, u32[]{:S(2)}, u32[]{:S(2)}) collective-permute-start(bf16[480,128]{1,0:T(8,128)(2,1)S(1)} %shard_map.130.refs_0_), channel_id=1, source_target_pairs={{0,8},{8,0},{16,24},{24,16},{1,9},{9,1},{17,25},{25,17},{2,10},{10... | collective-permute-start | bytes 368648 | tf_op jit(solution)/shard_map/ppermute | solution.py:432
  50.2 9.5 %collective-permute-start.22 = (bf16[480,128]{1,0:T(8,128)(2,1)S(1)}, bf16[480,128]{1,0:T(8,128)(2,1)S(1)}, u32[]{:S(2)}, u32[]{:S(2)}) collective-permute-start(bf16[480,128]{1,0:T(8,128)(2,1)S(1)} %shard_map.130.refs_0_), channel_id=1, source_target_pairs={{0,6},{2,4},{4,2},{6,0},{1,7},{3,5},{5,3},{7,1},{8,14},{10,12},{12... | collective-permute-start | bytes 368648 | tf_op jit(solution)/shard_map/ppermute | solution.py:432
  52.1 9.4 %collective-permute-start.21 = (bf16[480,128]{1,0:T(8,128)(2,1)S(1)}, bf16[480,128]{1,0:T(8,128)(2,1)S(1)}, u32[]{:S(2)}, u32[]{:S(2)}) collective-permute-start(bf16[480,128]{1,0:T(8,128)(2,1)S(1)} %shard_map.130.refs_0_), channel_id=1, source_target_pairs={{0,4},{2,6},{4,0},{6,2},{1,5},{3,7},{5,1},{7,3},{8,12},{10,14},{12... | collective-permute-start | bytes 368648 | tf_op jit(solution)/shard_map/ppermute | solution.py:432
  55.1 10.0 %collective-permute-start.23 = (bf16[2,1,3,1,64,256]{5,4,3,2,1,0:T(8,128)(2,1)S(1)}, bf16[2,1,3,1,64,256]{5,4,3,2,1,0:T(8,128)(2,1)S(1)}, u32[]{:S(2)}, u32[]{:S(2)}) collective-permute-start(bf16[2,1,3,1,64,256]{5,4,3,2,1,0:T(8,128)(2,1)S(1)} %get-tuple-element.97), channel_id=1, source_target_pairs={{0,16},{8,24},{16,0},{24,8},{1,17},{9,25},{17,1},{25,9},{2,18},{10... | collective-permute-start | bytes 589832 | tf_op jit(solution)/shard_map/ppermute | solution.py:432
  58.0 5.8 %collective-permute-start.20 = (bf16[480,128]{1,0:T(8,128)(2,1)S(1)}, bf16[480,128]{1,0:T(8,128)(2,1)S(1)}, u32[]{:S(2)}, u32[]{:S(2)}) collective-permute-start(bf16[480,128]{1,0:T(8,128)(2,1)S(1)} %shard_map.130.refs_0_), channel_id=1, source_target_pairs={{0,2},{2,0},{4,6},{6,4},{1,3},{3,1},{5,7},{7,5},{8,10},{10,8},{12,... | collective-permute-start | bytes 368648 | tf_op jit(solution)/shard_map/ppermute | solution.py:432
  58.2 8.0 %collective-permute-start.19 = (bf16[480,128]{1,0:T(8,128)(2,1)S(1)}, bf16[480,128]{1,0:T(8,128)(2,1)S(1)}, u32[]{:S(2)}, u32[]{:S(2)}) collective-permute-start(bf16[480,128]{1,0:T(8,128)(2,1)S(1)} %collective-permute-done.18.refs_0_), channel_id=1, source_target_pairs={{0,6},{2,4},{4,2},{6,0},{1,7},{3,5},{5,3},{7,1},{8,14},{10,12},{12... | collective-permute-start | bytes 368648 | tf_op jit(solution)/shard_map/ppermute | solution.py:432
  59.7 6.5 %collective-permute-start.26 = (bf16[480,128]{1,0:T(8,128)(2,1)S(1)}, bf16[480,128]{1,0:T(8,128)(2,1)S(1)}, u32[]{:S(2)}, u32[]{:S(2)}) collective-permute-start(bf16[480,128]{1,0:T(8,128)(2,1)S(1)} %collective-permute-done.18.refs_0_), channel_id=1, source_target_pairs={{0,4},{2,6},{4,0},{6,2},{1,5},{3,7},{5,1},{7,3},{8,12},{10,14},{12... | collective-permute-start | bytes 368648 | tf_op jit(solution)/shard_map/ppermute | solution.py:432
  61.5 5.0 %collective-permute-start.25 = (bf16[480,128]{1,0:T(8,128)(2,1)S(1)}, bf16[480,128]{1,0:T(8,128)(2,1)S(1)}, u32[]{:S(2)}, u32[]{:S(2)}) collective-permute-start(bf16[480,128]{1,0:T(8,128)(2,1)S(1)} %collective-permute-done.18.refs_0_), channel_id=1, source_target_pairs={{0,2},{2,0},{4,6},{6,4},{1,3},{3,1},{5,7},{7,5},{8,10},{10,8},{12,... | collective-permute-start | bytes 368648 | tf_op jit(solution)/shard_map/ppermute | solution.py:432
  66.5 2.1 %collective-permute-start.27 = (bf16[4,480,128]{2,1,0:T(8,128)(2,1)S(1)}, bf16[4,480,128]{2,1,0:T(8,128)(2,1)S(1)}, u32[]{:S(2)}, u32[]{:S(2)}) collective-permute-start(bf16[4,480,128]{2,1,0:T(8,128)(2,1)S(1)} %shard_map.134.away), channel_id=1, source_target_pairs={{0,1},{1,0},{2,3},{3,2},{4,5},{5,4},{6,7},{7,6},{8,9},{9,8},{10,11... | collective-permute-start | bytes 1474568 | tf_op jit(solution)/shard_map/ppermute | solution.py:432
  66.6 2.6 %collective-permute-start.24 = (bf16[4,480,128]{2,1,0:T(8,128)(2,1)S(1)}, bf16[4,480,128]{2,1,0:T(8,128)(2,1)S(1)}, u32[]{:S(2)}, u32[]{:S(2)}) collective-permute-start(bf16[4,480,128]{2,1,0:T(8,128)(2,1)S(1)} %shard_map.131.home), channel_id=1, source_target_pairs={{0,1},{1,0},{2,3},{3,2},{4,5},{5,4},{6,7},{7,6},{8,9},{9,8},{10,11... | collective-permute-start | bytes 1474568 | tf_op jit(solution)/shard_map/ppermute | solution.py:432
  (6 other events, 11.1 us)

commit v3 on v2

--- a/solution.py
+++ b/solution.py
@@ -11,7 +11,7 @@
 F32 = jnp.float32
 BF16 = jnp.bfloat16
 VMEM_LIMIT = 16 * 1024 * 1024
-SPLIT = 8
+SPLIT = 10
 
 
 def dot(left, right):

time: 71.2 us -> 70.9 us (level)
  transfers between devices with their start and end apart: 28 -> 28, of which waited for: 11 -> 11; matrix products, arithmetic and copies ran while one was open for 0% -> 0% of each run, Pallas kernels for 16% -> 15%
where the time goes in v3:
time: 70.9 us; the launch traced here: 70.6 us
  starting transfers between devices  35.3 us (50%)
  Pallas kernels  15.4 us (22%)
  waiting for transfers between devices  14.3 us (20%)
  local copies, waits for them, and re-layouts  3.96 us (6%)
  between operations  1.56 us (2%)
    ppermute x26, starting transfers between devices, pair(): lax.ppermute(array, axis, [(i, i ^ step) for i in range(lax.axis_size(axi...  34 us
    pallas_call x19, Pallas kernels, run(): pl.pallas_call(kernel, out_shape=[jax.ShapeDtypeStruct(shape, dtype) for...  15.4 us
    ppermute x26, waiting for transfers between devices, pair(): lax.ppermute(array, axis, [(i, i ^ step) for i in range(lax.axis_size(axi...  14.3 us
    unnamed x20, local copies, waits for them, and re-layouts  3.96 us
  transfers between devices with their start and end apart: 28, of which 11 were waited for; matrix products, arithmetic and copies ran while one was open for 0% of the time, Pallas kernels for 15%

profile of v3, /device:TPU:0, one launch (start us, length us, event | category | flops | bytes accessed | tf_op | source)
XLA Modules:
  0.0 70.6 jit_solution(14127398060779274958)
XLA Ops:
  0.6 0.9 %copy-done.6 = bf16[1,8,1,64,256]{4,3,2,1,0:T(8,128)(2,1)S(1)} copy-done((bf16[1,8,1,64,256]{4,3,2,1,0:T(8,128)(2,1)S(1)}, bf16[1,8,1,64,256]{4,3,2,1,0:T(8,128)(2,1)}, u32[]{:S(2)}) %copy-start.6) | copy-done | bytes 262168
  2.2 5.1 %collective-permute-start.2 = (bf16[5,1,64,256]{3,2,1,0:T(8,128)(2,1)S(1)}, bf16[5,1,64,256]{3,2,1,0:T(8,128)(2,1)S(1)}, u32[]{:S(2)}, u32[]{:S(2)}) collective-permute-start(bf16[5,1,64,256]{3,2,1,0:T(8,128)(2,1)S(1)} %get-tuple-element.72), channel_id=1, source_target_pairs={{0,24},{8,16},{16,8},{24,0},{1,25},{9,17},{17,9},{25,1},{2,26},{10... | collective-permute-start | bytes 491528 | tf_op jit(solution)/shard_map/ppermute | solution.py:432
  8.0 1.0 %copy-done.2 = bf16[1,4,4,64,256]{4,3,2,1,0:T(8,128)(2,1)S(1)} copy-done((bf16[1,4,4,64,256]{4,3,2,1,0:T(8,128)(2,1)S(1)}, bf16[1,4,4,64,256]{4,3,2,1,0:T(8,128)(2,1)}, u32[]{:S(2)}) %copy-start.2) | copy-done | bytes 524312
  9.1 1.7 %collective-permute-start = (bf16[4,64,256]{2,1,0:T(8,128)(2,1)S(1)}, bf16[4,64,256]{2,1,0:T(8,128)(2,1)S(1)}, u32[]{:S(2)}, u32[]{:S(2)}) collective-permute-start(bf16[4,64,256]{2,1,0:T(8,128)(2,1)S(1)} %get-tuple-element.66), channel_id=1, source_target_pairs={{0,2},{2,0},{4,6},{6,4},{1,3},{3,1},{5,7},{7,5},{8,10},{10,8},{12,... | collective-permute-start | bytes 393224 | tf_op jit(solution)/shard_map/ppermute | solution.py:432
  12.2 1.3 %copy-done = bf16[3,3,256,256]{3,2,1,0:T(8,128)(2,1)S(1)} copy-done((bf16[3,3,256,256]{3,2,1,0:T(8,128)(2,1)S(1)}, bf16[3,3,256,256]{3,2,1,0:T(8,128)(2,1)}, u32[]{:S(2)}) %copy-start) | copy-done | bytes 1179672
  14.1 1.9 %shard_map.118 = (bf16[1024,256]{1,0:T(8,128)(2,1)S(1)}, f32[1024,256]{1,0:T(8,128)S(1)}) custom-call(s32[1]{0:T(128)S(6)} %copy.20.valid_from, bf16[4,4,64,256]{3,2,1,0:T(8,128)(2,1)S(1)} %bitcast.17, f32[1,256]{1,0:T(1,128)S(1)} %bitcast.22, bf16[3,3,256,256]{3,2,1,0:T(8,128)(2,1)S(1)} %copy-done), custom_call_target="tpu_custom_call" | custom-call | flops 1207959552 | bytes 4194304 | tf_op jit(solution)/shard_map/pallas_call | solution.py:404
  16.0 1.7 %shard_map.121 = (bf16[1536,256]{1,0:T(8,128)(2,1)S(1)}, f32[1024,256]{1,0:T(8,128)S(1)}, bf16[2,512,256]{2,1,0:T(8,128)(2,1)S(1)}, bf16[768,256]{1,0:T(8,128)(2...) custom-call(s32[1]{0:T(128)S(6)} %copy.20.valid_from, ...), custom_call_target="tpu_custom_call" | custom-call | tf_op jit(solution)/shard_map/pallas_call | solution.py:404
  17.7 3.5 %collective-permute-done.3.refs_1_ = bf16[5,1,64,256]{3,2,1,0:T(8,128)(2,1)S(1)} collective-permute-done((bf16[5,1,64,256]{3,2,1,0:T(8,128)(2,1)S(1)}, bf16[5,1,64,256]{3,2,1,0:T(8,128)(2,1)S(1)}, u32[]{:S(2)}, u32[]{:S(2)}) %collective-permute-start.3) | collective-permute-done | bytes 163872 | tf_op jit(solution)/shard_map/ppermute | solution.py:432
  21.2 2.2 %shard_map.122 = (bf16[4,4,64,256]{3,2,1,0:T(8,128)(2,1)S(1)}, f32[2560,128]{1,0:T(8,128)S(1)}, bf16[2560,128]{1,0:T(8,128)(2,1)S(1)}) custom-call(bf16[1536,256]{1,0:T(8,128)(2,1)S(1)} %get-tuple-element.68.tall, f32[1024,256]{1,0:T(8,128)S(1)} %get-tuple-element.69.slope, bf16[2,512,256]{2,1,0:T(8,128)(2,1)S(1)} %get-tuple-element.70.active, ...), custom_call_target="tpu_custom_call" | custom-call | flops 1342177280 | bytes 6291456 | tf_op jit(solution)/shard_map/pallas_call | solution.py:404
  23.6 0.9 %shard_map.123 = (f32[1280,128]{1,0:T(8,128)S(1)}, bf16[1280,128]{1,0:T(8,128)(2,1)S(1)}) custom-call(bf16[1536,256]{1,0:T(8,128)(2,1)S(1)} %get-tuple-element.68.tall, bf16[4,4,64,256]{3,2,1,0:T(8,128)(2,1)S(1)} %get-tuple-element.91.pre_gradient.source), custom_call_target="tpu_custom_call" | custom-call | flops 1073741824 | bytes 6291456 | tf_op jit(solution)/shard_map/pallas_call | solution.py:404
  25.1 1.3 %collective-permute-done.6 = bf16[1280,128]{1,0:T(8,128)(2,1)S(1)} collective-permute-done((bf16[1280,128]{1,0:T(8,128)(2,1)S(1)}, bf16[1280,128]{1,0:T(8,128)(2,1)S(1)}, u32[]{:S(2)}, u32[]{:S(2)}) %collective-permute-start.6) | collective-permute-done | bytes 327712 | tf_op jit(solution)/shard_map/ppermute | solution.py:432
  26.5 2.5 %collective-permute-start.11 = (bf16[480,128]{1,0:T(8,128)(2,1)S(1)}, bf16[480,128]{1,0:T(8,128)(2,1)S(1)}, u32[]{:S(2)}, u32[]{:S(2)}) collective-permute-start(bf16[480,128]{1,0:T(8,128)(2,1)S(1)} %get-tuple-element.88), channel_id=1, source_target_pairs={{0,6},{2,4},{4,2},{6,0},{1,7},{3,5},{5,3},{7,1},{8,14},{10,12},{12... | collective-permute-start | bytes 368648 | tf_op jit(solution)/shard_map/ppermute | solution.py:432
  30.1 2.4 %collective-permute-start.7 = (bf16[480,128]{1,0:T(8,128)(2,1)S(1)}, bf16[480,128]{1,0:T(8,128)(2,1)S(1)}, u32[]{:S(2)}, u32[]{:S(2)}) collective-permute-start(bf16[480,128]{1,0:T(8,128)(2,1)S(1)} %get-tuple-element.81), channel_id=1, source_target_pairs={{0,6},{2,4},{4,2},{6,0},{1,7},{3,5},{5,3},{7,1},{8,14},{10,12},{12... | collective-permute-start | bytes 368648 | tf_op jit(solution)/shard_map/ppermute | solution.py:432
  32.5 0.9 %collective-permute-start.8 = (bf16[480,128]{1,0:T(8,128)(2,1)S(1)}, bf16[480,128]{1,0:T(8,128)(2,1)S(1)}, u32[]{:S(2)}, u32[]{:S(2)}) collective-permute-start(bf16[480,128]{1,0:T(8,128)(2,1)S(1)} %get-tuple-element.83), channel_id=1, source_target_pairs={{0,4},{2,6},{4,0},{6,2},{1,5},{3,7},{5,1},{7,3},{8,12},{10,14},{12... | collective-permute-start | bytes 368648 | tf_op jit(solution)/shard_map/ppermute | solution.py:432
  33.5 1.7 %collective-permute-start.9 = (bf16[480,128]{1,0:T(8,128)(2,1)S(1)}, bf16[480,128]{1,0:T(8,128)(2,1)S(1)}, u32[]{:S(2)}, u32[]{:S(2)}) collective-permute-start(bf16[480,128]{1,0:T(8,128)(2,1)S(1)} %get-tuple-element.84), channel_id=1, source_target_pairs={{0,2},{2,0},{4,6},{6,4},{1,3},{3,1},{5,7},{7,5},{8,10},{10,8},{12,... | collective-permute-start | bytes 368648 | tf_op jit(solution)/shard_map/ppermute | solution.py:432
  35.1 1.7 %collective-permute-done.12.refs_1_ = bf16[480,128]{1,0:T(8,128)(2,1)S(1)} collective-permute-done((bf16[480,128]{1,0:T(8,128)(2,1)S(1)}, bf16[480,128]{1,0:T(8,128)(2,1)S(1)}, u32[]{:S(2)}, u32[]{:S(2)}) %collective-permute-start.12) | collective-permute-done | bytes 122912 | tf_op jit(solution)/shard_map/ppermute | solution.py:432
  37.5 1.9 %collective-permute-done.7.refs_0_ = bf16[480,128]{1,0:T(8,128)(2,1)S(1)} collective-permute-done((bf16[480,128]{1,0:T(8,128)(2,1)S(1)}, bf16[480,128]{1,0:T(8,128)(2,1)S(1)}, u32[]{:S(2)}, u32[]{:S(2)}) %collective-permute-start.7) | collective-permute-done | bytes 122912 | tf_op jit(solution)/shard_map/ppermute | solution.py:432
  39.7 1.2 %collective-permute-start.16 = (bf16[4,64,256]{2,1,0:T(8,128)(2,1)S(1)}, bf16[4,64,256]{2,1,0:T(8,128)(2,1)S(1)}, u32[]{:S(2)}, u32[]{:S(2)}) collective-permute-start(bf16[4,64,256]{2,1,0:T(8,128)(2,1)S(1)} %get-tuple-element.92), channel_id=1, source_target_pairs={{0,2},{2,0},{4,6},{6,4},{1,3},{3,1},{5,7},{7,5},{8,10},{10,8},{12,... | collective-permute-start | bytes 393224 | tf_op jit(solution)/shard_map/ppermute | solution.py:432
  42.1 1.8 %collective-permute-start.15 = (bf16[480,128]{1,0:T(8,128)(2,1)S(1)}, bf16[480,128]{1,0:T(8,128)(2,1)S(1)}, u32[]{:S(2)}, u32[]{:S(2)}) collective-permute-start(bf16[480,128]{1,0:T(8,128)(2,1)S(1)} %shard_map.126.left), channel_id=1, source_target_pairs={{0,16},{8,24},{16,0},{24,8},{1,17},{9,25},{17,1},{25,9},{2,18},{10... | collective-permute-start | bytes 368648 | tf_op jit(solution)/shard_map/ppermute | solution.py:432
  43.9 0.8 %collective-permute-done.16.inner = bf16[4,64,256]{2,1,0:T(8,128)(2,1)S(1)} collective-permute-done((bf16[4,64,256]{2,1,0:T(8,128)(2,1)S(1)}, bf16[4,64,256]{2,1,0:T(8,128)(2,1)S(1)}, u32[]{:S(2)}, u32[]{:S(2)}) %collective-permute-start.16) | collective-permute-done | bytes 131104 | tf_op jit(solution)/shard_map/ppermute | solution.py:432
  44.8 2.9 %shard_map.129 = bf16[4,4,64,256]{3,2,1,0:T(8,128)(2,1)} custom-call(s32[1]{0:T(128)S(6)} %copy.20.valid_from, bf16[4,4,64,256]{3,2,1,0:T(8,128)(2,1)S(1)} %bitcast.18, bf16[4,4,64,256]{3,2,1,0:T(8,128)(2,1)S(1)} %get-tuple-element.91.pre_gradient.source, bf16[2,4,64,256]{3,2,1,0:T(8,128)(2,1)S(1)} %shard_map.128.halo, f32[1,256]{1,0:T(1,128)S(1)} %bitcast.24, ...), custom_call_target="tpu_custom_call" | custom-call | flops 1207959552 | bytes 4194304 | tf_op jit(solution)/shard_map/pallas_call | solution.py:404
  47.7 2.2 %collective-permute-done.15.right = bf16[480,128]{1,0:T(8,128)(2,1)S(1)} collective-permute-done((bf16[480,128]{1,0:T(8,128)(2,1)S(1)}, bf16[480,128]{1,0:T(8,128)(2,1)S(1)}, u32[]{:S(2)}, u32[]{:S(2)}) %collective-permute-start.15) | collective-permute-done | bytes 122912 | tf_op jit(solution)/shard_map/ppermute | solution.py:432
  50.0 1.9 %collective-permute-start.22 = (bf16[480,128]{1,0:T(8,128)(2,1)S(1)}, bf16[480,128]{1,0:T(8,128)(2,1)S(1)}, u32[]{:S(2)}, u32[]{:S(2)}) collective-permute-start(bf16[480,128]{1,0:T(8,128)(2,1)S(1)} %shard_map.130.refs_0_), channel_id=1, source_target_pairs={{0,6},{2,4},{4,2},{6,0},{1,7},{3,5},{5,3},{7,1},{8,14},{10,12},{12... | collective-permute-start | bytes 368648 | tf_op jit(solution)/shard_map/ppermute | solution.py:432
  52.0 2.9 %collective-permute-start.21 = (bf16[480,128]{1,0:T(8,128)(2,1)S(1)}, bf16[480,128]{1,0:T(8,128)(2,1)S(1)}, u32[]{:S(2)}, u32[]{:S(2)}) collective-permute-start(bf16[480,128]{1,0:T(8,128)(2,1)S(1)} %shard_map.130.refs_0_), channel_id=1, source_target_pairs={{0,4},{2,6},{4,0},{6,2},{1,5},{3,7},{5,1},{7,3},{8,12},{10,14},{12... | collective-permute-start | bytes 368648 | tf_op jit(solution)/shard_map/ppermute | solution.py:432
  54.9 2.9 %collective-permute-start.23 = (bf16[2,1,3,1,64,256]{5,4,3,2,1,0:T(8,128)(2,1)S(1)}, bf16[2,1,3,1,64,256]{5,4,3,2,1,0:T(8,128)(2,1)S(1)}, u32[]{:S(2)}, u32[]{:S(2)}) collective-permute-start(bf16[2,1,3,1,64,256]{5,4,3,2,1,0:T(8,128)(2,1)S(1)} %get-tuple-element.97), channel_id=1, source_target_pairs={{0,16},{8,24},{16,0},{24,8},{1,17},{9,25},{17,1},{25,9},{2,18},{10... | collective-permute-start | bytes 589832 | tf_op jit(solution)/shard_map/ppermute | solution.py:432
  57.8 1.5 %collective-permute-start.19 = (bf16[480,128]{1,0:T(8,128)(2,1)S(1)}, bf16[480,128]{1,0:T(8,128)(2,1)S(1)}, u32[]{:S(2)}, u32[]{:S(2)}) collective-permute-start(bf16[480,128]{1,0:T(8,128)(2,1)S(1)} %collective-permute-done.18.refs_0_), channel_id=1, source_target_pairs={{0,6},{2,4},{4,2},{6,0},{1,7},{3,5},{5,3},{7,1},{8,14},{10,12},{12... | collective-permute-start | bytes 368648 | tf_op jit(solution)/shard_map/ppermute | solution.py:432
  59.3 1.9 %collective-permute-start.26 = (bf16[480,128]{1,0:T(8,128)(2,1)S(1)}, bf16[480,128]{1,0:T(8,128)(2,1)S(1)}, u32[]{:S(2)}, u32[]{:S(2)}) collective-permute-start(bf16[480,128]{1,0:T(8,128)(2,1)S(1)} %collective-permute-done.18.refs_0_), channel_id=1, source_target_pairs={{0,4},{2,6},{4,0},{6,2},{1,5},{3,7},{5,1},{7,3},{8,12},{10,14},{12... | collective-permute-start | bytes 368648 | tf_op jit(solution)/shard_map/ppermute | solution.py:432
  61.2 1.9 %collective-permute-start.25 = (bf16[480,128]{1,0:T(8,128)(2,1)S(1)}, bf16[480,128]{1,0:T(8,128)(2,1)S(1)}, u32[]{:S(2)}, u32[]{:S(2)}) collective-permute-start(bf16[480,128]{1,0:T(8,128)(2,1)S(1)} %collective-permute-done.18.refs_0_), channel_id=1, source_target_pairs={{0,2},{2,0},{4,6},{6,4},{1,3},{3,1},{5,7},{7,5},{8,10},{10,8},{12,... | collective-permute-start | bytes 368648 | tf_op jit(solution)/shard_map/ppermute | solution.py:432
  63.6 0.8 %collective-permute-done.23.came = bf16[2,1,3,1,64,256]{5,4,3,2,1,0:T(8,128)(2,1)S(1)} collective-permute-done((bf16[2,1,3,1,64,256]{5,4,3,2,1,0:T(8,128)(2,1)S(1)}, bf16[2,1,3,1,64,256]{5,4,3,2,1,0:T(8,128)(2,1)S(1)}, u32[]{:S(2)}, u32[]{:S(2)}) %collective-permute-start.23) | collective-permute-done | bytes 196640 | tf_op jit(solution)/shard_map/ppermute | solution.py:432
  64.5 1.1 %shard_map.133 = bf16[8,1,64,256]{3,2,1,0:T(8,128)(2,1)} custom-call(bf16[3,256,256]{2,1,0:T(8,128)(2,1)S(1)} %copy-done.4, bf16[2,1,3,1,64,256]{5,4,3,2,1,0:T(8,128)(2,1)S(1)} %get-tuple-element.100.stay, bf16[2,1,3,1,64,256]{5,4,3,2,1,0:T(8,128)(2,1)S(1)} %collective-permute-done.23.came), custom_call_target="tpu_custom_call" | custom-call | flops 201326592 | bytes 2097152 | tf_op jit(solution)/shard_map/pallas_call | solution.py:404
  66.9 1.6 %shard_map.135 = (f32[9,256,256]{2,1,0:T(8,128)}, f32[3,256,256]{2,1,0:T(8,128)}, f32[3,256,256]{2,1,0:T(8,128)}, f32[256,128]{1,0:T(8,128)S(1)}) custom-call(bf16[4,480,128]{2,1,0:T(8,128)(2,1)S(1)} %shard_map.131.home, bf16[4,480,128]{2,1,0:T(8,128)(2,1)S(1)} %shard_map.134.away, bf16[3,3,256,256]{3,2,1,0:T(8,128)(2,1)S(1)} %copy-done.1), custom_call_target="tpu_custom_call" | custom-call | bytes 4194304 | tf_op jit(solution)/shard_map/pallas_call | solution.py:404
  68.9 1.6 %shard_map.136 = (f32[9,256,256]{2,1,0:T(8,128)}, f32[3,256,256]{2,1,0:T(8,128)}, f32[3,256,256]{2,1,0:T(8,128)}, f32[1,256]{1,0:T(1,128)}) custom-call(bf16[4,480,128]{2,1,0:T(8,128)(2,1)S(1)} %collective-permute-done.24.home, bf16[4,480,128]{2,1,0:T(8,128)(2,1)S(1)} %collective-permute-done.27.away, ...), custom_call_target="tpu_custom_call", output_to_operand_aliasing={{0}: (5, {}), {1}: (6, {}), {2}: (7, {})} | custom-call | bytes 4194304 | tf_op jit(solution)/shard_map/pallas_call | solution.py:404
  (63 shorter events, 9.4 us)
Async XLA Ops:
  2.2 15.5 %collective-permute-start.2 = (bf16[5,1,64,256]{3,2,1,0:T(8,128)(2,1)S(1)}, bf16[5,1,64,256]{3,2,1,0:T(8,128)(2,1)S(1)}, u32[]{:S(2)}, u32[]{:S(2)}) collective-permute-start(bf16[5,1,64,256]{3,2,1,0:T(8,128)(2,1)S(1)} %get-tuple-element.72), channel_id=1, source_target_pairs={{0,24},{8,16},{16,8},{24,0},{1,25},{9,17},{17,9},{25,1},{2,26},{10... | collective-permute-start | bytes 491528 | tf_op jit(solution)/shard_map/ppermute | solution.py:432
  7.3 13.9 %collective-permute-start.3 = (bf16[5,1,64,256]{3,2,1,0:T(8,128)(2,1)S(1)}, bf16[5,1,64,256]{3,2,1,0:T(8,128)(2,1)S(1)}, u32[]{:S(2)}, u32[]{:S(2)}) collective-permute-start(bf16[5,1,64,256]{3,2,1,0:T(8,128)(2,1)S(1)} %get-tuple-element.73), channel_id=1, source_target_pairs={{0,16},{8,24},{16,0},{24,8},{1,17},{9,25},{17,1},{25,9},{2,18},{10... | collective-permute-start | bytes 491528 | tf_op jit(solution)/shard_map/ppermute | solution.py:432
  7.3 13.9 %collective-permute-start.4 = (bf16[5,1,64,256]{3,2,1,0:T(8,128)(2,1)S(1)}, bf16[5,1,64,256]{3,2,1,0:T(8,128)(2,1)S(1)}, u32[]{:S(2)}, u32[]{:S(2)}) collective-permute-start(bf16[5,1,64,256]{3,2,1,0:T(8,128)(2,1)S(1)} %get-tuple-element.74), channel_id=1, source_target_pairs={{0,8},{8,0},{16,24},{24,16},{1,9},{9,1},{17,25},{25,17},{2,10},{10... | collective-permute-start | bytes 491528 | tf_op jit(solution)/shard_map/ppermute | solution.py:432
  9.0 7.0 %copy-start.5 = (bf16[3,256,256]{2,1,0:T(8,128)(2,1)S(1)}, bf16[3,256,256]{2,1,0:T(8,128)(2,1)}, u32[]{:S(2)}) copy-start(bf16[3,256,256]{2,1,0:T(8,128)(2,1)} %temporal.3) | copy-start | bytes 1179652
  9.1 6.9 %collective-permute-start = (bf16[4,64,256]{2,1,0:T(8,128)(2,1)S(1)}, bf16[4,64,256]{2,1,0:T(8,128)(2,1)S(1)}, u32[]{:S(2)}, u32[]{:S(2)}) collective-permute-start(bf16[4,64,256]{2,1,0:T(8,128)(2,1)S(1)} %get-tuple-element.66), channel_id=1, source_target_pairs={{0,2},{2,0},{4,6},{6,4},{1,3},{3,1},{5,7},{7,5},{8,10},{10,8},{12,... | collective-permute-start | bytes 393224 | tf_op jit(solution)/shard_map/ppermute | solution.py:432
  10.8 5.2 %collective-permute-start.1 = (bf16[4,64,256]{2,1,0:T(8,128)(2,1)S(1)}, bf16[4,64,256]{2,1,0:T(8,128)(2,1)S(1)}, u32[]{:S(2)}, u32[]{:S(2)}) collective-permute-start(bf16[4,64,256]{2,1,0:T(8,128)(2,1)S(1)} %get-tuple-element.67), channel_id=1, source_target_pairs={{2,4},{4,2},{3,5},{5,3},{10,12},{12,10},{11,13},{13,11},{18,20},{2... | collective-permute-start | bytes 393224 | tf_op jit(solution)/shard_map/ppermute | solution.py:428
  16.0 5.2 %copy-start.4 = (bf16[3,256,256]{2,1,0:T(8,128)(2,1)S(1)}, bf16[3,256,256]{2,1,0:T(8,128)(2,1)}, u32[]{:S(2)}) copy-start(bf16[3,256,256]{2,1,0:T(8,128)(2,1)} %mix.3) | copy-start | bytes 1179652
  23.5 2.8 %collective-permute-start.5 = (bf16[2560,128]{1,0:T(8,128)(2,1)S(1)}, bf16[2560,128]{1,0:T(8,128)(2,1)S(1)}, u32[]{:S(2)}, u32[]{:S(2)}) collective-permute-start(bf16[2560,128]{1,0:T(8,128)(2,1)S(1)} %get-tuple-element.76), channel_id=1, source_target_pairs={{0,1},{1,0},{2,3},{3,2},{4,5},{5,4},{6,7},{7,6},{8,9},{9,8},{10,11... | collective-permute-start | bytes 1966088 | tf_op jit(solution)/shard_map/ppermute | solution.py:432
  24.5 1.8 %collective-permute-start.6 = (bf16[1280,128]{1,0:T(8,128)(2,1)S(1)}, bf16[1280,128]{1,0:T(8,128)(2,1)S(1)}, u32[]{:S(2)}, u32[]{:S(2)}) collective-permute-start(bf16[1280,128]{1,0:T(8,128)(2,1)S(1)} %get-tuple-element.79), channel_id=1, source_target_pairs={{0,1},{1,0},{2,3},{3,2},{4,5},{5,4},{6,7},{7,6},{8,9},{9,8},{10,11... | collective-permute-start | bytes 983048 | tf_op jit(solution)/shard_map/ppermute | solution.py:432
  25.1 7.5 %collective-permute-start.10 = (bf16[1,2,3,1,64,256]{5,4,3,2,1,0:T(8,128)(2,1)S(1)}, bf16[1,2,3,1,64,256]{5,4,3,2,1,0:T(8,128)(2,1)S(1)}, u32[]{:S(2)}, u32[]{:S(2)}) collective-permute-start(bf16[1,2,3,1,64,256]{5,4,3,2,1,0:T(8,128)(2,1)S(1)} %get-tuple-element.86), channel_id=1, source_target_pairs={{0,8},{8,0},{16,24},{24,16},{1,9},{9,1},{17,25},{25,17},{2,10},{10... | collective-permute-start | bytes 589832 | tf_op jit(solution)/shard_map/ppermute | solution.py:432
  26.3 18.4 %copy-start.3 = (bf16[1,4,4,64,256]{4,3,2,1,0:T(8,128)(2,1)S(1)}, bf16[1,4,4,64,256]{4,3,2,1,0:T(8,128)(2,1)}, u32[]{:S(2)}) copy-start(bf16[1,4,4,64,256]{4,3,2,1,0:T(8,128)(2,1)} %param.7) | copy-start | bytes 1572868
  26.3 18.4 %copy-start.9 = (f32[256]{0:T(256)S(1)}, f32[256]{0:T(256)}, u32[]{:S(2)}) copy-start(f32[256]{0:T(256)} %param.9) | copy-start | bytes 3076
  26.5 7.0 %collective-permute-start.11 = (bf16[480,128]{1,0:T(8,128)(2,1)S(1)}, bf16[480,128]{1,0:T(8,128)(2,1)S(1)}, u32[]{:S(2)}, u32[]{:S(2)}) collective-permute-start(bf16[480,128]{1,0:T(8,128)(2,1)S(1)} %get-tuple-element.88), channel_id=1, source_target_pairs={{0,6},{2,4},{4,2},{6,0},{1,7},{3,5},{5,3},{7,1},{8,14},{10,12},{12... | collective-permute-start | bytes 368648 | tf_op jit(solution)/shard_map/ppermute | solution.py:432
  29.0 7.8 %collective-permute-start.12 = (bf16[480,128]{1,0:T(8,128)(2,1)S(1)}, bf16[480,128]{1,0:T(8,128)(2,1)S(1)}, u32[]{:S(2)}, u32[]{:S(2)}) collective-permute-start(bf16[480,128]{1,0:T(8,128)(2,1)S(1)} %get-tuple-element.89), channel_id=1, source_target_pairs={{0,4},{2,6},{4,0},{6,2},{1,5},{3,7},{5,1},{7,3},{8,12},{10,14},{12... | collective-permute-start | bytes 368648 | tf_op jit(solution)/shard_map/ppermute | solution.py:432
  29.5 7.3 %collective-permute-start.13 = (bf16[480,128]{1,0:T(8,128)(2,1)S(1)}, bf16[480,128]{1,0:T(8,128)(2,1)S(1)}, u32[]{:S(2)}, u32[]{:S(2)}) collective-permute-start(bf16[480,128]{1,0:T(8,128)(2,1)S(1)} %get-tuple-element.90), channel_id=1, source_target_pairs={{0,2},{2,0},{4,6},{6,4},{1,3},{3,1},{5,7},{7,5},{8,10},{10,8},{12,... | collective-permute-start | bytes 368648 | tf_op jit(solution)/shard_map/ppermute | solution.py:432
  30.1 9.3 %collective-permute-start.7 = (bf16[480,128]{1,0:T(8,128)(2,1)S(1)}, bf16[480,128]{1,0:T(8,128)(2,1)S(1)}, u32[]{:S(2)}, u32[]{:S(2)}) collective-permute-start(bf16[480,128]{1,0:T(8,128)(2,1)S(1)} %get-tuple-element.81), channel_id=1, source_target_pairs={{0,6},{2,4},{4,2},{6,0},{1,7},{3,5},{5,3},{7,1},{8,14},{10,12},{12... | collective-permute-start | bytes 368648 | tf_op jit(solution)/shard_map/ppermute | solution.py:432
  32.5 9.0 %collective-permute-start.8 = (bf16[480,128]{1,0:T(8,128)(2,1)S(1)}, bf16[480,128]{1,0:T(8,128)(2,1)S(1)}, u32[]{:S(2)}, u32[]{:S(2)}) collective-permute-start(bf16[480,128]{1,0:T(8,128)(2,1)S(1)} %get-tuple-element.83), channel_id=1, source_target_pairs={{0,4},{2,6},{4,0},{6,2},{1,5},{3,7},{5,1},{7,3},{8,12},{10,14},{12... | collective-permute-start | bytes 368648 | tf_op jit(solution)/shard_map/ppermute | solution.py:432
  33.5 8.1 %collective-permute-start.9 = (bf16[480,128]{1,0:T(8,128)(2,1)S(1)}, bf16[480,128]{1,0:T(8,128)(2,1)S(1)}, u32[]{:S(2)}, u32[]{:S(2)}) collective-permute-start(bf16[480,128]{1,0:T(8,128)(2,1)S(1)} %get-tuple-element.84), channel_id=1, source_target_pairs={{0,2},{2,0},{4,6},{6,4},{1,3},{3,1},{5,7},{7,5},{8,10},{10,8},{12,... | collective-permute-start | bytes 368648 | tf_op jit(solution)/shard_map/ppermute | solution.py:432
  36.9 5.1 %collective-permute-start.14 = (bf16[480,128]{1,0:T(8,128)(2,1)S(1)}, bf16[480,128]{1,0:T(8,128)(2,1)S(1)}, u32[]{:S(2)}, u32[]{:S(2)}) collective-permute-start(bf16[480,128]{1,0:T(8,128)(2,1)S(1)} %shard_map.125), channel_id=1, source_target_pairs={{0,8},{8,0},{16,24},{24,16},{1,9},{9,1},{17,25},{25,17},{2,10},{10... | collective-permute-start | bytes 368648 | tf_op jit(solution)/shard_map/ppermute | solution.py:432
  39.7 5.0 %collective-permute-start.16 = (bf16[4,64,256]{2,1,0:T(8,128)(2,1)S(1)}, bf16[4,64,256]{2,1,0:T(8,128)(2,1)S(1)}, u32[]{:S(2)}, u32[]{:S(2)}) collective-permute-start(bf16[4,64,256]{2,1,0:T(8,128)(2,1)S(1)} %get-tuple-element.92), channel_id=1, source_target_pairs={{0,2},{2,0},{4,6},{6,4},{1,3},{3,1},{5,7},{7,5},{8,10},{10,8},{12,... | collective-permute-start | bytes 393224 | tf_op jit(solution)/shard_map/ppermute | solution.py:432
  40.9 3.9 %collective-permute-start.17 = (bf16[4,64,256]{2,1,0:T(8,128)(2,1)S(1)}, bf16[4,64,256]{2,1,0:T(8,128)(2,1)S(1)}, u32[]{:S(2)}, u32[]{:S(2)}) collective-permute-start(bf16[4,64,256]{2,1,0:T(8,128)(2,1)S(1)} %get-tuple-element.93), channel_id=1, source_target_pairs={{2,4},{4,2},{3,5},{5,3},{10,12},{12,10},{11,13},{13,11},{18,20},{2... | collective-permute-start | bytes 393224 | tf_op jit(solution)/shard_map/ppermute | solution.py:428
  42.1 7.8 %collective-permute-start.15 = (bf16[480,128]{1,0:T(8,128)(2,1)S(1)}, bf16[480,128]{1,0:T(8,128)(2,1)S(1)}, u32[]{:S(2)}, u32[]{:S(2)}) collective-permute-start(bf16[480,128]{1,0:T(8,128)(2,1)S(1)} %shard_map.126.left), channel_id=1, source_target_pairs={{0,16},{8,24},{16,0},{24,8},{1,17},{9,25},{17,1},{25,9},{2,18},{10... | collective-permute-start | bytes 368648 | tf_op jit(solution)/shard_map/ppermute | solution.py:432
  49.9 7.9 %collective-permute-start.18 = (bf16[480,128]{1,0:T(8,128)(2,1)S(1)}, bf16[480,128]{1,0:T(8,128)(2,1)S(1)}, u32[]{:S(2)}, u32[]{:S(2)}) collective-permute-start(bf16[480,128]{1,0:T(8,128)(2,1)S(1)} %shard_map.130.refs_0_), channel_id=1, source_target_pairs={{0,8},{8,0},{16,24},{24,16},{1,9},{9,1},{17,25},{25,17},{2,10},{10... | collective-permute-start | bytes 368648 | tf_op jit(solution)/shard_map/ppermute | solution.py:432
  50.0 9.3 %collective-permute-start.22 = (bf16[480,128]{1,0:T(8,128)(2,1)S(1)}, bf16[480,128]{1,0:T(8,128)(2,1)S(1)}, u32[]{:S(2)}, u32[]{:S(2)}) collective-permute-start(bf16[480,128]{1,0:T(8,128)(2,1)S(1)} %shard_map.130.refs_0_), channel_id=1, source_target_pairs={{0,6},{2,4},{4,2},{6,0},{1,7},{3,5},{5,3},{7,1},{8,14},{10,12},{12... | collective-permute-start | bytes 368648 | tf_op jit(solution)/shard_map/ppermute | solution.py:432
  52.0 9.3 %collective-permute-start.21 = (bf16[480,128]{1,0:T(8,128)(2,1)S(1)}, bf16[480,128]{1,0:T(8,128)(2,1)S(1)}, u32[]{:S(2)}, u32[]{:S(2)}) collective-permute-start(bf16[480,128]{1,0:T(8,128)(2,1)S(1)} %shard_map.130.refs_0_), channel_id=1, source_target_pairs={{0,4},{2,6},{4,0},{6,2},{1,5},{3,7},{5,1},{7,3},{8,12},{10,14},{12... | collective-permute-start | bytes 368648 | tf_op jit(solution)/shard_map/ppermute | solution.py:432
  54.9 9.6 %collective-permute-start.23 = (bf16[2,1,3,1,64,256]{5,4,3,2,1,0:T(8,128)(2,1)S(1)}, bf16[2,1,3,1,64,256]{5,4,3,2,1,0:T(8,128)(2,1)S(1)}, u32[]{:S(2)}, u32[]{:S(2)}) collective-permute-start(bf16[2,1,3,1,64,256]{5,4,3,2,1,0:T(8,128)(2,1)S(1)} %get-tuple-element.97), channel_id=1, source_target_pairs={{0,16},{8,24},{16,0},{24,8},{1,17},{9,25},{17,1},{25,9},{2,18},{10... | collective-permute-start | bytes 589832 | tf_op jit(solution)/shard_map/ppermute | solution.py:432
  57.7 5.8 %collective-permute-start.20 = (bf16[480,128]{1,0:T(8,128)(2,1)S(1)}, bf16[480,128]{1,0:T(8,128)(2,1)S(1)}, u32[]{:S(2)}, u32[]{:S(2)}) collective-permute-start(bf16[480,128]{1,0:T(8,128)(2,1)S(1)} %shard_map.130.refs_0_), channel_id=1, source_target_pairs={{0,2},{2,0},{4,6},{6,4},{1,3},{3,1},{5,7},{7,5},{8,10},{10,8},{12,... | collective-permute-start | bytes 368648 | tf_op jit(solution)/shard_map/ppermute | solution.py:432
  57.8 7.7 %collective-permute-start.19 = (bf16[480,128]{1,0:T(8,128)(2,1)S(1)}, bf16[480,128]{1,0:T(8,128)(2,1)S(1)}, u32[]{:S(2)}, u32[]{:S(2)}) collective-permute-start(bf16[480,128]{1,0:T(8,128)(2,1)S(1)} %collective-permute-done.18.refs_0_), channel_id=1, source_target_pairs={{0,6},{2,4},{4,2},{6,0},{1,7},{3,5},{5,3},{7,1},{8,14},{10,12},{12... | collective-permute-start | bytes 368648 | tf_op jit(solution)/shard_map/ppermute | solution.py:432
  59.3 6.3 %collective-permute-start.26 = (bf16[480,128]{1,0:T(8,128)(2,1)S(1)}, bf16[480,128]{1,0:T(8,128)(2,1)S(1)}, u32[]{:S(2)}, u32[]{:S(2)}) collective-permute-start(bf16[480,128]{1,0:T(8,128)(2,1)S(1)} %collective-permute-done.18.refs_0_), channel_id=1, source_target_pairs={{0,4},{2,6},{4,0},{6,2},{1,5},{3,7},{5,1},{7,3},{8,12},{10,14},{12... | collective-permute-start | bytes 368648 | tf_op jit(solution)/shard_map/ppermute | solution.py:432
  61.2 5.0 %collective-permute-start.25 = (bf16[480,128]{1,0:T(8,128)(2,1)S(1)}, bf16[480,128]{1,0:T(8,128)(2,1)S(1)}, u32[]{:S(2)}, u32[]{:S(2)}) collective-permute-start(bf16[480,128]{1,0:T(8,128)(2,1)S(1)} %collective-permute-done.18.refs_0_), channel_id=1, source_target_pairs={{0,2},{2,0},{4,6},{6,4},{1,3},{3,1},{5,7},{7,5},{8,10},{10,8},{12,... | collective-permute-start | bytes 368648 | tf_op jit(solution)/shard_map/ppermute | solution.py:432
  66.3 2.1 %collective-permute-start.27 = (bf16[4,480,128]{2,1,0:T(8,128)(2,1)S(1)}, bf16[4,480,128]{2,1,0:T(8,128)(2,1)S(1)}, u32[]{:S(2)}, u32[]{:S(2)}) collective-permute-start(bf16[4,480,128]{2,1,0:T(8,128)(2,1)S(1)} %shard_map.134.away), channel_id=1, source_target_pairs={{0,1},{1,0},{2,3},{3,2},{4,5},{5,4},{6,7},{7,6},{8,9},{9,8},{10,11... | collective-permute-start | bytes 1474568 | tf_op jit(solution)/shard_map/ppermute | solution.py:432
  66.4 2.6 %collective-permute-start.24 = (bf16[4,480,128]{2,1,0:T(8,128)(2,1)S(1)}, bf16[4,480,128]{2,1,0:T(8,128)(2,1)S(1)}, u32[]{:S(2)}, u32[]{:S(2)}) collective-permute-start(bf16[4,480,128]{2,1,0:T(8,128)(2,1)S(1)} %shard_map.131.home), channel_id=1, source_target_pairs={{0,1},{1,0},{2,3},{3,2},{4,5},{5,4},{6,7},{7,6},{8,9},{9,8},{10,11... | collective-permute-start | bytes 1474568 | tf_op jit(solution)/shard_map/ppermute | solution.py:432
  (6 other events, 11.1 us)
